TPU v7x, 32 devices: a whole 2x2x4 slice. The times are simulated.
32 devices in a mesh: gx: 4 (over y, x), gy: 8 (over z, core).
Axes of the slice: x: 2, y: 2, z: 4, core: 2. Of those that a mesh axis runs over, the one named last changes fastest.
Arguments:
- right_side: float32 [16384, 64], P(('gx', 'gy')), may hold values from -6 to 6
- leaf_inverse: float32 [16384, 512], P(('gx', 'gy')), as said below
- basis_one: float32 [16384, 128], P(('gx', 'gy')), may hold values from -0.0625 to 0.0625
- basis_two: float32 [16384, 128], P(('gx', 'gy')), may hold values from -0.09375 to 0.09375
- factor_one: bfloat16 [1, 256, 256], replicated, may hold values from -0.5 to 0.5
- factor_two: bfloat16 [2, 256, 256], replicated, may hold values from -0.5 to 0.5
Outputs:
- solution: float32 [16384, 64], P(('gx', 'gy'))
Inputs may be any that keep to these rules, and one draw needn't show every extreme that they name: `leaf_inverse`: each block of 512 consecutive rows is a symmetric positive definite 512 x 512 matrix.
All inputs are finite; a program needn't handle non-finite values.
Results may differ from a plain program's by a relative error of at most 0.0003.
Values sent between devices are 32-bit elements; how exact they have to be, the bound alone decides.
No kernel may reach another device: no remote copies, remote signals or barrier semaphores. Data moves between devices by JAX's collectives and lax.ppermute only.
A program may use at most 64 MiB of HBM per device.

v0:
```python
import jax
import jax.numpy as jnp
from jax import lax
from jax.sharding import PartitionSpec as P

HIGH = lax.Precision.HIGHEST


def partner(value, axis, stride):
    mask = 2**stride
    pairs = [(source, source ^ mask) for source in range(lax.axis_size(axis))]
    return lax.ppermute(value, axis, pairs)


def matmul(left, right):
    return jnp.dot(left, right, precision=HIGH, preferred_element_type=jnp.float32)


def solve_small(matrix, right_terms):
    lower_factor = jnp.linalg.cholesky(matrix)
    middle = lax.linalg.triangular_solve(lower_factor, right_terms, left_side=True, lower=True)
    return lax.linalg.triangular_solve(
        lower_factor, middle, left_side=True, lower=True, transpose_a=True
    )


def group_total(packed, group_bits):
    fine_bits = lax.axis_size("gy").bit_length() - 1
    packed = lax.psum(packed, "gy")
    coarse_bits = group_bits - fine_bits
    if coarse_bits > 0:
        for bit_index in range(coarse_bits):
            packed = packed + partner(packed, "gx", bit_index)
    return packed


def body(right_side, leaf_inverse, basis_one, basis_two, factor_one, factor_two):
    level_bases = (basis_one, basis_two)
    factors = (factor_one, factor_two)
    rank_width = basis_one.shape[1]
    rhs_width = right_side.shape[1]
    fine_bits = lax.axis_size("gy").bit_length() - 1
    total_bits = fine_bits + lax.axis_size("gx").bit_length() - 1
    flat_index = lax.axis_index("gx") * lax.axis_size("gy") + lax.axis_index("gy")
    identity = jnp.eye(2 * rank_width, dtype=jnp.float32)
    current = matmul(leaf_inverse, jnp.concatenate((right_side,) + level_bases, axis=1))
    for level_index in range(len(level_bases), 0, -1):
        width_used = rhs_width + (level_index - 1) * rank_width
        remaining = current[:, :width_used]
        solved = current[:, width_used : width_used + rank_width]
        basis_rows = level_bases[level_index - 1]
        gram_local = matmul(basis_rows.T, solved)
        projection = matmul(basis_rows.T, remaining)
        group_bits = total_bits - level_index
        pair_index = flat_index // 2 ** (group_bits + 1)
        half_index = flat_index // 2**group_bits % 2
        factor = lax.dynamic_index_in_dim(
            factors[level_index - 1], pair_index, 0, keepdims=False
        ).astype(jnp.float32)
        mine_rows = lax.dynamic_slice_in_dim(factor, half_index * rank_width, rank_width, 0)
        packed = group_total(jnp.concatenate((gram_local, projection), axis=1), group_bits)
        others = partner(packed, "gx", group_bits - fine_bits)
        other_rows = lax.dynamic_slice_in_dim(factor, (1 - half_index) * rank_width, rank_width, 0)
        capacitance = identity + matmul(mine_rows.T, matmul(packed[:, :rank_width], mine_rows))
        capacitance = capacitance + matmul(other_rows.T, matmul(others[:, :rank_width], other_rows))
        right_terms = matmul(mine_rows.T, packed[:, rank_width:]) + matmul(
            other_rows.T, others[:, rank_width:]
        )
        coefficient = solve_small(capacitance, right_terms)
        current = remaining - matmul(solved, matmul(mine_rows, coefficient))
    return current


def solution(mesh):
    in_specs = (
        P(("gx", "gy"), None),
        P(("gx", "gy"), None),
        P(("gx", "gy"), None),
        P(("gx", "gy"), None),
        P(),
        P(),
    )
    out_specs = P(("gx", "gy"), None)
    return jax.shard_map(body, mesh=mesh, in_specs=in_specs, out_specs=out_specs, check_vma=False)
```

profile of v0, /device:TPU:0, one launch (start us, length us, event | category | flops | bytes accessed | tf_op | source)
XLA Modules:
  0.0 276.0 jit_solution(5293598732219570769)
XLA Ops:
  6.5 1.1 copy.7
  7.9 3.9 %convolution_bitcast_fusion = f32[512,320]{0,1:T(8,128)S(1)} fusion(f32[512,512]{1,0:T(8,128)S(1)} %copy-done, f32[512,128]{1,0:T(8,128)S(1)} %copy-done.1, f32[512,128]{1,0:T(8,128)} %param.9, f32[512,64]{1,0:T(8,128)S(1)} %copy.7), kind=kOutput, calls=%fused_computation.4 | convolution fusion | flops 1006960640 | bytes 2359296 | tf_op jit(solution)/shard_map/dot_general | solution.py:16
  12.7 0.7 pad_maximum_fusion
  13.7 54.6 %all-reduce.4.cloned.1.call-done = f32[128,320]{0,1:T(8,128)} async-done(((f32[128,320]{0,1:T(8,128)}), f32[128,320]{0,1:T(8,128)}) %all-reduce.4.cloned.1.call-update) | async-done | bytes 163856 | tf_op jit(solution)/shard_map/psum | solution.py:29
  68.3 1.1 fusion.33
  70.4 1.5 collective-permute-start
  72.1 4.4 %collective-permute-done = f32[128,320]{0,1:T(8,128)S(1)} collective-permute-done((f32[128,320]{0,1:T(8,128)S(1)}, f32[128,320]{0,1:T(8,128)S(1)}, u32[]{:S(2)}, u32[]{:S(2)}) %collective-permute-start) | collective-permute-done | bytes 163872 | tf_op jit(solution)/shard_map/ppermute | solution.py:12
  77.2 11.7 %cholesky.130 = f32[128,128]{1,0:T(8,128)S(1)} custom-call(f32[128,128]{1,0:T(8,128)S(1)} %cholesky.194), custom_call_target="Cholesky" | custom-call | tf_op jit(solution)/shard_map/jit(cholesky)/cholesky | solution.py:20
  89.0 9.8 %custom-call.21 = f32[1,128,128]{1,2,0:T(8,128)S(1)} custom-call(f32[1,128,128]{2,1,0:T(8,128)S(1)} %get-tuple-element.49), custom_call_target="InvertDiagBlocksLowerTriangular" | custom-call | tf_op jit(solution)/shard_map/jit(cholesky)/cholesky | solution.py:20
  99.3 11.7 %cholesky.147 = f32[128,128]{1,0:T(8,128)S(1)} custom-call(f32[128,128]{1,0:T(8,128)S(1)} %convolution_subtract_fusion.4), custom_call_target="Cholesky" | custom-call | tf_op jit(solution)/shard_map/jit(cholesky)/cholesky | solution.py:20
  111.0 0.7 compare_reduce_fusion.2
  113.1 4.1 %while.2 = (s32[]{:T(128)}, f32[256,256]{1,0:T(8,128)S(1)}, s32[2,2]{1,0:T(2,128)S(1)}, f32[2,128,128]{2,1,0:T(8,128)S(1)}, s32[]{:T(128)}) while((s32[]{:T(128)}, f32[256,256]{1,0:T(8,128)S(1)}, s32[2,2]{1,0:T(2,128)S(1)}, f32[2,128,128]{2,1,0:T(8,128)S(1)}, s32[]{:T(128)}) %tuple.41), condition=%wide.while_cond, body=%wide.while_body.sunk | while | flops 2 | bytes 131189 | solution.py:22
  113.2 0.7 fusion.129
  113.8 1.3 bitcast_dynamic-update-slice_fusion.4
  115.2 0.7 fusion.129
  115.9 1.3 bitcast_dynamic-update-slice_fusion.4
  117.2 19.9 %custom-call.18 = f32[2,128,128]{1,2,0:T(8,128)S(1)} custom-call(f32[2,128,128]{2,1,0:T(8,128)S(1)} %get-tuple-element.13), custom_call_target="InvertDiagBlocksLowerTriangular" | custom-call | tf_op jit(solution)/shard_map/triangular_solve | solution.py:22
  141.7 52.6 %all-reduce.6.cloned.1.call-done = f32[128,192]{0,1:T(8,128)} async-done(((f32[128,192]{0,1:T(8,128)}), f32[128,192]{0,1:T(8,128)}) %all-reduce.6.cloned.1.call-update) | async-done | bytes 98320 | tf_op jit(solution)/shard_map/psum | solution.py:29
  194.4 1.5 collective-permute-start.1
  195.8 3.4 %collective-permute-done.1 = f32[128,192]{0,1:T(8,128)S(1)} collective-permute-done((f32[128,192]{0,1:T(8,128)}, f32[128,192]{0,1:T(8,128)S(1)}, u32[]{:S(2)}, u32[]{:S(2)}) %collective-permute-start.1) | collective-permute-done | bytes 98336 | tf_op jit(solution)/shard_map/ppermute | solution.py:12
  199.2 0.9 add.96
  200.1 1.5 collective-permute-start.2
  202.2 2.5 collective-permute-done.2
  205.6 11.7 %cholesky.164 = f32[128,128]{1,0:T(8,128)S(1)} custom-call(f32[128,128]{1,0:T(8,128)S(1)} %cholesky.197), custom_call_target="Cholesky" | custom-call | tf_op jit(solution)/shard_map/jit(cholesky)/cholesky | solution.py:20
  217.4 9.8 %custom-call.22 = f32[1,128,128]{1,2,0:T(8,128)S(1)} custom-call(f32[1,128,128]{2,1,0:T(8,128)S(1)} %get-tuple-element.45), custom_call_target="InvertDiagBlocksLowerTriangular" | custom-call | tf_op jit(solution)/shard_map/jit(cholesky)/cholesky | solution.py:20
  227.7 11.9 %cholesky.181 = f32[128,128]{1,0:T(8,128)S(1)} custom-call(f32[128,128]{1,0:T(8,128)S(1)} %convolution_subtract_fusion.3), custom_call_target="Cholesky" | custom-call | tf_op jit(solution)/shard_map/jit(cholesky)/cholesky | solution.py:20
  240.3 0.7 compare_reduce_fusion
  242.4 4.1 %while.3 = (s32[]{:T(128)}, f32[256,256]{1,0:T(8,128)S(1)}, s32[2,2]{1,0:T(2,128)S(1)}, f32[2,128,128]{2,1,0:T(8,128)S(1)}, s32[]{:T(128)}) while((s32[]{:T(128)}, f32[256,256]{1,0:T(8,128)S(1)}, s32[2,2]{1,0:T(2,128)S(1)}, f32[2,128,128]{2,1,0:T(8,128)S(1)}, s32[]{:T(128)}) %tuple.51), condition=%wide.while_cond.1, body=%wide.while_body.1.sunk | while | flops 2 | bytes 131189 | solution.py:22
  243.0 1.4 bitcast_dynamic-update-slice_fusion.5
  245.0 1.4 bitcast_dynamic-update-slice_fusion.5
  246.5 19.7 %custom-call.19 = f32[2,128,128]{1,2,0:T(8,128)S(1)} custom-call(f32[2,128,128]{2,1,0:T(8,128)S(1)} %get-tuple-element.21), custom_call_target="InvertDiagBlocksLowerTriangular" | custom-call | tf_op jit(solution)/shard_map/triangular_solve | solution.py:22
  268.2 1.0 convolution_subtract_fusion.1
  (76 shorter events, 14.2 us)
Async XLA Ops:
  6.5 1.3 copy-start
  6.5 1.3 copy-start.1
  6.5 61.8 %all-reduce.4.cloned.1.call-start = ((), (), s32[]{:S(2)}) async-start(), calls=%async_computation | async-start | bytes 327680 | tf_op jit(solution)/shard_map/psum | solution.py:29
  12.7 55.6 %copy-start.4 = (bf16[2,256,256]{2,1,0:T(8,128)(2,1)S(1)}, bf16[2,256,256]{2,1,0:T(8,128)(2,1)}, u32[]{:S(2)}) copy-start(bf16[2,256,256]{2,1,0:T(8,128)(2,1)} %param.12) | copy-start | bytes 786436
  13.4 181.0 %all-reduce.6.cloned.1.call-start = ((), (), s32[]{:S(2)}) async-start(), calls=%async_computation.1 | async-start | bytes 196608 | tf_op jit(solution)/shard_map/psum | solution.py:29
  69.4 0.9 copy-start.5
  70.4 6.1 %collective-permute-start = (f32[128,320]{0,1:T(8,128)S(1)}, f32[128,320]{0,1:T(8,128)S(1)}, u32[]{:S(2)}, u32[]{:S(2)}) collective-permute-start(f32[128,320]{0,1:T(8,128)S(1)} %copy-done.5), channel_id=1, source_target_pairs={{0,8},{8,0},{16,24},{24,16},{1,9},{9,1},{17,25},{25,17},{2,10},{10... | collective-permute-start | bytes 491528 | tf_op jit(solution)/shard_map/ppermute | solution.py:12
  139.4 1.0 copy-start.2
  194.4 4.8 %collective-permute-start.1 = (f32[128,192]{0,1:T(8,128)}, f32[128,192]{0,1:T(8,128)S(1)}, u32[]{:S(2)}, u32[]{:S(2)}) collective-permute-start(f32[128,192]{0,1:T(8,128)} %all-reduce.6.cloned.1.call-done), channel_id=1, source_target_pairs={{0,8},{8,0},{16,24},{24,16},{1,9},{9,1},{17,25},{25,17},{2,10},{10... | collective-permute-start | bytes 294920 | tf_op jit(solution)/shard_map/ppermute | solution.py:12
  195.8 5.8 %copy-start.3 = (bf16[1,256,256]{2,1,0:T(8,128)(2,1)S(1)}, bf16[1,256,256]{2,1,0:T(8,128)(2,1)}, u32[]{:S(2)}) copy-start(bf16[1,256,256]{2,1,0:T(8,128)(2,1)} %param.11) | copy-start | bytes 393220
  200.1 4.7 %collective-permute-start.2 = (f32[128,192]{0,1:T(8,128)S(1)}, f32[128,192]{0,1:T(8,128)S(1)}, u32[]{:S(2)}, u32[]{:S(2)}) collective-permute-start(f32[128,192]{0,1:T(8,128)S(1)} %add.96), channel_id=1, source_target_pairs={{0,16},{8,24},{16,0},{24,8},{1,17},{9,25},{17,1},{25,9},{2,18},{10... | collective-permute-start | bytes 294920 | tf_op jit(solution)/shard_map/ppermute | solution.py:12
Sparse Core Ops, SparseCore 0:
  13.5 54.7 all-reduce.3
  141.9 52.4 all-reduce.5
where the time goes:
time: 276 us
  waiting for transfers between devices  118 us (43%)
  other arithmetic  111 us (40%)
  between operations  16.5 us (6%)
  matrix products  15.5 us (6%)
  local copies, waits for them, and re-layouts  10.8 us (4%)
  starting transfers between devices  4.7 us (2%)
    psum x2, waiting for transfers between devices, group_total(): packed = lax.psum(packed, 'gy')  107 us
    another operation x13, other arithmetic, solve_small(): lower_factor = jnp.linalg.cholesky(matrix)  68.9 us
    another operation x5, other arithmetic, solve_small(): lax.linalg.triangular_solve(lower_factor, middle, left_side=True, lower=T...  39.6 us
    dot_general x21, matrix products, matmul(): jnp.dot(left, right, precision=HIGH, preferred_element_type=jnp.float32)  11.4 us
    ppermute x3, waiting for transfers between devices, partner(): return lax.ppermute(value, axis, pairs)  10.3 us
    another operation x12, local copies, waits for them, and re-layouts  8.08 us
  transfers between devices with their start and end apart: 5, of which 5 were waited for; matrix products, arithmetic and copies ran while one was open for 0% of the time, Pallas kernels for 0%

commit v1 on v0

v1 whole, which is shorter than its diff:
```python
import jax
import jax.numpy as jnp
from jax import lax
from jax.experimental import pallas as pl
from jax.experimental.pallas import tpu as pltpu
from jax.sharding import PartitionSpec as P

HIGH = lax.Precision.HIGHEST
F32 = jnp.float32
SUB = 8
VMEM_BYTES = 32 * 1024 * 1024


def partner(value, axis, mask):
    pairs = [(source, source ^ mask) for source in range(lax.axis_size(axis))]
    return lax.ppermute(value, axis, pairs)


def matmul(left, right):
    return jnp.dot(left, right, precision=HIGH, preferred_element_type=F32)


def matmul_tn(left, right):
    return lax.dot_general(
        left, right, (((0,), (0,)), ((), ())), precision=HIGH, preferred_element_type=F32
    )


def sweep_block(elements):
    e = [list(row) for row in elements]

    def get(i, j):
        return e[i][j] if i >= j else e[j][i]

    for t in range(SUB):
        scale = 1.0 / e[t][t]
        old = [get(i, t) for i in range(SUB)]
        new = [old[i] * scale for i in range(SUB)]
        for i in range(SUB):
            for j in range(i + 1):
                if i != t and j != t:
                    e[i][j] = e[i][j] - new[i] * old[j]
        for i in range(SUB):
            if i > t:
                e[i][t] = new[i]
            elif i < t:
                e[t][i] = new[i]
        e[t][t] = -scale
    return get


def inverse_spd(matrix):
    order = matrix.shape[0]
    panel = (SUB, order)
    row_at = lax.broadcasted_iota(jnp.int32, panel, 0)
    lane_at = lax.broadcasted_iota(jnp.int32, panel, 1)
    rows = [matrix[SUB * i : SUB * (i + 1), :] for i in range(order // SUB)]
    for k in range(order // SUB):
        base = SUB * k
        pivot_row = rows[k]
        columns = [
            jnp.broadcast_to(pivot_row[:, base + j : base + j + 1], panel) for j in range(SUB)
        ]
        get = sweep_block(
            [
                [jnp.broadcast_to(columns[j][i : i + 1, :], panel) for j in range(i + 1)]
                for i in range(SUB)
            ]
        )
        inside = (lane_at >= base) & (lane_at < base + SUB)
        unit = jnp.where(lane_at - base == row_at, 1.0, 0.0)
        pivot_row = jnp.where(inside, unit, pivot_row)
        scaled = None
        for j in range(SUB):
            column = get(SUB - 1, j)
            for i in range(SUB - 2, -1, -1):
                column = jnp.where(row_at == i, get(i, j), column)
            term = column * jnp.broadcast_to(pivot_row[j : j + 1, :], panel)
            scaled = term if scaled is None else scaled + term
        spread = [jnp.broadcast_to(scaled[j : j + 1, :], panel) for j in range(SUB)]
        for i in range(order // SUB):
            if i == k:
                continue
            total = jnp.where(inside, 0.0, rows[i])
            for j in range(SUB):
                column = jnp.broadcast_to(rows[i][:, base + j : base + j + 1], panel)
                total = total + column * spread[j]
            rows[i] = total
        rows[k] = -scaled
    return jnp.concatenate(rows, axis=0)


def solve_spd(system, rank):
    first, second = system[:rank], system[rank:]
    head = matmul(inverse_spd(first[:, :rank]), first[:, rank:])
    rest = second[:, rank:] - matmul(second[:, :rank], head)
    low = matmul(inverse_spd(rest[:, :rank]), rest[:, rank:])
    high = head[:, rank:] - matmul(head[:, :rank], low)
    return jnp.concatenate((high, low), axis=0)


def add_eye(system):
    row_at = lax.broadcasted_iota(jnp.int32, system.shape, 0)
    lane_at = lax.broadcasted_iota(jnp.int32, system.shape, 1)
    return system + jnp.where(row_at == lane_at, 1.0, 0.0)


def local_kernel(rhs_ref, leaf_ref, one_ref, two_ref, solved_ref, keep_ref, give_ref):
    rank = one_ref.shape[1]
    width = rhs_ref.shape[1]
    bases = jnp.concatenate((two_ref[...], one_ref[...]), axis=1)
    solved = matmul(leaf_ref[...], jnp.concatenate((bases, rhs_ref[...]), axis=1))
    solved_ref[...] = solved
    products = matmul_tn(bases, solved)
    g22 = products[:rank, :rank]
    g21 = products[:rank, rank : 2 * rank]
    g11 = products[rank:, rank : 2 * rank]
    row_at = lax.broadcasted_iota(jnp.int32, (rank, rank), 0)
    lane_at = lax.broadcasted_iota(jnp.int32, (rank, rank), 1)
    both = jnp.where(row_at >= lane_at, g22, g11)
    diagonal = jnp.sum(jnp.where(row_at == lane_at, g11, 0.0), axis=0, keepdims=True)
    terms = jnp.concatenate((products[:rank, 2 * rank :], products[rank:, 2 * rank :]), axis=1)
    half = keep_ref.shape[0] - SUB
    cut = half - rank
    pad = jnp.broadcast_to(diagonal, (SUB, rank))
    low = jnp.concatenate((both, terms[:cut], pad), axis=0)
    high = jnp.concatenate((g21, terms[cut:], pad), axis=0)
    upper = lax.axis_index("gy") % 2 == 1
    keep_ref[...] = jnp.where(upper, high, low)
    give_ref[...] = jnp.where(upper, low, high)


def unpack(low, high, rank):
    cut = rank // 2
    row_at = lax.broadcasted_iota(jnp.int32, (rank, rank), 0)
    lane_at = lax.broadcasted_iota(jnp.int32, (rank, rank), 1)
    both = low[:rank]
    flipped = both.T
    terms = jnp.concatenate((low[rank : rank + cut], high[rank : rank + cut]), axis=0)
    diagonal = jnp.broadcast_to(low[rank + cut : rank + cut + 1], (rank, rank))
    g22 = jnp.where(row_at >= lane_at, both, flipped)
    g11 = jnp.where(
        row_at < lane_at, both, jnp.where(row_at == lane_at, diagonal, flipped)
    )
    g21 = high[:rank]
    return g22, g21, g11, terms[:, : rank // 2], terms[:, rank // 2 :]


def second_kernel(mine_ref, other_ref, factor_ref, out_ref, update_ref):
    rank = factor_ref.shape[0] // 2
    upper = lax.axis_index("gy") % 2 == 1
    mine, other = mine_ref[...], other_ref[...]
    low = jnp.where(upper, other, mine)
    high = jnp.where(upper, mine, other)
    factor = factor_ref[...]
    g22, g21, g11, terms, later = [], [], [], [], []
    for side in range(2):
        parts = unpack(low[side], high[side], rank)
        g22.append(parts[0])
        g21.append(parts[1])
        g11.append(parts[2])
        terms.append(parts[3])
        later.append(parts[4])
    wide = jnp.concatenate(
        [
            jnp.concatenate(
                (matmul(g22[side], factor[side * rank : (side + 1) * rank]), g21[side], terms[side]),
                axis=1,
            )
            for side in range(2)
        ],
        axis=0,
    )
    update = matmul(factor, solve_spd(add_eye(matmul_tn(factor, wide)), rank))
    update_ref[...] = update[:rank]
    start = jnp.concatenate((g11[0] + g11[1], later[0] + later[1]), axis=1)
    out_ref[...] = start - matmul_tn(jnp.concatenate(g21, axis=0), update)


def first_kernel(mine_ref, other_ref, factor_ref, update_ref, solved_ref, out_ref):
    rank = factor_ref.shape[0] // 2
    factor = factor_ref[...]
    wide = jnp.concatenate(
        [
            jnp.concatenate(
                (
                    matmul(ref[:, :rank], factor[side * rank : (side + 1) * rank]),
                    ref[:, rank:],
                ),
                axis=1,
            )
            for side, ref in enumerate((mine_ref, other_ref))
        ],
        axis=0,
    )
    solution_terms = solve_spd(add_eye(matmul_tn(factor, wide)), rank)
    outer = matmul(factor[:rank], solution_terms)
    inner = update_ref[:, rank:] - matmul(update_ref[:, :rank], outer)
    out_ref[...] = solved_ref[:, 2 * rank :] - matmul(
        solved_ref[:, : 2 * rank], jnp.concatenate((inner, outer), axis=0)
    )


def call(kernel, shapes, *args):
    return pl.pallas_call(
        kernel,
        out_shape=[jax.ShapeDtypeStruct(shape, F32) for shape in shapes],
        compiler_params=pltpu.CompilerParams(vmem_limit_bytes=VMEM_BYTES),
    )(*args)


def pick_factor(factor, flat_index, group_bits, rank):
    pair_index = flat_index // 2 ** (group_bits + 1)
    half_index = flat_index // 2**group_bits % 2
    chosen = lax.dynamic_index_in_dim(factor, pair_index, 0, keepdims=False).astype(F32)
    return jnp.where(half_index == 1, jnp.roll(chosen, rank, axis=0), chosen)


def body(right_side, leaf_inverse, basis_one, basis_two, factor_one, factor_two):
    rank = basis_one.shape[1]
    rows, width = right_side.shape
    fine_bits = lax.axis_size("gy").bit_length() - 1
    total_bits = fine_bits + lax.axis_size("gx").bit_length() - 1
    flat_index = lax.axis_index("gx") * lax.axis_size("gy") + lax.axis_index("gy")
    two_bits, one_bits = total_bits - 2, total_bits - 1
    half = rank + rank // 2 + SUB
    solved, keep, give = call(
        local_kernel,
        [(rows, 2 * rank + width), (half, rank), (half, rank)],
        right_side,
        leaf_inverse,
        basis_one,
        basis_two,
    )
    total = keep + partner(give, "gy", 1)
    for bit in range(1, fine_bits):
        total = total + partner(total, "gy", 2**bit)
    for bit in range(two_bits - fine_bits):
        total = total + partner(total, "gx", 2**bit)
    sibling = partner(total, "gx", 2 ** (two_bits - fine_bits))
    mine = jnp.stack((total, sibling))
    other = partner(mine, "gy", 1)
    products, update = call(
        second_kernel,
        [(rank, rank + width), (rank, rank + width)],
        mine,
        other,
        pick_factor(factor_two, flat_index, two_bits, rank),
    )
    others = partner(products, "gx", 2 ** (one_bits - fine_bits))
    (result,) = call(
        first_kernel,
        [(rows, width)],
        products,
        others,
        pick_factor(factor_one, flat_index, one_bits, rank),
        update,
        solved,
    )
    return result


def solution(mesh):
    split = P(("gx", "gy"), None)
    return jax.shard_map(
        body,
        mesh=mesh,
        in_specs=(split, split, split, split, P(), P()),
        out_specs=split,
        check_vma=False,
    )
```

time: 276 us -> 62.8 us (0.23)
  other arithmetic: 111 us -> 0.15 us
  waiting for transfers between devices: 118 us -> 16.8 us
  Pallas kernels: 0 us -> 31.3 us
  between operations: 16.5 us -> 0.16 us
  matrix products: 15.5 us -> 0 us
  local copies, waits for them, and re-layouts: 10.8 us -> 4.89 us
  starting transfers between devices: 4.7 us -> 9.24 us
    another operation x18 -> x1, other arithmetic: 109 us -> 0.01 us  [body(): mine = jnp.stack((total, sibling))]
    psum x2 -> x0, waiting for transfers between devices: 107 us -> none  [group_total(): packed = lax.psum(packed, 'gy')]
    pallas_call x0 -> x3, Pallas kernels: none -> 31.3 us  [call(): pl.pallas_call(kernel, out_shape=[jax.ShapeDtypeStruct(shape, F32) for sh...]
    dot_general x21 -> x0, matrix products: 11.4 us -> none  [matmul(): jnp.dot(left, right, precision=HIGH, preferred_element_type=jnp.float32)]
    another operation x17 -> x0, local copies, waits for them, and re-layouts: 8.2 us -> none
    ppermute x3 -> x6, waiting for transfers between devices: 10.3 us -> 16.8 us  [partner(): return lax.ppermute(value, axis, pairs)]
    ppermute x3 -> x6, starting transfers between devices: 4.48 us -> 9.24 us  [partner(): return lax.ppermute(value, axis, pairs)]
    another operation x16 -> x0, matrix products: 4.1 us -> none  [the longest x6 1.59 us: solve_small(): lax.linalg.triangular_solve(lower_factor, right_terms, left_side=True, lo...]
  transfers between devices with their start and end apart: 5 -> 6, of which waited for: 5 -> 6; matrix products, arithmetic and copies ran while one was open for 0% -> 0% of each run, Pallas kernels for 0% -> 0%
where the time goes in v1:
time: 62.8 us; the launch traced here: 62.6 us
  Pallas kernels  31.3 us (50%)
  waiting for transfers between devices  16.8 us (27%)
  starting transfers between devices  9.24 us (15%)
  local copies, waits for them, and re-layouts  4.89 us (8%)
    pallas_call x3, Pallas kernels, call(): pl.pallas_call(kernel, out_shape=[jax.ShapeDtypeStruct(shape, F32) for sh...  31.3 us
    ppermute x6, waiting for transfers between devices, partner(): return lax.ppermute(value, axis, pairs)  16.8 us
    ppermute x6, starting transfers between devices, partner(): return lax.ppermute(value, axis, pairs)  9.24 us
    unnamed x11, local copies, waits for them, and re-layouts  4.08 us
  transfers between devices with their start and end apart: 6, of which 6 were waited for; matrix products, arithmetic and copies ran while one was open for 0% of the time, Pallas kernels for 0%

profile of v1, /device:TPU:0, one launch (start us, length us, event | category | flops | bytes accessed | tf_op | source)
XLA Modules:
  0.0 62.6 jit_solution(2321552136924426636)
XLA Ops:
  0.0 0.0 copy-start.1
  0.0 1.1 %copy.7.rhs_ref = f32[512,64]{1,0:T(8,128)S(1)} copy(f32[512,64]{0,1:T(8,128)} %param.6) | data formatting | bytes 262144 | tf_op args[0]
  1.1 0.0 copy-done.1
  1.1 0.0 copy-start
  1.1 1.2 %copy-done = f32[512,512]{1,0:T(8,128)S(1)} copy-done((f32[512,512]{1,0:T(8,128)S(1)}, f32[512,512]{1,0:T(8,128)}, u32[]{:S(2)}) %copy-start) | copy-done | bytes 1048600
  2.3 0.0 copy-start.2
  2.3 0.9 %copy-done.2 = f32[512,128]{1,0:T(8,128)S(1)} copy-done((f32[512,128]{1,0:T(8,128)S(1)}, f32[512,128]{1,0:T(8,128)}, u32[]{:S(2)}) %copy-start.2) | copy-done | bytes 262168
  3.3 2.8 %shard_map.64 = (f32[512,320]{1,0:T(8,128)S(1)}, f32[200,128]{1,0:T(8,128)S(1)}, f32[200,128]{1,0:T(8,128)S(1)}) custom-call(f32[512,64]{1,0:T(8,128)S(1)} %copy.7.rhs_ref, f32[512,512]{1,0:T(8,128)S(1)} %copy-done, f32[512,128]{1,0:T(8,128)S(1)} %copy-done.1, f32[512,128]{1,0:T(8,128)S(1)} %copy-done.2), custom_call_target="tpu_custom_call" | custom-call | tf_op jit(solution)/shard_map/pallas_call | solution.py:205
  6.1 0.0 copy-start.4
  6.1 0.5 collective-permute-start
  6.6 0.9 %collective-permute-done = f32[200,128]{1,0:T(8,128)S(1)} collective-permute-done((f32[200,128]{1,0:T(8,128)S(1)}, f32[200,128]{1,0:T(8,128)S(1)}, u32[]{:S(2)}, u32[]{:S(2)}) %collective-permute-start) | collective-permute-done | bytes 102432 | tf_op jit(solution)/shard_map/ppermute | solution.py:16
  7.6 3.0 %collective-permute-start.1 = (f32[200,128]{1,0:T(8,128)S(1)}, f32[200,128]{1,0:T(8,128)S(1)}, u32[]{:S(2)}, u32[]{:S(2)}) collective-permute-start(f32[200,128]{1,0:T(8,128)S(1)} %add.28), channel_id=1, source_target_pairs={{0,2},{1,3},{2,0},{3,1},{4,6},{5,7},{6,4},{7,5},{8,10},{9,11},{10,... | collective-permute-start | bytes 307208 | tf_op jit(solution)/shard_map/ppermute | solution.py:16
  10.6 0.0 copy-done.4
  10.6 3.2 %collective-permute-done.1 = f32[200,128]{1,0:T(8,128)S(1)} collective-permute-done((f32[200,128]{1,0:T(8,128)S(1)}, f32[200,128]{1,0:T(8,128)S(1)}, u32[]{:S(2)}, u32[]{:S(2)}) %collective-permute-start.1) | collective-permute-done | bytes 102432 | tf_op jit(solution)/shard_map/ppermute | solution.py:16
  13.8 2.8 %collective-permute-start.2 = (f32[200,128]{1,0:T(8,128)S(1)}, f32[200,128]{1,0:T(8,128)S(1)}, u32[]{:S(2)}, u32[]{:S(2)}) collective-permute-start(f32[200,128]{1,0:T(8,128)S(1)} %add.29), channel_id=1, source_target_pairs={{0,4},{1,5},{2,6},{3,7},{4,0},{5,1},{6,2},{7,3},{8,12},{9,13},{10,... | collective-permute-start | bytes 307208 | tf_op jit(solution)/shard_map/ppermute | solution.py:16
  16.6 0.0 copy-start.3
  16.7 0.8 %copy-done.3 = bf16[1,256,256]{2,1,0:T(8,128)(2,1)S(1)} copy-done((bf16[1,256,256]{2,1,0:T(8,128)(2,1)S(1)}, bf16[1,256,256]{2,1,0:T(8,128)(2,1)}, u32[]{:S(2)}) %copy-start.3) | copy-done | bytes 131096
  17.5 3.8 %collective-permute-done.2 = f32[200,128]{1,0:T(8,128)S(1)} collective-permute-done((f32[200,128]{1,0:T(8,128)S(1)}, f32[200,128]{1,0:T(8,128)S(1)}, u32[]{:S(2)}, u32[]{:S(2)}) %collective-permute-start.2) | collective-permute-done | bytes 102432 | tf_op jit(solution)/shard_map/ppermute | solution.py:16
  21.4 1.4 %collective-permute-start.3 = (f32[200,128]{1,0:T(8,128)S(1)}, f32[200,128]{1,0:T(8,128)S(1)}, u32[]{:S(2)}, u32[]{:S(2)}) collective-permute-start(f32[200,128]{1,0:T(8,128)S(1)} %add.30), channel_id=1, source_target_pairs={{0,8},{8,0},{16,24},{24,16},{1,9},{9,1},{17,25},{25,17},{2,10},{10... | collective-permute-start | bytes 307208 | tf_op jit(solution)/shard_map/ppermute | solution.py:16
  22.8 3.3 %collective-permute-done.3 = f32[200,128]{1,0:T(8,128)S(1)} collective-permute-done((f32[200,128]{1,0:T(8,128)S(1)}, f32[200,128]{1,0:T(8,128)S(1)}, u32[]{:S(2)}, u32[]{:S(2)}) %collective-permute-start.3) | collective-permute-done | bytes 102432 | tf_op jit(solution)/shard_map/ppermute | solution.py:16
  26.1 0.1 collective-permute-start.4
  26.2 1.4 %collective-permute-done.4.other_ref = f32[2,200,128]{2,1,0:T(8,128)S(1)} collective-permute-done((f32[2,200,128]{2,1,0:T(8,128)S(1)}, f32[2,200,128]{2,1,0:T(8,128)S(1)}, u32[]{:S(2)}, u32[]{:S(2)}) %collective-permute-start.4) | collective-permute-done | bytes 204832 | tf_op jit(solution)/shard_map/ppermute | solution.py:16
  27.6 14.3 %shard_map.65 = (f32[128,192]{1,0:T(8,128)S(1)}, f32[128,192]{1,0:T(8,128)S(1)}) custom-call(f32[2,200,128]{2,1,0:T(8,128)S(1)} %pad_maximum_fusion.mine_ref, f32[2,200,128]{2,1,0:T(8,128)S(1)} %collective-permute-done.4.other_ref, f32[256,256]{1,0:T(8,128)S(1)} %maximum_select_fusion.factor_ref), custom_call_target="tpu_custom_call" | custom-call | tf_op jit(solution)/shard_map/pallas_call | solution.py:205
  42.0 1.4 %collective-permute-start.5 = (f32[128,192]{1,0:T(8,128)S(1)}, f32[128,192]{1,0:T(8,128)S(1)}, u32[]{:S(2)}, u32[]{:S(2)}) collective-permute-start(f32[128,192]{1,0:T(8,128)S(1)} %get-tuple-element.12.mine_ref), channel_id=1, source_target_pairs={{0,16},{8,24},{16,0},{24,8},{1,17},{9,25},{17,1},{25,9},{2,18},{10... | collective-permute-start | bytes 294920 | tf_op jit(solution)/shard_map/ppermute | solution.py:16
  43.4 4.1 %collective-permute-done.5.other_ref = f32[128,192]{1,0:T(8,128)S(1)} collective-permute-done((f32[128,192]{1,0:T(8,128)S(1)}, f32[128,192]{1,0:T(8,128)S(1)}, u32[]{:S(2)}, u32[]{:S(2)}) %collective-permute-start.5) | collective-permute-done | bytes 98336 | tf_op jit(solution)/shard_map/ppermute | solution.py:16
  47.6 14.2 %shard_map.66 = f32[512,64]{1,0:T(8,128)S(1)} custom-call(f32[128,192]{1,0:T(8,128)S(1)} %get-tuple-element.12.mine_ref, f32[128,192]{1,0:T(8,128)S(1)} %collective-permute-done.5.other_ref, f32[256,256]{1,0:T(8,128)S(1)} %maximum_select_fusion.1.factor_ref, f32[128,192]{1,0:T(8,128)S(1)} %get-tuple-element.13.update_ref, ...), custom_call_target="tpu_custom_call" | custom-call | tf_op jit(solution)/shard_map/pallas_call | solution.py:205
  61.8 0.8 %copy.8 = f32[512,64]{0,1:T(8,128)} copy(f32[512,64]{1,0:T(8,128)S(1)} %shard_map.66) | data formatting | bytes 262144 | tf_op jit(solution)/shard_map/pallas_call | solution.py:205
  (10 shorter events, 0.2 us)
Async XLA Ops:
  0.0 1.1 %copy-start.1 = (f32[512,128]{1,0:T(8,128)S(1)}, f32[512,128]{1,0:T(8,128)}, u32[]{:S(2)}) copy-start(f32[512,128]{1,0:T(8,128)} %one_ref.1) | copy-start | bytes 786436
  1.1 1.2 %copy-start = (f32[512,512]{1,0:T(8,128)S(1)}, f32[512,512]{1,0:T(8,128)}, u32[]{:S(2)}) copy-start(f32[512,512]{1,0:T(8,128)} %leaf_ref.1) | copy-start | bytes 3145732
  2.3 0.9 %copy-start.2 = (f32[512,128]{1,0:T(8,128)S(1)}, f32[512,128]{1,0:T(8,128)}, u32[]{:S(2)}) copy-start(f32[512,128]{1,0:T(8,128)} %two_ref.1) | copy-start | bytes 786436
  6.1 4.5 %copy-start.4 = (bf16[2,256,256]{2,1,0:T(8,128)(2,1)S(1)}, bf16[2,256,256]{2,1,0:T(8,128)(2,1)}, u32[]{:S(2)}) copy-start(bf16[2,256,256]{2,1,0:T(8,128)(2,1)} %param.11) | copy-start | bytes 786436
  6.1 1.5 %collective-permute-start = (f32[200,128]{1,0:T(8,128)S(1)}, f32[200,128]{1,0:T(8,128)S(1)}, u32[]{:S(2)}, u32[]{:S(2)}) collective-permute-start(f32[200,128]{1,0:T(8,128)S(1)} %get-tuple-element.11), channel_id=1, source_target_pairs={{0,1},{1,0},{2,3},{3,2},{4,5},{5,4},{6,7},{7,6},{8,9},{9,8},{10,11... | collective-permute-start | bytes 307208 | tf_op jit(solution)/shard_map/ppermute | solution.py:16
  7.6 6.2 %collective-permute-start.1 = (f32[200,128]{1,0:T(8,128)S(1)}, f32[200,128]{1,0:T(8,128)S(1)}, u32[]{:S(2)}, u32[]{:S(2)}) collective-permute-start(f32[200,128]{1,0:T(8,128)S(1)} %add.28), channel_id=1, source_target_pairs={{0,2},{1,3},{2,0},{3,1},{4,6},{5,7},{6,4},{7,5},{8,10},{9,11},{10,... | collective-permute-start | bytes 307208 | tf_op jit(solution)/shard_map/ppermute | solution.py:16
  13.8 7.6 %collective-permute-start.2 = (f32[200,128]{1,0:T(8,128)S(1)}, f32[200,128]{1,0:T(8,128)S(1)}, u32[]{:S(2)}, u32[]{:S(2)}) collective-permute-start(f32[200,128]{1,0:T(8,128)S(1)} %add.29), channel_id=1, source_target_pairs={{0,4},{1,5},{2,6},{3,7},{4,0},{5,1},{6,2},{7,3},{8,12},{9,13},{10,... | collective-permute-start | bytes 307208 | tf_op jit(solution)/shard_map/ppermute | solution.py:16
  16.6 0.9 %copy-start.3 = (bf16[1,256,256]{2,1,0:T(8,128)(2,1)S(1)}, bf16[1,256,256]{2,1,0:T(8,128)(2,1)}, u32[]{:S(2)}) copy-start(bf16[1,256,256]{2,1,0:T(8,128)(2,1)} %param.10) | copy-start | bytes 393220
  21.4 4.7 %collective-permute-start.3 = (f32[200,128]{1,0:T(8,128)S(1)}, f32[200,128]{1,0:T(8,128)S(1)}, u32[]{:S(2)}, u32[]{:S(2)}) collective-permute-start(f32[200,128]{1,0:T(8,128)S(1)} %add.30), channel_id=1, source_target_pairs={{0,8},{8,0},{16,24},{24,16},{1,9},{9,1},{17,25},{25,17},{2,10},{10... | collective-permute-start | bytes 307208 | tf_op jit(solution)/shard_map/ppermute | solution.py:16
  26.1 1.5 %collective-permute-start.4 = (f32[2,200,128]{2,1,0:T(8,128)S(1)}, f32[2,200,128]{2,1,0:T(8,128)S(1)}, u32[]{:S(2)}, u32[]{:S(2)}) collective-permute-start(f32[2,200,128]{2,1,0:T(8,128)S(1)} %pad_maximum_fusion.mine_ref), channel_id=1, source_target_pairs={{0,1},{1,0},{2,3},{3,2},{4,5},{5,4},{6,7},{7,6},{8,9},{9,8},{10,11... | collective-permute-start | bytes 614408 | tf_op jit(solution)/shard_map/ppermute | solution.py:16
  42.0 5.6 %collective-permute-start.5 = (f32[128,192]{1,0:T(8,128)S(1)}, f32[128,192]{1,0:T(8,128)S(1)}, u32[]{:S(2)}, u32[]{:S(2)}) collective-permute-start(f32[128,192]{1,0:T(8,128)S(1)} %get-tuple-element.12.mine_ref), channel_id=1, source_target_pairs={{0,16},{8,24},{16,0},{24,8},{1,17},{9,25},{17,1},{25,9},{2,18},{10... | collective-permute-start | bytes 294920 | tf_op jit(solution)/shard_map/ppermute | solution.py:16

commit v2 on v0

v2 whole, which is shorter than its diff:
```python
import jax
import jax.numpy as jnp
from jax import lax
from jax.experimental import pallas as pl
from jax.experimental.pallas import tpu as pltpu
from jax.sharding import PartitionSpec as P

F32 = jnp.float32
BF16 = jnp.bfloat16
SUB = 8
NEAR = 2
VMEM_BYTES = 32 * 1024 * 1024
LOCAL_VMEM_BYTES = 107 * 512 * 1024

NN = (((1,), (0,)), ((), ()))
NT = (((1,), (1,)), ((), ()))


def partner(value, axis, mask):
    pairs = [(source, source ^ mask) for source in range(lax.axis_size(axis))]
    return lax.ppermute(value, axis, pairs)


def single(left, right, dims=NN):
    return lax.dot_general(left, right, dims, preferred_element_type=F32)


def times_factor(value, factor, dims=NN):
    high, low = split_pair(value)
    return single(high, factor, dims) + single(low, factor, dims)


def factor_times(factor, value):
    high, low = split_pair(value)
    return single(factor, high) + single(factor, low)


def split_pair(value):
    high = value.astype(BF16)
    return high, (value - high.astype(F32)).astype(BF16)


def pair_matmul(left, right, dims=NN):
    return single(left[0], right[0], dims) + (
        single(left[0], right[1], dims) + single(left[1], right[0], dims)
    )


def matmul(left, right, dims=NN):
    return pair_matmul(split_pair(left), split_pair(right), dims)


def tree_sum(terms):
    terms = list(terms)
    while len(terms) > 1:
        terms = [
            terms[i] + terms[i + 1] if i + 1 < len(terms) else terms[i]
            for i in range(0, len(terms), 2)
        ]
    return terms[0]


def across(panel, lane):
    return jnp.broadcast_to(panel[:, lane : lane + 1], panel.shape)


def down(panel, row):
    return jnp.broadcast_to(panel[row : row + 1, :], panel.shape)


def sweep_columns(columns, row_at):
    columns = list(columns)
    for t in range(SUB):
        pivot = columns[t]
        scale = 1.0 / down(pivot, t)
        here = row_at == t
        for j in range(SUB):
            if j != t:
                weight = down(columns[j], t) * scale
                columns[j] = jnp.where(here, weight, columns[j] - pivot * weight)
        columns[t] = jnp.where(here, scale, -(pivot * scale))
    return columns


def inverse_spd(matrix):
    order = matrix.shape[0]
    count = order // SUB
    shape = (SUB, order)
    row_at = lax.broadcasted_iota(jnp.int32, shape, 0)
    lane_at = lax.broadcasted_iota(jnp.int32, shape, 1)
    rows = [matrix[SUB * i : SUB * (i + 1), :] for i in range(count)]

    def place(panel, k):
        parts = [panel]
        if k > 0:
            parts = [jnp.zeros((SUB * k, order), F32)] + parts
        if k < count - 1:
            parts = parts + [jnp.zeros((SUB * (count - 1 - k), order), F32)]
        return jnp.concatenate(parts, axis=0)

    block = [across(rows[0], j) for j in range(SUB)]
    beside = [across(rows[1], a) for a in range(SUB)]
    ahead = [across(rows[1], SUB + j) for j in range(SUB)]
    spread_of = {i: [across(rows[i], a) for a in range(SUB)] for i in range(2, 1 + NEAR)}
    for k in range(count):
        base = SUB * k
        inverse = sweep_columns(block, row_at)
        inside = (lane_at >= base) & (lane_at < base + SUB)
        unit = jnp.where(lane_at - base == row_at, 1.0, 0.0)
        pivot_row = jnp.where(inside, unit, rows[k])
        scaled = tree_sum(inverse[b] * down(pivot_row, b) for b in range(SUB))
        if k < count - 1:
            weights = [
                tree_sum(down(inverse[b], a) * beside[b] for b in range(SUB)) for a in range(SUB)
            ]
            block = [
                ahead[j] - tree_sum(beside[a] * down(weights[a], j) for a in range(SUB))
                for j in range(SUB)
            ]
        spread = [down(scaled, a) for a in range(SUB)]
        near = list(range(k + 1, min(count, k + 1 + NEAR)))
        spread_of[k + 1] = beside
        for i in reversed(near):
            rows[i] = jnp.where(inside, 0.0, rows[i]) - tree_sum(
                spread_of[i][a] * spread[a] for a in range(SUB)
            )
        far = [i for i in range(count) if i != k and i not in near]
        left_high, left_mid = split_pair(jnp.concatenate([rows[i] for i in far], axis=0))
        scaled_high = scaled.astype(BF16).astype(F32)
        right_high = place(scaled_high, k).astype(BF16)
        right_mid = place(scaled - scaled_high, k).astype(BF16)
        update = single(
            jnp.concatenate((left_high, left_mid), axis=1),
            jnp.concatenate((right_high, right_high), axis=0),
        ) + single(left_high, right_mid)
        for place_at, i in enumerate(far):
            rows[i] = (
                jnp.where(inside, 0.0, rows[i]) - update[SUB * place_at : SUB * (place_at + 1)]
            )
        rows[k] = scaled
        if k < count - 2:
            after = base + SUB
            beside = [across(rows[k + 2], after + a) for a in range(SUB)]
            ahead = [across(rows[k + 2], after + SUB + j) for j in range(SUB)]
            spread_of = {
                i: [across(rows[i], after + a) for a in range(SUB)]
                for i in range(k + 3, min(count, k + 2 + NEAR))
            }
    return jnp.concatenate(rows, axis=0)


def add_eye(system):
    row_at = lax.broadcasted_iota(jnp.int32, system.shape, 0)
    lane_at = lax.broadcasted_iota(jnp.int32, system.shape, 1)
    return system + jnp.where(row_at == lane_at, 1.0, 0.0)


def capacitance_solve(grams, terms, factor, flipped, rank):
    wide = jnp.concatenate(
        [
            times_factor(gram, factor[side * rank : (side + 1) * rank])
            for side, gram in enumerate(grams)
        ],
        axis=0,
    )
    system = add_eye(factor_times(flipped, wide))
    rights = times_factor(terms, factor)
    corner = system[:rank, rank:]
    inverse = inverse_spd(system[:rank, :rank])
    head = matmul(inverse, corner)
    rest = system[rank:, rank:] - matmul(system[rank:, :rank], head)
    first = rights[:, :rank]
    second = rights[:, rank:] - matmul(first, head)
    lead = matmul(first, inverse)
    low = matmul(second, inverse_spd(rest))
    high = lead - matmul(low, head, NT)
    return times_factor(jnp.concatenate((high, low), axis=1), flipped)


def local_kernel(
    rhs_hbm, leaf_hbm, one_hbm, two_hbm, solved_ref, keep_ref, give_ref,
    rhs_ref, leaf_ref, bases_ref, sems,
):
    rank = one_hbm.shape[1]
    rows = leaf_hbm.shape[0]
    chunk = 2 * rank
    copies = [
        pltpu.make_async_copy(two_hbm, bases_ref.at[:, :rank], sems.at[0]),
        pltpu.make_async_copy(one_hbm, bases_ref.at[:, rank:], sems.at[1]),
        pltpu.make_async_copy(rhs_hbm, rhs_ref, sems.at[2]),
    ] + [
        pltpu.make_async_copy(leaf_hbm.at[at : at + chunk], leaf_ref.at[at : at + chunk], sem)
        for at, sem in ((c * chunk, sems.at[3 + c]) for c in range(rows // chunk))
    ]
    for copy in copies:
        copy.start()
    for copy in copies[:3]:
        copy.wait()
    bases = bases_ref[...]
    left = split_pair(jnp.concatenate((bases.T, rhs_ref[...]), axis=0))
    bases = split_pair(bases)
    solved = None
    for c in range(rows // chunk):
        copies[3 + c].wait()
        at = c * chunk
        part = pair_matmul(
            [piece[:, at : at + chunk] for piece in left], split_pair(leaf_ref[at : at + chunk, :])
        )
        solved = part if solved is None else solved + part
    solved_ref[...] = solved
    products = pair_matmul(split_pair(solved), bases)
    g22 = products[:rank, :rank]
    g12 = products[rank : 2 * rank, :rank]
    g11 = products[rank : 2 * rank, rank:]
    terms = products[2 * rank :]
    row_at = lax.broadcasted_iota(jnp.int32, (rank, rank), 0)
    lane_at = lax.broadcasted_iota(jnp.int32, (rank, rank), 1)
    both = jnp.where(row_at >= lane_at, g22, g11)
    diagonal = jnp.sum(jnp.where(row_at == lane_at, g11, 0.0), axis=0, keepdims=True)
    pad = jnp.broadcast_to(diagonal, (SUB, rank))
    low = jnp.concatenate((both, terms[:, :rank], pad), axis=0)
    high = jnp.concatenate((g12, terms[:, rank:], pad), axis=0)
    upper = lax.axis_index("gy") % 2 == 1
    keep_ref[...] = jnp.where(upper, high, low)
    give_ref[...] = jnp.where(upper, low, high)


def factor_kernel(one_ref, two_ref, *out_refs):
    fine = lax.axis_size("gy")
    count = lax.axis_size("gx") * fine
    flat = lax.axis_index("gx") * fine + lax.axis_index("gy")
    for level, ref in ((1, one_ref), (2, two_ref)):
        block = count // 2**level
        chosen = ref[flat // (2 * block)].astype(F32)
        rank = chosen.shape[0] // 2
        swapped = jnp.concatenate((chosen[rank:], chosen[:rank]), axis=0)
        chosen = jnp.where(flat // block % 2 == 1, swapped, chosen)
        out_refs[2 * level - 2][...] = chosen.astype(BF16)
        out_refs[2 * level - 1][...] = chosen.T.astype(BF16)


def second_kernel(mine_ref, other_ref, factor_ref, flipped_ref, out_ref, update_ref):
    rank = factor_ref.shape[0] // 2
    upper = lax.axis_index("gy") % 2 == 1
    row_at = lax.broadcasted_iota(jnp.int32, (rank, rank), 0)
    lane_at = lax.broadcasted_iota(jnp.int32, (rank, rank), 1)
    g22, coupling, start = [], [], []
    for side in range(2):
        mine, other = mine_ref[side], other_ref[side]
        low = jnp.where(upper, other, mine)
        high = jnp.where(upper, mine, other)
        end = low.shape[0] - SUB
        both = low[:rank]
        mirror = both.T
        diagonal = jnp.broadcast_to(low[end : end + 1], (rank, rank))
        g22.append(jnp.where(row_at >= lane_at, both, mirror))
        g11 = jnp.where(row_at < lane_at, both, jnp.where(row_at == lane_at, diagonal, mirror))
        coupling.append(jnp.concatenate((high[:rank], low[rank:end]), axis=0))
        start.append(jnp.concatenate((g11, high[rank:end]), axis=0))
    terms = jnp.concatenate(coupling, axis=1)
    update = capacitance_solve(g22, terms, factor_ref[...], flipped_ref[...], rank)
    update_ref[...] = update[:, :rank]
    out_ref[...] = start[0] + start[1] - matmul(update, terms[:rank], NT)


def first_kernel(
    mine_ref, other_ref, factor_ref, flipped_ref, update_ref, solved_ref, out_ref
):
    rank = factor_ref.shape[0] // 2
    mine, other = mine_ref[...], other_ref[...]
    terms = jnp.concatenate((mine[rank:], other[rank:]), axis=1)
    outer = capacitance_solve(
        (mine[:rank], other[:rank]), terms, factor_ref[...], flipped_ref[...], rank
    )[:, :rank]
    inner = update_ref[rank:, :] - matmul(outer, update_ref[:rank, :])
    out_ref[...] = solved_ref[2 * rank :, :] - pair_matmul(
        split_pair(jnp.concatenate((inner, outer), axis=1)),
        split_pair(solved_ref[: 2 * rank, :]),
    )


def call(kernel, shapes, *args, vmem=VMEM_BYTES, **options):
    return pl.pallas_call(
        kernel,
        out_shape=[jax.ShapeDtypeStruct(shape, dtype) for shape, dtype in shapes],
        compiler_params=pltpu.CompilerParams(vmem_limit_bytes=vmem),
        **options,
    )(*args)


def body(right_side, leaf_inverse, basis_one, basis_two, factor_one, factor_two):
    rank = basis_one.shape[1]
    rows, width = right_side.shape
    fine_bits = lax.axis_size("gy").bit_length() - 1
    total_bits = fine_bits + lax.axis_size("gx").bit_length() - 1
    two_bits, one_bits = total_bits - 2, total_bits - 1
    half = rank + width + SUB
    solved, keep, give = call(
        local_kernel,
        [((2 * rank + width, rows), F32), ((half, rank), F32), ((half, rank), F32)],
        right_side.T,
        leaf_inverse,
        basis_one,
        basis_two,
        vmem=LOCAL_VMEM_BYTES,
        in_specs=[pl.BlockSpec(memory_space=pl.ANY)] * 4,
        scratch_shapes=[
            pltpu.VMEM((width, rows), F32),
            pltpu.VMEM((rows, rows), F32),
            pltpu.VMEM((rows, 2 * rank), F32),
            pltpu.SemaphoreType.DMA((3 + rows // (2 * rank),)),
        ],
    )
    total = keep + partner(give, "gy", 1)
    factor_1, flipped_1, factor_2, flipped_2 = call(
        factor_kernel, [((2 * rank, 2 * rank), BF16)] * 4, factor_one, factor_two
    )
    factors = (factor_1, flipped_1, factor_2, flipped_2)
    for bit in range(1, fine_bits):
        received = partner(total, "gy", 2**bit)
        if bit == 1:
            received, factors = lax.optimization_barrier((received, factors))
        total = total + received
    factor_1, flipped_1, factor_2, flipped_2 = factors
    for bit in range(two_bits - fine_bits):
        total = total + partner(total, "gx", 2**bit)
    sibling = partner(total, "gx", 2 ** (two_bits - fine_bits))
    mine = jnp.stack((total, sibling))
    other = partner(mine, "gy", 1)
    products, update = call(
        second_kernel, [((rank + width, rank), F32)] * 2, mine, other, factor_2, flipped_2
    )
    others = partner(products, "gx", 2 ** (one_bits - fine_bits))
    (result,) = call(
        first_kernel,
        [((width, rows), F32)],
        products,
        others,
        factor_1,
        flipped_1,
        update,
        solved,
    )
    return result.T


def solution(mesh):
    rows = P(("gx", "gy"), None)
    return jax.shard_map(
        body,
        mesh=mesh,
        in_specs=(rows, rows, rows, rows, P(), P()),
        out_specs=rows,
        check_vma=False,
    )
```

time: 276 us -> 46.3 us (0.17)
  other arithmetic: 111 us -> 0.06 us
  waiting for transfers between devices: 118 us -> 17 us
  Pallas kernels: 0 us -> 18.9 us
  between operations: 16.5 us -> 0.06 us
  matrix products: 15.5 us -> 0 us
  local copies, waits for them, and re-layouts: 10.8 us -> 0.92 us
  starting transfers between devices: 4.7 us -> 9.24 us
    another operation x18 -> x1, other arithmetic: 109 us -> 0.01 us  [body(): mine = jnp.stack((total, sibling))]
    psum x2 -> x0, waiting for transfers between devices: 107 us -> none  [group_total(): packed = lax.psum(packed, 'gy')]
    pallas_call x0 -> x4, Pallas kernels: none -> 18.9 us  [call(): pl.pallas_call(kernel, out_shape=[jax.ShapeDtypeStruct(shape, dtype) for...]
    dot_general x21 -> x0, matrix products: 11.4 us -> none  [matmul(): jnp.dot(left, right, precision=HIGH, preferred_element_type=jnp.float32)]
    another operation x17 -> x0, local copies, waits for them, and re-layouts: 8.2 us -> none
    ppermute x3 -> x6, waiting for transfers between devices: 10.3 us -> 17 us  [partner(): return lax.ppermute(value, axis, pairs)]
    ppermute x3 -> x6, starting transfers between devices: 4.48 us -> 9.24 us  [partner(): return lax.ppermute(value, axis, pairs)]
    another operation x16 -> x0, matrix products: 4.1 us -> none  [the longest x6 1.59 us: solve_small(): lax.linalg.triangular_solve(lower_factor, right_terms, left_side=True, lo...]
  transfers between devices with their start and end apart: 5 -> 6, of which waited for: 5 -> 6; matrix products, arithmetic and copies ran while one was open for 0% -> 0% of each run, Pallas kernels for 0% -> 0%
where the time goes in v2:
time: 46.3 us; the launch traced here: 46.2 us
  Pallas kernels  18.9 us (41%)
  waiting for transfers between devices  17 us (37%)
  starting transfers between devices  9.24 us (20%)
  local copies, waits for them, and re-layouts  0.92 us (2%)
    pallas_call x4, Pallas kernels, call(): pl.pallas_call(kernel, out_shape=[jax.ShapeDtypeStruct(shape, dtype) for...  18.9 us
    ppermute x6, waiting for transfers between devices, partner(): return lax.ppermute(value, axis, pairs)  17 us
    ppermute x6, starting transfers between devices, partner(): return lax.ppermute(value, axis, pairs)  9.24 us
  transfers between devices with their start and end apart: 6, of which 6 were waited for; matrix products, arithmetic and copies ran while one was open for 0% of the time, Pallas kernels for 0%

profile of v2, /device:TPU:0, one launch (start us, length us, event | category | flops | bytes accessed | tf_op | source)
XLA Modules:
  0.0 46.2 jit_solution(12776860143471586151)
XLA Ops:
  0.0 0.0 copy-start.3
  0.0 0.9 %copy-done.3 = f32[512,64]{0,1:T(8,128)S(1)} copy-done((f32[512,64]{0,1:T(8,128)S(1)}, f32[512,64]{0,1:T(8,128)}, u32[]{:S(2)}) %copy-start.3) | copy-done | bytes 131096
  0.9 0.0 copy-start.2
  0.9 3.2 %shard_map.64 = (f32[320,512]{1,0:T(8,128)}, f32[200,128]{1,0:T(8,128)S(1)}, f32[200,128]{1,0:T(8,128)S(1)}) custom-call(f32[64,512]{1,0:T(8,128)S(1)} %bitcast.4, f32[512,512]{1,0:T(8,128)} %leaf_hbm.1, f32[512,128]{1,0:T(8,128)} %one_hbm.1, f32[512,128]{1,0:T(8,128)} %two_hbm.1), custom_call_target="tpu_custom_call" | custom-call | tf_op jit(solution)/shard_map/pallas_call | solution.py:283
  4.1 0.0 copy-start.1
  4.1 0.5 %collective-permute-start = (f32[200,128]{1,0:T(8,128)S(1)}, f32[200,128]{1,0:T(8,128)S(1)}, u32[]{:S(2)}, u32[]{:S(2)}) collective-permute-start(f32[200,128]{1,0:T(8,128)S(1)} %get-tuple-element.20), channel_id=1, source_target_pairs={{0,1},{1,0},{2,3},{3,2},{4,5},{5,4},{6,7},{7,6},{8,9},{9,8},{10,11... | collective-permute-start | bytes 307208 | tf_op jit(solution)/shard_map/ppermute | solution.py:21
  4.6 0.9 %collective-permute-done = f32[200,128]{1,0:T(8,128)S(1)} collective-permute-done((f32[200,128]{1,0:T(8,128)S(1)}, f32[200,128]{1,0:T(8,128)S(1)}, u32[]{:S(2)}, u32[]{:S(2)}) %collective-permute-start) | collective-permute-done | bytes 102432 | tf_op jit(solution)/shard_map/ppermute | solution.py:21
  5.6 3.0 %collective-permute-start.1 = (f32[200,128]{1,0:T(8,128)S(1)}, f32[200,128]{1,0:T(8,128)S(1)}, u32[]{:S(2)}, u32[]{:S(2)}) collective-permute-start(f32[200,128]{1,0:T(8,128)S(1)} %add.9), channel_id=1, source_target_pairs={{0,2},{1,3},{2,0},{3,1},{4,6},{5,7},{6,4},{7,5},{8,10},{9,11},{10,... | collective-permute-start | bytes 307208 | tf_op jit(solution)/shard_map/ppermute | solution.py:21
  8.6 0.0 copy-done.2
  8.6 0.0 copy-done.1
  8.6 0.1 shard_map.65
  8.7 3.0 %collective-permute-done.1 = f32[200,128]{1,0:T(8,128)S(1)} collective-permute-done((f32[200,128]{1,0:T(8,128)S(1)}, f32[200,128]{1,0:T(8,128)S(1)}, u32[]{:S(2)}, u32[]{:S(2)}) %collective-permute-start.1) | collective-permute-done | bytes 102432 | tf_op jit(solution)/shard_map/ppermute | solution.py:21
  11.8 0.0 copy-start
  11.8 2.8 %collective-permute-start.2 = (f32[200,128]{1,0:T(8,128)S(1)}, f32[200,128]{1,0:T(8,128)S(1)}, u32[]{:S(2)}, u32[]{:S(2)}) collective-permute-start(f32[200,128]{1,0:T(8,128)S(1)} %add.10), channel_id=1, source_target_pairs={{0,4},{1,5},{2,6},{3,7},{4,0},{5,1},{6,2},{7,3},{8,12},{9,13},{10,... | collective-permute-start | bytes 307208 | tf_op jit(solution)/shard_map/ppermute | solution.py:21
  14.6 4.8 %collective-permute-done.2 = f32[200,128]{1,0:T(8,128)S(1)} collective-permute-done((f32[200,128]{1,0:T(8,128)S(1)}, f32[200,128]{1,0:T(8,128)S(1)}, u32[]{:S(2)}, u32[]{:S(2)}) %collective-permute-start.2) | collective-permute-done | bytes 102432 | tf_op jit(solution)/shard_map/ppermute | solution.py:21
  19.4 1.4 %collective-permute-start.3 = (f32[200,128]{1,0:T(8,128)S(1)}, f32[200,128]{1,0:T(8,128)S(1)}, u32[]{:S(2)}, u32[]{:S(2)}) collective-permute-start(f32[200,128]{1,0:T(8,128)S(1)} %add.11), channel_id=1, source_target_pairs={{0,8},{8,0},{16,24},{24,16},{1,9},{9,1},{17,25},{25,17},{2,10},{10... | collective-permute-start | bytes 307208 | tf_op jit(solution)/shard_map/ppermute | solution.py:21
  20.8 3.3 %collective-permute-done.3 = f32[200,128]{1,0:T(8,128)S(1)} collective-permute-done((f32[200,128]{1,0:T(8,128)S(1)}, f32[200,128]{1,0:T(8,128)S(1)}, u32[]{:S(2)}, u32[]{:S(2)}) %collective-permute-start.3) | collective-permute-done | bytes 102432 | tf_op jit(solution)/shard_map/ppermute | solution.py:21
  24.2 0.1 collective-permute-start.4
  24.2 1.4 %collective-permute-done.4.other_ref = f32[2,200,128]{2,1,0:T(8,128)S(1)} collective-permute-done((f32[2,200,128]{2,1,0:T(8,128)S(1)}, f32[2,200,128]{2,1,0:T(8,128)S(1)}, u32[]{:S(2)}, u32[]{:S(2)}) %collective-permute-start.4) | collective-permute-done | bytes 204832 | tf_op jit(solution)/shard_map/ppermute | solution.py:21
  25.7 7.5 %shard_map.66 = (f32[192,128]{1,0:T(8,128)S(1)}, f32[192,128]{1,0:T(8,128)S(1)}) custom-call(f32[2,200,128]{2,1,0:T(8,128)S(1)} %pad_maximum_fusion.mine_ref, f32[2,200,128]{2,1,0:T(8,128)S(1)} %collective-permute-done.4.other_ref, bf16[256,256]{1,0:T(8,128)(2,1)S(1)} %get-tuple-element.26.factor_ref, bf16[256,256]{1,0:T(8,128)(2,1)S(1)} %get-tuple-element.27.flipped_ref), custom_call_target="tpu_custom_call" | custom-call | tf_op jit(solution)/shard_map/pallas_call | solution.py:283
  33.1 1.4 %collective-permute-start.5 = (f32[192,128]{1,0:T(8,128)S(1)}, f32[192,128]{1,0:T(8,128)S(1)}, u32[]{:S(2)}, u32[]{:S(2)}) collective-permute-start(f32[192,128]{1,0:T(8,128)S(1)} %get-tuple-element.28.mine_ref), channel_id=1, source_target_pairs={{0,16},{8,24},{16,0},{24,8},{1,17},{9,25},{17,1},{25,9},{2,18},{10... | collective-permute-start | bytes 294920 | tf_op jit(solution)/shard_map/ppermute | solution.py:21
  34.6 3.5 %collective-permute-done.5.other_ref = f32[192,128]{1,0:T(8,128)S(1)} collective-permute-done((f32[192,128]{1,0:T(8,128)S(1)}, f32[192,128]{1,0:T(8,128)S(1)}, u32[]{:S(2)}, u32[]{:S(2)}) %collective-permute-start.5) | collective-permute-done | bytes 98336 | tf_op jit(solution)/shard_map/ppermute | solution.py:21
  38.0 0.0 copy-done
  38.0 8.2 %shard_map.67 = f32[64,512]{1,0:T(8,128)} custom-call(f32[192,128]{1,0:T(8,128)S(1)} %get-tuple-element.28.mine_ref, f32[192,128]{1,0:T(8,128)S(1)} %collective-permute-done.5.other_ref, bf16[256,256]{1,0:T(8,128)(2,1)S(1)} %get-tuple-element.29.factor_ref, bf16[256,256]{1,0:T(8,128)(2,1)S(1)} %get-tuple-element.30.flipped_ref, ...), custom_call_target="tpu_custom_call" | custom-call | tf_op jit(solution)/shard_map/pallas_call | solution.py:283
  (4 shorter events, 0.1 us)
Async XLA Ops:
  0.0 0.9 %copy-start.3 = (f32[512,64]{0,1:T(8,128)S(1)}, f32[512,64]{0,1:T(8,128)}, u32[]{:S(2)}) copy-start(f32[512,64]{0,1:T(8,128)} %param.6) | copy-start | bytes 393220
  0.9 7.7 %copy-start.2 = (bf16[1,256,256]{2,1,0:T(8,128)(2,1)S(1)}, bf16[1,256,256]{2,1,0:T(8,128)(2,1)}, u32[]{:S(2)}) copy-start(bf16[1,256,256]{2,1,0:T(8,128)(2,1)} %one_ref.1) | copy-start | bytes 393220
  4.1 4.5 %copy-start.1 = (bf16[2,256,256]{2,1,0:T(8,128)(2,1)S(1)}, bf16[2,256,256]{2,1,0:T(8,128)(2,1)}, u32[]{:S(2)}) copy-start(bf16[2,256,256]{2,1,0:T(8,128)(2,1)} %two_ref.1) | copy-start | bytes 786436
  4.1 1.5 %collective-permute-start = (f32[200,128]{1,0:T(8,128)S(1)}, f32[200,128]{1,0:T(8,128)S(1)}, u32[]{:S(2)}, u32[]{:S(2)}) collective-permute-start(f32[200,128]{1,0:T(8,128)S(1)} %get-tuple-element.20), channel_id=1, source_target_pairs={{0,1},{1,0},{2,3},{3,2},{4,5},{5,4},{6,7},{7,6},{8,9},{9,8},{10,11... | collective-permute-start | bytes 307208 | tf_op jit(solution)/shard_map/ppermute | solution.py:21
  5.6 6.2 %collective-permute-start.1 = (f32[200,128]{1,0:T(8,128)S(1)}, f32[200,128]{1,0:T(8,128)S(1)}, u32[]{:S(2)}, u32[]{:S(2)}) collective-permute-start(f32[200,128]{1,0:T(8,128)S(1)} %add.9), channel_id=1, source_target_pairs={{0,2},{1,3},{2,0},{3,1},{4,6},{5,7},{6,4},{7,5},{8,10},{9,11},{10,... | collective-permute-start | bytes 307208 | tf_op jit(solution)/shard_map/ppermute | solution.py:21
  11.8 26.2 %copy-start = (f32[320,512]{1,0:T(8,128)S(1)}, f32[320,512]{1,0:T(8,128)}, u32[]{:S(2)}) copy-start(f32[320,512]{1,0:T(8,128)} %get-tuple-element.32.solved_ref) | copy-start | bytes 1966084
  11.8 7.6 %collective-permute-start.2 = (f32[200,128]{1,0:T(8,128)S(1)}, f32[200,128]{1,0:T(8,128)S(1)}, u32[]{:S(2)}, u32[]{:S(2)}) collective-permute-start(f32[200,128]{1,0:T(8,128)S(1)} %add.10), channel_id=1, source_target_pairs={{0,4},{1,5},{2,6},{3,7},{4,0},{5,1},{6,2},{7,3},{8,12},{9,13},{10,... | collective-permute-start | bytes 307208 | tf_op jit(solution)/shard_map/ppermute | solution.py:21
  19.4 4.7 %collective-permute-start.3 = (f32[200,128]{1,0:T(8,128)S(1)}, f32[200,128]{1,0:T(8,128)S(1)}, u32[]{:S(2)}, u32[]{:S(2)}) collective-permute-start(f32[200,128]{1,0:T(8,128)S(1)} %add.11), channel_id=1, source_target_pairs={{0,8},{8,0},{16,24},{24,16},{1,9},{9,1},{17,25},{25,17},{2,10},{10... | collective-permute-start | bytes 307208 | tf_op jit(solution)/shard_map/ppermute | solution.py:21
  24.2 1.5 %collective-permute-start.4 = (f32[2,200,128]{2,1,0:T(8,128)S(1)}, f32[2,200,128]{2,1,0:T(8,128)S(1)}, u32[]{:S(2)}, u32[]{:S(2)}) collective-permute-start(f32[2,200,128]{2,1,0:T(8,128)S(1)} %pad_maximum_fusion.mine_ref), channel_id=1, source_target_pairs={{0,1},{1,0},{2,3},{3,2},{4,5},{5,4},{6,7},{7,6},{8,9},{9,8},{10,11... | collective-permute-start | bytes 614408 | tf_op jit(solution)/shard_map/ppermute | solution.py:21
  33.1 4.9 %collective-permute-start.5 = (f32[192,128]{1,0:T(8,128)S(1)}, f32[192,128]{1,0:T(8,128)S(1)}, u32[]{:S(2)}, u32[]{:S(2)}) collective-permute-start(f32[192,128]{1,0:T(8,128)S(1)} %get-tuple-element.28.mine_ref), channel_id=1, source_target_pairs={{0,16},{8,24},{16,0},{24,8},{1,17},{9,25},{17,1},{25,9},{2,18},{10... | collective-permute-start | bytes 294920 | tf_op jit(solution)/shard_map/ppermute | solution.py:21

commit v3 on v2

--- a/solution.py
+++ b/solution.py
@@ -10,10 +10,11 @@
 SUB = 8
 NEAR = 2
 VMEM_BYTES = 32 * 1024 * 1024
-LOCAL_VMEM_BYTES = 107 * 512 * 1024
+LOCAL_VMEM_BYTES = 54988 * 1024
 
 NN = (((1,), (0,)), ((), ()))
 NT = (((1,), (1,)), ((), ()))
+TN = (((0,), (0,)), ((), ()))
 
 
 def partner(value, axis, mask):
@@ -155,7 +156,7 @@
     return system + jnp.where(row_at == lane_at, 1.0, 0.0)
 
 
-def capacitance_solve(grams, terms, factor, flipped, rank):
+def eliminate(grams, factor, flipped, rank):
     wide = jnp.concatenate(
         [
             times_factor(gram, factor[side * rank : (side + 1) * rank])
@@ -164,21 +165,14 @@
         axis=0,
     )
     system = add_eye(factor_times(flipped, wide))
-    rights = times_factor(terms, factor)
-    corner = system[:rank, rank:]
     inverse = inverse_spd(system[:rank, :rank])
-    head = matmul(inverse, corner)
-    rest = system[rank:, rank:] - matmul(system[rank:, :rank], head)
-    first = rights[:, :rank]
-    second = rights[:, rank:] - matmul(first, head)
-    lead = matmul(first, inverse)
-    low = matmul(second, inverse_spd(rest))
-    high = lead - matmul(low, head, NT)
-    return times_factor(jnp.concatenate((high, low), axis=1), flipped)
+    head = matmul(inverse, system[:rank, rank:])
+    return inverse, head, system[rank:, rank:] - matmul(system[rank:, :rank], head)
 
 
 def local_kernel(
-    rhs_hbm, leaf_hbm, one_hbm, two_hbm, solved_ref, keep_ref, give_ref,
+    rhs_hbm, leaf_hbm, one_hbm, two_hbm, solved_ref,
+    keep_gram_ref, give_gram_ref, keep_ref, give_ref,
     rhs_ref, leaf_ref, bases_ref, sems,
 ):
     rank = one_hbm.shape[1]
@@ -209,18 +203,13 @@
         solved = part if solved is None else solved + part
     solved_ref[...] = solved
     products = pair_matmul(split_pair(solved), bases)
-    g22 = products[:rank, :rank]
-    g12 = products[rank : 2 * rank, :rank]
-    g11 = products[rank : 2 * rank, rank:]
-    terms = products[2 * rank :]
-    row_at = lax.broadcasted_iota(jnp.int32, (rank, rank), 0)
-    lane_at = lax.broadcasted_iota(jnp.int32, (rank, rank), 1)
-    both = jnp.where(row_at >= lane_at, g22, g11)
-    diagonal = jnp.sum(jnp.where(row_at == lane_at, g11, 0.0), axis=0, keepdims=True)
-    pad = jnp.broadcast_to(diagonal, (SUB, rank))
-    low = jnp.concatenate((both, terms[:, :rank], pad), axis=0)
-    high = jnp.concatenate((g12, terms[:, rank:], pad), axis=0)
+    half = rank // 2
+    gram = products[:rank, :rank]
+    low = jnp.concatenate((products[rank : 2 * rank, :rank], products[2 * rank :, :rank]), axis=0)
+    high = jnp.concatenate((products[rank : 2 * rank, rank:], products[2 * rank :, rank:]), axis=0)
     upper = lax.axis_index("gy") % 2 == 1
+    keep_gram_ref[...] = jnp.where(upper, gram[half:], gram[:half])
+    give_gram_ref[...] = jnp.where(upper, gram[:half], gram[half:])
     keep_ref[...] = jnp.where(upper, high, low)
     give_ref[...] = jnp.where(upper, low, high)
 
@@ -239,44 +228,76 @@
         out_refs[2 * level - 1][...] = chosen.T.astype(BF16)
 
 
-def second_kernel(mine_ref, other_ref, factor_ref, flipped_ref, out_ref, update_ref):
+def in_order(mine, other):
+    upper = lax.axis_index("gy") % 2 == 1
+    return jnp.where(upper, other, mine), jnp.where(upper, mine, other)
+
+
+def second_head_kernel(mine_ref, other_ref, factor_ref, flipped_ref, inverse_ref, head_ref, rest_ref):
     rank = factor_ref.shape[0] // 2
-    upper = lax.axis_index("gy") % 2 == 1
-    row_at = lax.broadcasted_iota(jnp.int32, (rank, rank), 0)
-    lane_at = lax.broadcasted_iota(jnp.int32, (rank, rank), 1)
-    g22, coupling, start = [], [], []
+    grams = [
+        jnp.concatenate(in_order(mine_ref[side], other_ref[side]), axis=0) for side in range(2)
+    ]
+    inverse_ref[...], head_ref[...], rest_ref[...] = eliminate(
+        grams, factor_ref[...], flipped_ref[...], rank
+    )
+
+
+def inverse_kernel(rest_ref, head_ref, flipped_ref, out_ref, back_ref):
+    rank = rest_ref.shape[0]
+    back_ref[...] = backward(head_ref[...], flipped_ref[...], rank)
+    out_ref[...] = inverse_spd(rest_ref[...])
+
+
+def backward(head, flipped, rank):
+    high, low = split_pair(head)
+    return flipped[rank:].astype(F32) - (
+        single(high, flipped[:rank], TN) + single(low, flipped[:rank], TN)
+    )
+
+
+def second_tail_kernel(
+    mine_ref, other_ref, factor_ref, flipped_ref, inverse_ref, head_ref, inverse_rest_ref,
+    back_ref, out_ref, update_ref,
+):
+    rank = factor_ref.shape[0] // 2
+    coupling, start = [], []
     for side in range(2):
-        mine, other = mine_ref[side], other_ref[side]
-        low = jnp.where(upper, other, mine)
-        high = jnp.where(upper, mine, other)
-        end = low.shape[0] - SUB
-        both = low[:rank]
-        mirror = both.T
-        diagonal = jnp.broadcast_to(low[end : end + 1], (rank, rank))
-        g22.append(jnp.where(row_at >= lane_at, both, mirror))
-        g11 = jnp.where(row_at < lane_at, both, jnp.where(row_at == lane_at, diagonal, mirror))
-        coupling.append(jnp.concatenate((high[:rank], low[rank:end]), axis=0))
-        start.append(jnp.concatenate((g11, high[rank:end]), axis=0))
+        low, high = in_order(mine_ref[side], other_ref[side])
+        coupling.append(low)
+        start.append(high)
     terms = jnp.concatenate(coupling, axis=1)
-    update = capacitance_solve(g22, terms, factor_ref[...], flipped_ref[...], rank)
+    rights = times_factor(terms, factor_ref[...])
+    first = rights[:, :rank]
+    second = rights[:, rank:] - matmul(first, head_ref[...])
+    lead = matmul(first, inverse_ref[...])
+    low = matmul(second, inverse_rest_ref[...])
+    update = times_factor(lead, flipped_ref[:rank, :]) + matmul(low, back_ref[...])
     update_ref[...] = update[:, :rank]
     out_ref[...] = start[0] + start[1] - matmul(update, terms[:rank], NT)
 
 
-def first_kernel(
-    mine_ref, other_ref, factor_ref, flipped_ref, update_ref, solved_ref, out_ref
-):
+def correct_kernel(update_ref, solved_ref, thin_ref, bases_ref):
+    rank = update_ref.shape[1]
+    change = matmul(update_ref[...], solved_ref[:rank, :])
+    thin_ref[...] = solved_ref[2 * rank :, :] - change[rank:]
+    bases_ref[...] = solved_ref[rank : 2 * rank, :] - change[:rank]
+
+
+def first_kernel(mine_ref, other_ref, factor_ref, flipped_ref, thin_ref, bases_ref, out_ref):
     rank = factor_ref.shape[0] // 2
     mine, other = mine_ref[...], other_ref[...]
-    terms = jnp.concatenate((mine[rank:], other[rank:]), axis=1)
-    outer = capacitance_solve(
-        (mine[:rank], other[:rank]), terms, factor_ref[...], flipped_ref[...], rank
-    )[:, :rank]
-    inner = update_ref[rank:, :] - matmul(outer, update_ref[:rank, :])
-    out_ref[...] = solved_ref[2 * rank :, :] - pair_matmul(
-        split_pair(jnp.concatenate((inner, outer), axis=1)),
-        split_pair(solved_ref[: 2 * rank, :]),
-    )
+    factor, flipped = factor_ref[...], flipped_ref[:, : factor_ref.shape[0] // 2]
+    inverse, head, rest = eliminate((mine[:rank], other[:rank]), factor, flipped_ref[...], rank)
+    rights = times_factor(jnp.concatenate((mine[rank:], other[rank:]), axis=1), factor)
+    first = rights[:, :rank]
+    second = rights[:, rank:] - matmul(first, head)
+    bases = split_pair(bases_ref[...])
+    outer = times_factor(matmul(first, inverse), flipped[:rank])
+    start = thin_ref[...] - pair_matmul(split_pair(outer), bases)
+    last = split_pair(pair_matmul(split_pair(backward(head, flipped, rank)), bases))
+    low = matmul(second, inverse_spd(rest))
+    out_ref[...] = start - pair_matmul(split_pair(low), last)
 
 
 def call(kernel, shapes, *args, vmem=VMEM_BYTES, **options):
@@ -294,10 +315,10 @@
     fine_bits = lax.axis_size("gy").bit_length() - 1
     total_bits = fine_bits + lax.axis_size("gx").bit_length() - 1
     two_bits, one_bits = total_bits - 2, total_bits - 1
-    half = rank + width + SUB
-    solved, keep, give = call(
+    half, tall = (rank // 2, rank), (rank + width, rank)
+    solved, keep_gram, give_gram, keep, give = call(
         local_kernel,
-        [((2 * rank + width, rows), F32), ((half, rank), F32), ((half, rank), F32)],
+        [((2 * rank + width, rows), F32)] + [(half, F32)] * 2 + [(tall, F32)] * 2,
         right_side.T,
         leaf_inverse,
         basis_one,
@@ -311,26 +332,52 @@
             pltpu.SemaphoreType.DMA((3 + rows // (2 * rank),)),
         ],
     )
+    gram = keep_gram + partner(give_gram, "gy", 1)
     total = keep + partner(give, "gy", 1)
-    factor_1, flipped_1, factor_2, flipped_2 = call(
+    factors = call(
         factor_kernel, [((2 * rank, 2 * rank), BF16)] * 4, factor_one, factor_two
     )
-    factors = (factor_1, flipped_1, factor_2, flipped_2)
-    for bit in range(1, fine_bits):
-        received = partner(total, "gy", 2**bit)
-        if bit == 1:
+    stages = [("gy", 2**bit) for bit in range(1, fine_bits)] + [
+        ("gx", 2**bit) for bit in range(two_bits - fine_bits)
+    ]
+    sibling_mask = 2 ** (two_bits - fine_bits)
+    for index, (axis, mask) in enumerate(stages):
+        received = partner(gram, axis, mask)
+        if index == 0:
             received, factors = lax.optimization_barrier((received, factors))
-        total = total + received
+        gram = gram + received
+        total = total + partner(total, axis, mask)
     factor_1, flipped_1, factor_2, flipped_2 = factors
-    for bit in range(two_bits - fine_bits):
-        total = total + partner(total, "gx", 2**bit)
-    sibling = partner(total, "gx", 2 ** (two_bits - fine_bits))
-    mine = jnp.stack((total, sibling))
-    other = partner(mine, "gy", 1)
+    gram = jnp.stack((gram, partner(gram, "gx", sibling_mask)))
+    other_gram = partner(gram, "gy", 1)
+    other_gram, total = lax.optimization_barrier((other_gram, total))
+    received = partner(total, "gx", sibling_mask)
+    inverse, head, rest = call(
+        second_head_kernel, [((rank, rank), F32)] * 3, gram, other_gram, factor_2, flipped_2
+    )
+    rest, received = lax.optimization_barrier((rest, received))
+    total = jnp.stack((total, received))
+    other = partner(total, "gy", 1)
+    inverse_rest, back = call(
+        inverse_kernel, [((rank, rank), F32), ((rank, 2 * rank), F32)], rest, head, flipped_2
+    )
     products, update = call(
-        second_kernel, [((rank + width, rank), F32)] * 2, mine, other, factor_2, flipped_2
+        second_tail_kernel,
+        [(tall, F32)] * 2,
+        total,
+        other,
+        factor_2,
+        flipped_2,
+        inverse,
+        head,
+        inverse_rest,
+        back,
     )
     others = partner(products, "gx", 2 ** (one_bits - fine_bits))
+    thin, bases = call(
+        correct_kernel, [((width, rows), F32), ((rank, rows), F32)], update, solved
+    )
+    others, thin, bases = lax.optimization_barrier((others, thin, bases))
     (result,) = call(
         first_kernel,
         [((width, rows), F32)],
@@ -338,8 +385,8 @@
         others,
         factor_1,
         flipped_1,
-        update,
-        solved,
+        thin,
+        bases,
     )
     return result.T
 

time: 46.3 us -> 44.4 us (0.959)
  waiting for transfers between devices: 17 us -> 10.8 us
  starting transfers between devices: 9.24 us -> 13 us
  Pallas kernels: 18.9 us -> 19.5 us
    ppermute x6 -> x11, waiting for transfers between devices: 17 us -> 10.8 us  [partner(): return lax.ppermute(value, axis, pairs)]
    ppermute x6 -> x11, starting transfers between devices: 9.24 us -> 13 us  [partner(): return lax.ppermute(value, axis, pairs)]
    pallas_call x4 -> x7, Pallas kernels: 18.9 us -> 19.5 us  [call(): pl.pallas_call(kernel, out_shape=[jax.ShapeDtypeStruct(shape, dtype) for...]
  transfers between devices with their start and end apart: 6 -> 11, of which waited for: 6 -> 6; matrix products, arithmetic and copies ran while one was open for 0% -> 0% of each run, Pallas kernels for 0% -> 16%
where the time goes in v3:
time: 44.4 us; the launch traced here: 44.2 us
  Pallas kernels  19.5 us (44%)
  starting transfers between devices  13 us (29%)
  waiting for transfers between devices  10.8 us (24%)
  local copies, waits for them, and re-layouts  0.7 us (2%)
    pallas_call x7, Pallas kernels, call(): pl.pallas_call(kernel, out_shape=[jax.ShapeDtypeStruct(shape, dtype) for...  19.5 us
    ppermute x11, starting transfers between devices, partner(): return lax.ppermute(value, axis, pairs)  13 us
    ppermute x11, waiting for transfers between devices, partner(): return lax.ppermute(value, axis, pairs)  10.8 us
  transfers between devices with their start and end apart: 11, of which 6 were waited for; matrix products, arithmetic and copies ran while one was open for 0% of the time, Pallas kernels for 16%

profile of v3, /device:TPU:0, one launch (start us, length us, event | category | flops | bytes accessed | tf_op | source)
XLA Modules:
  0.0 44.2 jit_solution(1575335496619296422)
XLA Ops:
  0.0 3.5 %shard_map.64 = (f32[320,512]{1,0:T(8,128)}, f32[64,128]{1,0:T(8,128)S(1)}, f32[64,128]{1,0:T(8,128)S(1)}, f32[192,128]{1,0:T(8,128)S(1)}, f32[192,128]{1,0:T(8,128)}) custom-call(f32[64,512]{1,0:T(8,128)} %bitcast.8, f32[512,512]{1,0:T(8,128)} %leaf_hbm.1, f32[512,128]{1,0:T(8,128)} %one_hbm.1, f32[512,128]{1,0:T(8,128)} %two_hbm.1), custom_call_target="tpu_custom_call" | custom-call | tf_op jit(solution)/shard_map/pallas_call | solution.py:304
  3.5 0.0 copy-start.1
  3.5 0.5 %collective-permute-start.5 = (f32[192,128]{1,0:T(8,128)}, f32[192,128]{1,0:T(8,128)S(1)}, u32[]{:S(2)}, u32[]{:S(2)}) collective-permute-start(f32[192,128]{1,0:T(8,128)} %get-tuple-element.43), channel_id=1, source_target_pairs={{0,1},{1,0},{2,3},{3,2},{4,5},{5,4},{6,7},{7,6},{8,9},{9,8},{10,11... | collective-permute-start | bytes 294920 | tf_op jit(solution)/shard_map/ppermute | solution.py:22
  4.1 0.1 collective-permute-start
  4.1 1.1 %collective-permute-done = f32[64,128]{1,0:T(8,128)S(1)} collective-permute-done((f32[64,128]{1,0:T(8,128)S(1)}, f32[64,128]{1,0:T(8,128)S(1)}, u32[]{:S(2)}, u32[]{:S(2)}) %collective-permute-start) | collective-permute-done | bytes 32800 | tf_op jit(solution)/shard_map/ppermute | solution.py:22
  5.3 2.7 %collective-permute-start.1 = (f32[64,128]{1,0:T(8,128)S(1)}, f32[64,128]{1,0:T(8,128)S(1)}, u32[]{:S(2)}, u32[]{:S(2)}) collective-permute-start(f32[64,128]{1,0:T(8,128)S(1)} %add.18), channel_id=1, source_target_pairs={{0,2},{1,3},{2,0},{3,1},{4,6},{5,7},{6,4},{7,5},{8,10},{9,11},{10,... | collective-permute-start | bytes 98312 | tf_op jit(solution)/shard_map/ppermute | solution.py:22
  8.0 0.0 collective-permute-done.5
  8.0 0.2 collective-permute-start.6
  8.2 0.7 %copy-done.2 = bf16[1,256,256]{2,1,0:T(8,128)(2,1)S(1)} copy-done((bf16[1,256,256]{2,1,0:T(8,128)(2,1)S(1)}, bf16[1,256,256]{2,1,0:T(8,128)(2,1)}, u32[]{:S(2)}) %copy-start.2) | copy-done | bytes 131096
  8.9 0.1 shard_map.65
  9.1 0.8 %collective-permute-done.1 = f32[64,128]{1,0:T(8,128)S(1)} collective-permute-done((f32[64,128]{1,0:T(8,128)S(1)}, f32[64,128]{1,0:T(8,128)S(1)}, u32[]{:S(2)}, u32[]{:S(2)}) %collective-permute-start.1) | collective-permute-done | bytes 32800 | tf_op jit(solution)/shard_map/ppermute | solution.py:22
  9.9 3.0 %collective-permute-start.2 = (f32[64,128]{1,0:T(8,128)S(1)}, f32[64,128]{1,0:T(8,128)S(1)}, u32[]{:S(2)}, u32[]{:S(2)}) collective-permute-start(f32[64,128]{1,0:T(8,128)S(1)} %add.19), channel_id=1, source_target_pairs={{0,4},{1,5},{2,6},{3,7},{4,0},{5,1},{6,2},{7,3},{8,12},{9,13},{10,... | collective-permute-start | bytes 98312 | tf_op jit(solution)/shard_map/ppermute | solution.py:22
  12.9 2.0 %collective-permute-done.2 = f32[64,128]{1,0:T(8,128)S(1)} collective-permute-done((f32[64,128]{1,0:T(8,128)S(1)}, f32[64,128]{1,0:T(8,128)S(1)}, u32[]{:S(2)}, u32[]{:S(2)}) %collective-permute-start.2) | collective-permute-done | bytes 32800 | tf_op jit(solution)/shard_map/ppermute | solution.py:22
  15.0 1.7 %collective-permute-start.3 = (f32[64,128]{1,0:T(8,128)S(1)}, f32[64,128]{1,0:T(8,128)S(1)}, u32[]{:S(2)}, u32[]{:S(2)}) collective-permute-start(f32[64,128]{1,0:T(8,128)S(1)} %add.20), channel_id=1, source_target_pairs={{0,8},{8,0},{16,24},{24,16},{1,9},{9,1},{17,25},{25,17},{2,10},{10... | collective-permute-start | bytes 98312 | tf_op jit(solution)/shard_map/ppermute | solution.py:22
  16.7 0.0 collective-permute-done.6
  16.7 2.7 %collective-permute-start.7 = (f32[192,128]{1,0:T(8,128)S(1)}, f32[192,128]{1,0:T(8,128)S(1)}, u32[]{:S(2)}, u32[]{:S(2)}) collective-permute-start(f32[192,128]{1,0:T(8,128)S(1)} %add.22), channel_id=1, source_target_pairs={{0,4},{1,5},{2,6},{3,7},{4,0},{5,1},{6,2},{7,3},{8,12},{9,13},{10,... | collective-permute-start | bytes 294920 | tf_op jit(solution)/shard_map/ppermute | solution.py:22
  19.3 0.0 collective-permute-done.3
  19.3 0.1 collective-permute-start.4
  19.4 2.8 %collective-permute-done.7 = f32[192,128]{1,0:T(8,128)S(1)} collective-permute-done((f32[192,128]{1,0:T(8,128)S(1)}, f32[192,128]{1,0:T(8,128)S(1)}, u32[]{:S(2)}, u32[]{:S(2)}) %collective-permute-start.7) | collective-permute-done | bytes 98336 | tf_op jit(solution)/shard_map/ppermute | solution.py:22
  22.3 0.0 collective-permute-done.4.other_ref
  22.3 0.4 collective-permute-start.8
  22.7 3.6 %shard_map.66 = (f32[128,128]{1,0:T(8,128)S(1)}, f32[128,128]{1,0:T(8,128)S(1)}, f32[128,128]{1,0:T(8,128)S(1)}) custom-call(f32[2,64,128]{2,1,0:T(8,128)S(1)} %pad_maximum_fusion.1.mine_ref, f32[2,64,128]{2,1,0:T(8,128)S(1)} %collective-permute-done.4.other_ref, bf16[256,256]{1,0:T(8,128)(2,1)S(1)} %get-tuple-element.46.factor_ref, ...), custom_call_target="tpu_custom_call" | custom-call | tf_op jit(solution)/shard_map/pallas_call | solution.py:304
  26.3 0.6 %collective-permute-done.8 = f32[192,128]{1,0:T(8,128)S(1)} collective-permute-done((f32[192,128]{1,0:T(8,128)S(1)}, f32[192,128]{1,0:T(8,128)S(1)}, u32[]{:S(2)}, u32[]{:S(2)}) %collective-permute-start.8) | collective-permute-done | bytes 98336 | tf_op jit(solution)/shard_map/ppermute | solution.py:22
  27.0 0.1 collective-permute-start.9
  27.1 2.9 %shard_map.67 = (f32[128,128]{1,0:T(8,128)S(1)}, f32[128,256]{1,0:T(8,128)S(1)}) custom-call(f32[128,128]{1,0:T(8,128)S(1)} %get-tuple-element.52.rest_ref, f32[128,128]{1,0:T(8,128)S(1)} %get-tuple-element.51.head_ref, bf16[256,256]{1,0:T(8,128)(2,1)S(1)} %get-tuple-element.47.flipped_ref), custom_call_target="tpu_custom_call" | custom-call | tf_op jit(solution)/shard_map/pallas_call | solution.py:304
  30.0 0.0 collective-permute-done.9.other_ref
  30.0 1.0 %shard_map.68 = (f32[192,128]{1,0:T(8,128)S(1)}, f32[192,128]{1,0:T(8,128)S(1)}) custom-call(f32[2,192,128]{2,1,0:T(8,128)S(1)} %pad_maximum_fusion.mine_ref, f32[2,192,128]{2,1,0:T(8,128)S(1)} %collective-permute-done.9.other_ref, bf16[256,256]{1,0:T(8,128)(2,1)S(1)} %get-tuple-element.46.factor_ref, bf16[256,256]{1,0:T(8,128)(2,1)S(1)} %get-tuple-element.47.flipped_ref, ...), custom_call_target="tpu_custom_call" | custom-call | tf_op jit(solution)/shard_map/pallas_call | solution.py:304
  31.0 1.6 %collective-permute-start.10 = (f32[192,128]{1,0:T(8,128)S(1)}, f32[192,128]{1,0:T(8,128)S(1)}, u32[]{:S(2)}, u32[]{:S(2)}) collective-permute-start(f32[192,128]{1,0:T(8,128)S(1)} %get-tuple-element.55.mine_ref), channel_id=1, source_target_pairs={{0,16},{8,24},{16,0},{24,8},{1,17},{9,25},{17,1},{25,9},{2,18},{10... | collective-permute-start | bytes 294920 | tf_op jit(solution)/shard_map/ppermute | solution.py:22
  32.6 0.0 copy-done
  32.6 0.3 shard_map.69
  32.9 3.4 %collective-permute-done.10.other_ref = f32[192,128]{1,0:T(8,128)S(1)} collective-permute-done((f32[192,128]{1,0:T(8,128)S(1)}, f32[192,128]{1,0:T(8,128)S(1)}, u32[]{:S(2)}, u32[]{:S(2)}) %collective-permute-start.10) | collective-permute-done | bytes 98336 | tf_op jit(solution)/shard_map/ppermute | solution.py:22
  36.3 8.0 %shard_map.70 = f32[64,512]{1,0:T(8,128)} custom-call(f32[192,128]{1,0:T(8,128)S(1)} %get-tuple-element.55.mine_ref, f32[192,128]{1,0:T(8,128)S(1)} %collective-permute-done.10.other_ref, bf16[256,256]{1,0:T(8,128)(2,1)S(1)} %get-tuple-element.61.factor_ref, bf16[256,256]{1,0:T(8,128)(2,1)S(1)} %get-tuple-element.62.flipped_ref, ...), custom_call_target="tpu_custom_call" | custom-call | tf_op jit(solution)/shard_map/pallas_call | solution.py:304
  (11 shorter events, 0.1 us)
Async XLA Ops:
  3.5 4.7 %copy-start.1 = (bf16[2,256,256]{2,1,0:T(8,128)(2,1)S(1)}, bf16[2,256,256]{2,1,0:T(8,128)(2,1)}, u32[]{:S(2)}) copy-start(bf16[2,256,256]{2,1,0:T(8,128)(2,1)} %two_ref.1) | copy-start | bytes 786436
  3.5 4.5 %collective-permute-start.5 = (f32[192,128]{1,0:T(8,128)}, f32[192,128]{1,0:T(8,128)S(1)}, u32[]{:S(2)}, u32[]{:S(2)}) collective-permute-start(f32[192,128]{1,0:T(8,128)} %get-tuple-element.43), channel_id=1, source_target_pairs={{0,1},{1,0},{2,3},{3,2},{4,5},{5,4},{6,7},{7,6},{8,9},{9,8},{10,11... | collective-permute-start | bytes 294920 | tf_op jit(solution)/shard_map/ppermute | solution.py:22
  4.1 1.2 %collective-permute-start = (f32[64,128]{1,0:T(8,128)S(1)}, f32[64,128]{1,0:T(8,128)S(1)}, u32[]{:S(2)}, u32[]{:S(2)}) collective-permute-start(f32[64,128]{1,0:T(8,128)S(1)} %get-tuple-element.36), channel_id=1, source_target_pairs={{0,1},{1,0},{2,3},{3,2},{4,5},{5,4},{6,7},{7,6},{8,9},{9,8},{10,11... | collective-permute-start | bytes 98312 | tf_op jit(solution)/shard_map/ppermute | solution.py:22
  5.3 4.6 %collective-permute-start.1 = (f32[64,128]{1,0:T(8,128)S(1)}, f32[64,128]{1,0:T(8,128)S(1)}, u32[]{:S(2)}, u32[]{:S(2)}) collective-permute-start(f32[64,128]{1,0:T(8,128)S(1)} %add.18), channel_id=1, source_target_pairs={{0,2},{1,3},{2,0},{3,1},{4,6},{5,7},{6,4},{7,5},{8,10},{9,11},{10,... | collective-permute-start | bytes 98312 | tf_op jit(solution)/shard_map/ppermute | solution.py:22
  8.0 0.9 %copy-start.2 = (bf16[1,256,256]{2,1,0:T(8,128)(2,1)S(1)}, bf16[1,256,256]{2,1,0:T(8,128)(2,1)}, u32[]{:S(2)}) copy-start(bf16[1,256,256]{2,1,0:T(8,128)(2,1)} %one_ref.1) | copy-start | bytes 393220
  8.0 8.6 %collective-permute-start.6 = (f32[192,128]{1,0:T(8,128)S(1)}, f32[192,128]{1,0:T(8,128)S(1)}, u32[]{:S(2)}, u32[]{:S(2)}) collective-permute-start(f32[192,128]{1,0:T(8,128)S(1)} %add.21), channel_id=1, source_target_pairs={{0,2},{1,3},{2,0},{3,1},{4,6},{5,7},{6,4},{7,5},{8,10},{9,11},{10,... | collective-permute-start | bytes 294920 | tf_op jit(solution)/shard_map/ppermute | solution.py:22
  9.9 5.1 %collective-permute-start.2 = (f32[64,128]{1,0:T(8,128)S(1)}, f32[64,128]{1,0:T(8,128)S(1)}, u32[]{:S(2)}, u32[]{:S(2)}) collective-permute-start(f32[64,128]{1,0:T(8,128)S(1)} %add.19), channel_id=1, source_target_pairs={{0,4},{1,5},{2,6},{3,7},{4,0},{5,1},{6,2},{7,3},{8,12},{9,13},{10,... | collective-permute-start | bytes 98312 | tf_op jit(solution)/shard_map/ppermute | solution.py:22
  15.0 4.4 %collective-permute-start.3 = (f32[64,128]{1,0:T(8,128)S(1)}, f32[64,128]{1,0:T(8,128)S(1)}, u32[]{:S(2)}, u32[]{:S(2)}) collective-permute-start(f32[64,128]{1,0:T(8,128)S(1)} %add.20), channel_id=1, source_target_pairs={{0,8},{8,0},{16,24},{24,16},{1,9},{9,1},{17,25},{25,17},{2,10},{10... | collective-permute-start | bytes 98312 | tf_op jit(solution)/shard_map/ppermute | solution.py:22
  16.7 5.6 %collective-permute-start.7 = (f32[192,128]{1,0:T(8,128)S(1)}, f32[192,128]{1,0:T(8,128)S(1)}, u32[]{:S(2)}, u32[]{:S(2)}) collective-permute-start(f32[192,128]{1,0:T(8,128)S(1)} %add.22), channel_id=1, source_target_pairs={{0,4},{1,5},{2,6},{3,7},{4,0},{5,1},{6,2},{7,3},{8,12},{9,13},{10,... | collective-permute-start | bytes 294920 | tf_op jit(solution)/shard_map/ppermute | solution.py:22
  19.3 2.9 %collective-permute-start.4 = (f32[2,64,128]{2,1,0:T(8,128)S(1)}, f32[2,64,128]{2,1,0:T(8,128)S(1)}, u32[]{:S(2)}, u32[]{:S(2)}) collective-permute-start(f32[2,64,128]{2,1,0:T(8,128)S(1)} %pad_maximum_fusion.1.mine_ref), channel_id=1, source_target_pairs={{0,1},{1,0},{2,3},{3,2},{4,5},{5,4},{6,7},{7,6},{8,9},{9,8},{10,11... | collective-permute-start | bytes 196616 | tf_op jit(solution)/shard_map/ppermute | solution.py:22
  22.3 4.7 %collective-permute-start.8 = (f32[192,128]{1,0:T(8,128)S(1)}, f32[192,128]{1,0:T(8,128)S(1)}, u32[]{:S(2)}, u32[]{:S(2)}) collective-permute-start(f32[192,128]{1,0:T(8,128)S(1)} %add.23), channel_id=1, source_target_pairs={{0,8},{8,0},{16,24},{24,16},{1,9},{9,1},{17,25},{25,17},{2,10},{10... | collective-permute-start | bytes 294920 | tf_op jit(solution)/shard_map/ppermute | solution.py:22
  27.0 5.6 %copy-start = (f32[320,512]{1,0:T(8,128)S(1)}, f32[320,512]{1,0:T(8,128)}, u32[]{:S(2)}) copy-start(f32[320,512]{1,0:T(8,128)} %get-tuple-element.57.solved_ref) | copy-start | bytes 1966084
  27.0 3.0 %collective-permute-start.9 = (f32[2,192,128]{2,1,0:T(8,128)S(1)}, f32[2,192,128]{2,1,0:T(8,128)S(1)}, u32[]{:S(2)}, u32[]{:S(2)}) collective-permute-start(f32[2,192,128]{2,1,0:T(8,128)S(1)} %pad_maximum_fusion.mine_ref), channel_id=1, source_target_pairs={{0,1},{1,0},{2,3},{3,2},{4,5},{5,4},{6,7},{7,6},{8,9},{9,8},{10,11... | collective-permute-start | bytes 589832 | tf_op jit(solution)/shard_map/ppermute | solution.py:22
  31.0 5.3 %collective-permute-start.10 = (f32[192,128]{1,0:T(8,128)S(1)}, f32[192,128]{1,0:T(8,128)S(1)}, u32[]{:S(2)}, u32[]{:S(2)}) collective-permute-start(f32[192,128]{1,0:T(8,128)S(1)} %get-tuple-element.55.mine_ref), channel_id=1, source_target_pairs={{0,16},{8,24},{16,0},{24,8},{1,17},{9,25},{17,1},{25,9},{2,18},{10... | collective-permute-start | bytes 294920 | tf_op jit(solution)/shard_map/ppermute | solution.py:22

commit v4 on v3

--- a/solution.py
+++ b/solution.py
@@ -83,7 +83,7 @@
     return columns
 
 
-def inverse_spd(matrix):
+def factor_spd(matrix):
     order = matrix.shape[0]
     count = order // SUB
     shape = (SUB, order)
@@ -94,11 +94,12 @@
     def place(panel, k):
         parts = [panel]
         if k > 0:
-            parts = [jnp.zeros((SUB * k, order), F32)] + parts
+            parts = [jnp.zeros((SUB * k, panel.shape[1]), F32)] + parts
         if k < count - 1:
-            parts = parts + [jnp.zeros((SUB * (count - 1 - k), order), F32)]
+            parts = parts + [jnp.zeros((SUB * (count - 1 - k), panel.shape[1]), F32)]
         return jnp.concatenate(parts, axis=0)
 
+    lower, upper = [], []
     block = [across(rows[0], j) for j in range(SUB)]
     beside = [across(rows[1], a) for a in range(SUB)]
     ahead = [across(rows[1], SUB + j) for j in range(SUB)]
@@ -125,20 +126,20 @@
             rows[i] = jnp.where(inside, 0.0, rows[i]) - tree_sum(
                 spread_of[i][a] * spread[a] for a in range(SUB)
             )
-        far = [i for i in range(count) if i != k and i not in near]
-        left_high, left_mid = split_pair(jnp.concatenate([rows[i] for i in far], axis=0))
-        scaled_high = scaled.astype(BF16).astype(F32)
-        right_high = place(scaled_high, k).astype(BF16)
-        right_mid = place(scaled - scaled_high, k).astype(BF16)
-        update = single(
-            jnp.concatenate((left_high, left_mid), axis=1),
-            jnp.concatenate((right_high, right_high), axis=0),
-        ) + single(left_high, right_mid)
-        for place_at, i in enumerate(far):
-            rows[i] = (
-                jnp.where(inside, 0.0, rows[i]) - update[SUB * place_at : SUB * (place_at + 1)]
-            )
-        rows[k] = scaled
+        far = list(range(k + 1 + NEAR, count))
+        if far:
+            left = jnp.concatenate([rows[i] for i in far], axis=0)
+            left_rest = left - left.astype(BF16).astype(F32)
+            right = scaled.astype(BF16).astype(F32)
+            both = single(left, place(jnp.concatenate((right, scaled - right), axis=1), k))
+            update = both[:, :order] + both[:, order:] + single(left_rest, place(right, k))
+            for place_at, i in enumerate(far):
+                rows[i] = (
+                    jnp.where(inside, 0.0, rows[i]) - update[SUB * place_at : SUB * (place_at + 1)]
+                )
+        done = lane_at < base + SUB
+        lower.append(jnp.where(done, pivot_row, 0.0))
+        upper.append(jnp.where(done, scaled, 0.0))
         if k < count - 2:
             after = base + SUB
             beside = [across(rows[k + 2], after + a) for a in range(SUB)]
@@ -147,7 +148,7 @@
                 i: [across(rows[i], after + a) for a in range(SUB)]
                 for i in range(k + 3, min(count, k + 2 + NEAR))
             }
-    return jnp.concatenate(rows, axis=0)
+    return jnp.concatenate(lower, axis=0), jnp.concatenate(upper, axis=0)
 
 
 def add_eye(system):
@@ -165,9 +166,17 @@
         axis=0,
     )
     system = add_eye(factor_times(flipped, wide))
-    inverse = inverse_spd(system[:rank, :rank])
-    head = matmul(inverse, system[:rank, rank:])
-    return inverse, head, system[rank:, rank:] - matmul(system[rank:, :rank], head)
+    lower, scaled = factor_spd(system[:rank, :rank])
+    beside = matmul(jnp.concatenate((lower, scaled), axis=0), system[:rank, rank:])
+    rest = system[rank:, rank:] - matmul(beside[:rank], beside[rank:], TN)
+    return lower, scaled, beside[rank:], rest
+
+
+def backward(head, flipped, rank):
+    high, low = split_pair(head)
+    return flipped[rank:].astype(F32) - (
+        single(high, flipped[:rank], TN) + single(low, flipped[:rank], TN)
+    )
 
 
 def local_kernel(
@@ -233,46 +242,36 @@
     return jnp.where(upper, other, mine), jnp.where(upper, mine, other)
 
 
-def second_head_kernel(mine_ref, other_ref, factor_ref, flipped_ref, inverse_ref, head_ref, rest_ref):
+def second_head_kernel(mine_ref, other_ref, factor_ref, flipped_ref, *out_refs):
     rank = factor_ref.shape[0] // 2
     grams = [
         jnp.concatenate(in_order(mine_ref[side], other_ref[side]), axis=0) for side in range(2)
     ]
-    inverse_ref[...], head_ref[...], rest_ref[...] = eliminate(
-        grams, factor_ref[...], flipped_ref[...], rank
-    )
-
-
-def inverse_kernel(rest_ref, head_ref, flipped_ref, out_ref, back_ref):
+    parts = eliminate(grams, factor_ref[...], flipped_ref[...], rank)
+    for ref, part in zip(out_refs, parts):
+        ref[...] = part
+
+
+def kernel_of_pair(lower_ref, scaled_ref, beside_ref, rest_ref, flipped_ref, out_ref):
     rank = rest_ref.shape[0]
-    back_ref[...] = backward(head_ref[...], flipped_ref[...], rank)
-    out_ref[...] = inverse_spd(rest_ref[...])
-
-
-def backward(head, flipped, rank):
-    high, low = split_pair(head)
-    return flipped[rank:].astype(F32) - (
-        single(high, flipped[:rank], TN) + single(low, flipped[:rank], TN)
-    )
-
-
-def second_tail_kernel(
-    mine_ref, other_ref, factor_ref, flipped_ref, inverse_ref, head_ref, inverse_rest_ref,
-    back_ref, out_ref, update_ref,
-):
-    rank = factor_ref.shape[0] // 2
+    flipped = flipped_ref[...]
+    head = matmul(lower_ref[...], beside_ref[...], TN)
+    back = backward(head, flipped, rank)
+    ahead = times_factor(jnp.concatenate((lower_ref[...], scaled_ref[...]), axis=0), flipped[:rank])
+    base = matmul(ahead[:rank], ahead[rank:], TN)
+    last = matmul(jnp.concatenate(factor_spd(rest_ref[...]), axis=0), back)
+    out_ref[...] = base + matmul(last[:rank], last[rank:], TN)
+
+
+def second_tail_kernel(mine_ref, other_ref, pair_ref, out_ref, update_ref):
+    rank = pair_ref.shape[0] // 2
     coupling, start = [], []
     for side in range(2):
         low, high = in_order(mine_ref[side], other_ref[side])
         coupling.append(low)
         start.append(high)
     terms = jnp.concatenate(coupling, axis=1)
-    rights = times_factor(terms, factor_ref[...])
-    first = rights[:, :rank]
-    second = rights[:, rank:] - matmul(first, head_ref[...])
-    lead = matmul(first, inverse_ref[...])
-    low = matmul(second, inverse_rest_ref[...])
-    update = times_factor(lead, flipped_ref[:rank, :]) + matmul(low, back_ref[...])
+    update = matmul(terms, pair_ref[...])
     update_ref[...] = update[:, :rank]
     out_ref[...] = start[0] + start[1] - matmul(update, terms[:rank], NT)
 
@@ -288,16 +287,19 @@
     rank = factor_ref.shape[0] // 2
     mine, other = mine_ref[...], other_ref[...]
     factor, flipped = factor_ref[...], flipped_ref[:, : factor_ref.shape[0] // 2]
-    inverse, head, rest = eliminate((mine[:rank], other[:rank]), factor, flipped_ref[...], rank)
+    lower, scaled, beside, rest = eliminate(
+        (mine[:rank], other[:rank]), factor, flipped_ref[...], rank
+    )
+    head = matmul(lower, beside, TN)
     rights = times_factor(jnp.concatenate((mine[rank:], other[rank:]), axis=1), factor)
     first = rights[:, :rank]
     second = rights[:, rank:] - matmul(first, head)
     bases = split_pair(bases_ref[...])
-    outer = times_factor(matmul(first, inverse), flipped[:rank])
+    outer = times_factor(matmul(matmul(first, lower, NT), scaled), flipped[:rank])
     start = thin_ref[...] - pair_matmul(split_pair(outer), bases)
-    last = split_pair(pair_matmul(split_pair(backward(head, flipped, rank)), bases))
-    low = matmul(second, inverse_spd(rest))
-    out_ref[...] = start - pair_matmul(split_pair(low), last)
+    last = pair_matmul(split_pair(backward(head, flipped, rank)), bases)
+    lower, scaled = factor_spd(rest)
+    out_ref[...] = start - matmul(matmul(second, lower, NT), matmul(scaled, last))
 
 
 def call(kernel, shapes, *args, vmem=VMEM_BYTES, **options):
@@ -352,27 +354,16 @@
     other_gram = partner(gram, "gy", 1)
     other_gram, total = lax.optimization_barrier((other_gram, total))
     received = partner(total, "gx", sibling_mask)
-    inverse, head, rest = call(
-        second_head_kernel, [((rank, rank), F32)] * 3, gram, other_gram, factor_2, flipped_2
+    lower, scaled, beside, rest = call(
+        second_head_kernel, [((rank, rank), F32)] * 4, gram, other_gram, factor_2, flipped_2
     )
     rest, received = lax.optimization_barrier((rest, received))
     total = jnp.stack((total, received))
     other = partner(total, "gy", 1)
-    inverse_rest, back = call(
-        inverse_kernel, [((rank, rank), F32), ((rank, 2 * rank), F32)], rest, head, flipped_2
-    )
-    products, update = call(
-        second_tail_kernel,
-        [(tall, F32)] * 2,
-        total,
-        other,
-        factor_2,
-        flipped_2,
-        inverse,
-        head,
-        inverse_rest,
-        back,
-    )
+    (pair,) = call(
+        kernel_of_pair, [((2 * rank, 2 * rank), F32)], lower, scaled, beside, rest, flipped_2
+    )
+    products, update = call(second_tail_kernel, [(tall, F32)] * 2, total, other, pair)
     others = partner(products, "gx", 2 ** (one_bits - fine_bits))
     thin, bases = call(
         correct_kernel, [((width, rows), F32), ((rank, rows), F32)], update, solved

time: 44.4 us -> 43.8 us (0.986)
  Pallas kernels: 19.5 us -> 18.5 us
    pallas_call x7, Pallas kernels: 19.5 us -> 18.5 us  [call(): pl.pallas_call(kernel, out_shape=[jax.ShapeDtypeStruct(shape, dtype) for...]
where the time goes in v4:
time: 43.8 us; the launch traced here: 43.6 us
  Pallas kernels  18.5 us (42%)
  starting transfers between devices  13 us (30%)
  waiting for transfers between devices  11.2 us (26%)
  local copies, waits for them, and re-layouts  0.7 us (2%)
    pallas_call x7, Pallas kernels, call(): pl.pallas_call(kernel, out_shape=[jax.ShapeDtypeStruct(shape, dtype) for...  18.5 us
    ppermute x11, starting transfers between devices, partner(): return lax.ppermute(value, axis, pairs)  13 us
    ppermute x11, waiting for transfers between devices, partner(): return lax.ppermute(value, axis, pairs)  11.2 us
  transfers between devices with their start and end apart: 11, of which 6 were waited for; matrix products, arithmetic and copies ran while one was open for 0% of the time, Pallas kernels for 16%

profile of v4, /device:TPU:0, one launch (start us, length us, event | category | flops | bytes accessed | tf_op | source)
XLA Modules:
  0.0 43.6 jit_solution(14731979685646454766)
XLA Ops:
  0.0 3.5 %shard_map.64 = (f32[320,512]{1,0:T(8,128)}, f32[64,128]{1,0:T(8,128)S(1)}, f32[64,128]{1,0:T(8,128)S(1)}, f32[192,128]{1,0:T(8,128)S(1)}, f32[192,128]{1,0:T(8,128)}) custom-call(f32[64,512]{1,0:T(8,128)} %bitcast.8, f32[512,512]{1,0:T(8,128)} %leaf_hbm.1, f32[512,128]{1,0:T(8,128)} %one_hbm.1, f32[512,128]{1,0:T(8,128)} %two_hbm.1), custom_call_target="tpu_custom_call" | custom-call | tf_op jit(solution)/shard_map/pallas_call | solution.py:306
  3.5 0.0 copy-start.1
  3.5 0.5 %collective-permute-start.5 = (f32[192,128]{1,0:T(8,128)}, f32[192,128]{1,0:T(8,128)S(1)}, u32[]{:S(2)}, u32[]{:S(2)}) collective-permute-start(f32[192,128]{1,0:T(8,128)} %get-tuple-element.42), channel_id=1, source_target_pairs={{0,1},{1,0},{2,3},{3,2},{4,5},{5,4},{6,7},{7,6},{8,9},{9,8},{10,11... | collective-permute-start | bytes 294920 | tf_op jit(solution)/shard_map/ppermute | solution.py:22
  4.1 0.1 collective-permute-start
  4.1 1.1 %collective-permute-done = f32[64,128]{1,0:T(8,128)S(1)} collective-permute-done((f32[64,128]{1,0:T(8,128)S(1)}, f32[64,128]{1,0:T(8,128)S(1)}, u32[]{:S(2)}, u32[]{:S(2)}) %collective-permute-start) | collective-permute-done | bytes 32800 | tf_op jit(solution)/shard_map/ppermute | solution.py:22
  5.3 2.7 %collective-permute-start.1 = (f32[64,128]{1,0:T(8,128)S(1)}, f32[64,128]{1,0:T(8,128)S(1)}, u32[]{:S(2)}, u32[]{:S(2)}) collective-permute-start(f32[64,128]{1,0:T(8,128)S(1)} %add.18), channel_id=1, source_target_pairs={{0,2},{1,3},{2,0},{3,1},{4,6},{5,7},{6,4},{7,5},{8,10},{9,11},{10,... | collective-permute-start | bytes 98312 | tf_op jit(solution)/shard_map/ppermute | solution.py:22
  8.0 0.0 collective-permute-done.5
  8.0 0.2 collective-permute-start.6
  8.2 0.0 copy-done.1
  8.2 0.7 %copy-done.2 = bf16[1,256,256]{2,1,0:T(8,128)(2,1)S(1)} copy-done((bf16[1,256,256]{2,1,0:T(8,128)(2,1)S(1)}, bf16[1,256,256]{2,1,0:T(8,128)(2,1)}, u32[]{:S(2)}) %copy-start.2) | copy-done | bytes 131096
  8.9 0.1 shard_map.65
  9.1 0.8 %collective-permute-done.1 = f32[64,128]{1,0:T(8,128)S(1)} collective-permute-done((f32[64,128]{1,0:T(8,128)S(1)}, f32[64,128]{1,0:T(8,128)S(1)}, u32[]{:S(2)}, u32[]{:S(2)}) %collective-permute-start.1) | collective-permute-done | bytes 32800 | tf_op jit(solution)/shard_map/ppermute | solution.py:22
  9.9 3.0 %collective-permute-start.2 = (f32[64,128]{1,0:T(8,128)S(1)}, f32[64,128]{1,0:T(8,128)S(1)}, u32[]{:S(2)}, u32[]{:S(2)}) collective-permute-start(f32[64,128]{1,0:T(8,128)S(1)} %add.19), channel_id=1, source_target_pairs={{0,4},{1,5},{2,6},{3,7},{4,0},{5,1},{6,2},{7,3},{8,12},{9,13},{10,... | collective-permute-start | bytes 98312 | tf_op jit(solution)/shard_map/ppermute | solution.py:22
  12.9 2.0 %collective-permute-done.2 = f32[64,128]{1,0:T(8,128)S(1)} collective-permute-done((f32[64,128]{1,0:T(8,128)S(1)}, f32[64,128]{1,0:T(8,128)S(1)}, u32[]{:S(2)}, u32[]{:S(2)}) %collective-permute-start.2) | collective-permute-done | bytes 32800 | tf_op jit(solution)/shard_map/ppermute | solution.py:22
  15.0 1.7 %collective-permute-start.3 = (f32[64,128]{1,0:T(8,128)S(1)}, f32[64,128]{1,0:T(8,128)S(1)}, u32[]{:S(2)}, u32[]{:S(2)}) collective-permute-start(f32[64,128]{1,0:T(8,128)S(1)} %add.20), channel_id=1, source_target_pairs={{0,8},{8,0},{16,24},{24,16},{1,9},{9,1},{17,25},{25,17},{2,10},{10... | collective-permute-start | bytes 98312 | tf_op jit(solution)/shard_map/ppermute | solution.py:22
  16.7 0.0 collective-permute-done.6
  16.7 2.7 %collective-permute-start.7 = (f32[192,128]{1,0:T(8,128)S(1)}, f32[192,128]{1,0:T(8,128)S(1)}, u32[]{:S(2)}, u32[]{:S(2)}) collective-permute-start(f32[192,128]{1,0:T(8,128)S(1)} %add.22), channel_id=1, source_target_pairs={{0,4},{1,5},{2,6},{3,7},{4,0},{5,1},{6,2},{7,3},{8,12},{9,13},{10,... | collective-permute-start | bytes 294920 | tf_op jit(solution)/shard_map/ppermute | solution.py:22
  19.3 0.0 collective-permute-done.3
  19.3 0.1 collective-permute-start.4
  19.4 2.8 %collective-permute-done.7 = f32[192,128]{1,0:T(8,128)S(1)} collective-permute-done((f32[192,128]{1,0:T(8,128)S(1)}, f32[192,128]{1,0:T(8,128)S(1)}, u32[]{:S(2)}, u32[]{:S(2)}) %collective-permute-start.7) | collective-permute-done | bytes 98336 | tf_op jit(solution)/shard_map/ppermute | solution.py:22
  22.3 0.0 collective-permute-done.4.other_ref
  22.3 0.4 collective-permute-start.8
  22.7 3.2 %shard_map.66 = (f32[128,128]{1,0:T(8,128)S(1)}, f32[128,128]{1,0:T(8,128)S(1)}, f32[128,128]{1,0:T(8,128)S(1)}, f32[128,128]{1,0:T(8,128)S(1)}) custom-call(f32[2,64,128]{2,1,0:T(8,128)S(1)} %pad_maximum_fusion.1.mine_ref, f32[2,64,128]{2,1,0:T(8,128)S(1)} %collective-permute-done.4.other_ref, bf16[256,256]{1,0:T(8,128)(2,1)S(1)} %get-tuple-element.45.factor_ref, ...), custom_call_target="tpu_custom_call" | custom-call | tf_op jit(solution)/shard_map/pallas_call | solution.py:306
  25.9 1.0 %collective-permute-done.8 = f32[192,128]{1,0:T(8,128)S(1)} collective-permute-done((f32[192,128]{1,0:T(8,128)S(1)}, f32[192,128]{1,0:T(8,128)S(1)}, u32[]{:S(2)}, u32[]{:S(2)}) %collective-permute-start.8) | collective-permute-done | bytes 98336 | tf_op jit(solution)/shard_map/ppermute | solution.py:22
  27.0 0.1 collective-permute-start.9
  27.1 3.4 %shard_map.67.pair_ref = f32[256,256]{1,0:T(8,128)S(1)} custom-call(f32[128,128]{1,0:T(8,128)S(1)} %get-tuple-element.49.lower_ref, f32[128,128]{1,0:T(8,128)S(1)} %get-tuple-element.50.scaled_ref, f32[128,128]{1,0:T(8,128)S(1)} %get-tuple-element.51.beside_ref, f32[128,128]{1,0:T(8,128)S(1)} %get-tuple-element.52.rest_ref, ...), custom_call_target="tpu_custom_call" | custom-call | tf_op jit(solution)/shard_map/pallas_call | solution.py:306
  30.5 0.0 collective-permute-done.9.other_ref
  30.5 0.5 %shard_map.68 = (f32[192,128]{1,0:T(8,128)S(1)}, f32[192,128]{1,0:T(8,128)S(1)}) custom-call(f32[2,192,128]{2,1,0:T(8,128)S(1)} %pad_maximum_fusion.mine_ref, f32[2,192,128]{2,1,0:T(8,128)S(1)} %collective-permute-done.9.other_ref, f32[256,256]{1,0:T(8,128)S(1)} %shard_map.67.pair_ref), custom_call_target="tpu_custom_call" | custom-call | tf_op jit(solution)/shard_map/pallas_call | solution.py:306
  31.0 1.6 %collective-permute-start.10 = (f32[192,128]{1,0:T(8,128)S(1)}, f32[192,128]{1,0:T(8,128)S(1)}, u32[]{:S(2)}, u32[]{:S(2)}) collective-permute-start(f32[192,128]{1,0:T(8,128)S(1)} %get-tuple-element.53.mine_ref), channel_id=1, source_target_pairs={{0,16},{8,24},{16,0},{24,8},{1,17},{9,25},{17,1},{25,9},{2,18},{10... | collective-permute-start | bytes 294920 | tf_op jit(solution)/shard_map/ppermute | solution.py:22
  32.6 0.3 shard_map.69
  32.9 3.3 %collective-permute-done.10.other_ref = f32[192,128]{1,0:T(8,128)S(1)} collective-permute-done((f32[192,128]{1,0:T(8,128)S(1)}, f32[192,128]{1,0:T(8,128)S(1)}, u32[]{:S(2)}, u32[]{:S(2)}) %collective-permute-start.10) | collective-permute-done | bytes 98336 | tf_op jit(solution)/shard_map/ppermute | solution.py:22
  36.3 7.3 %shard_map.70 = f32[64,512]{1,0:T(8,128)} custom-call(f32[192,128]{1,0:T(8,128)S(1)} %get-tuple-element.53.mine_ref, f32[192,128]{1,0:T(8,128)S(1)} %collective-permute-done.10.other_ref, bf16[256,256]{1,0:T(8,128)(2,1)S(1)} %get-tuple-element.59.factor_ref, bf16[256,256]{1,0:T(8,128)(2,1)S(1)} %get-tuple-element.60.flipped_ref, ...), custom_call_target="tpu_custom_call" | custom-call | tf_op jit(solution)/shard_map/pallas_call | solution.py:306
  (11 shorter events, 0.1 us)
Async XLA Ops:
  3.5 4.7 %copy-start.1 = (bf16[2,256,256]{2,1,0:T(8,128)(2,1)S(1)}, bf16[2,256,256]{2,1,0:T(8,128)(2,1)}, u32[]{:S(2)}) copy-start(bf16[2,256,256]{2,1,0:T(8,128)(2,1)} %two_ref.1) | copy-start | bytes 786436
  3.5 4.5 %collective-permute-start.5 = (f32[192,128]{1,0:T(8,128)}, f32[192,128]{1,0:T(8,128)S(1)}, u32[]{:S(2)}, u32[]{:S(2)}) collective-permute-start(f32[192,128]{1,0:T(8,128)} %get-tuple-element.42), channel_id=1, source_target_pairs={{0,1},{1,0},{2,3},{3,2},{4,5},{5,4},{6,7},{7,6},{8,9},{9,8},{10,11... | collective-permute-start | bytes 294920 | tf_op jit(solution)/shard_map/ppermute | solution.py:22
  4.1 1.2 %collective-permute-start = (f32[64,128]{1,0:T(8,128)S(1)}, f32[64,128]{1,0:T(8,128)S(1)}, u32[]{:S(2)}, u32[]{:S(2)}) collective-permute-start(f32[64,128]{1,0:T(8,128)S(1)} %get-tuple-element.35), channel_id=1, source_target_pairs={{0,1},{1,0},{2,3},{3,2},{4,5},{5,4},{6,7},{7,6},{8,9},{9,8},{10,11... | collective-permute-start | bytes 98312 | tf_op jit(solution)/shard_map/ppermute | solution.py:22
  5.3 4.6 %collective-permute-start.1 = (f32[64,128]{1,0:T(8,128)S(1)}, f32[64,128]{1,0:T(8,128)S(1)}, u32[]{:S(2)}, u32[]{:S(2)}) collective-permute-start(f32[64,128]{1,0:T(8,128)S(1)} %add.18), channel_id=1, source_target_pairs={{0,2},{1,3},{2,0},{3,1},{4,6},{5,7},{6,4},{7,5},{8,10},{9,11},{10,... | collective-permute-start | bytes 98312 | tf_op jit(solution)/shard_map/ppermute | solution.py:22
  8.0 0.9 %copy-start.2 = (bf16[1,256,256]{2,1,0:T(8,128)(2,1)S(1)}, bf16[1,256,256]{2,1,0:T(8,128)(2,1)}, u32[]{:S(2)}) copy-start(bf16[1,256,256]{2,1,0:T(8,128)(2,1)} %one_ref.1) | copy-start | bytes 393220
  8.0 8.6 %collective-permute-start.6 = (f32[192,128]{1,0:T(8,128)S(1)}, f32[192,128]{1,0:T(8,128)S(1)}, u32[]{:S(2)}, u32[]{:S(2)}) collective-permute-start(f32[192,128]{1,0:T(8,128)S(1)} %add.21), channel_id=1, source_target_pairs={{0,2},{1,3},{2,0},{3,1},{4,6},{5,7},{6,4},{7,5},{8,10},{9,11},{10,... | collective-permute-start | bytes 294920 | tf_op jit(solution)/shard_map/ppermute | solution.py:22
  9.9 5.1 %collective-permute-start.2 = (f32[64,128]{1,0:T(8,128)S(1)}, f32[64,128]{1,0:T(8,128)S(1)}, u32[]{:S(2)}, u32[]{:S(2)}) collective-permute-start(f32[64,128]{1,0:T(8,128)S(1)} %add.19), channel_id=1, source_target_pairs={{0,4},{1,5},{2,6},{3,7},{4,0},{5,1},{6,2},{7,3},{8,12},{9,13},{10,... | collective-permute-start | bytes 98312 | tf_op jit(solution)/shard_map/ppermute | solution.py:22
  15.0 4.4 %collective-permute-start.3 = (f32[64,128]{1,0:T(8,128)S(1)}, f32[64,128]{1,0:T(8,128)S(1)}, u32[]{:S(2)}, u32[]{:S(2)}) collective-permute-start(f32[64,128]{1,0:T(8,128)S(1)} %add.20), channel_id=1, source_target_pairs={{0,8},{8,0},{16,24},{24,16},{1,9},{9,1},{17,25},{25,17},{2,10},{10... | collective-permute-start | bytes 98312 | tf_op jit(solution)/shard_map/ppermute | solution.py:22
  16.7 5.6 %collective-permute-start.7 = (f32[192,128]{1,0:T(8,128)S(1)}, f32[192,128]{1,0:T(8,128)S(1)}, u32[]{:S(2)}, u32[]{:S(2)}) collective-permute-start(f32[192,128]{1,0:T(8,128)S(1)} %add.22), channel_id=1, source_target_pairs={{0,4},{1,5},{2,6},{3,7},{4,0},{5,1},{6,2},{7,3},{8,12},{9,13},{10,... | collective-permute-start | bytes 294920 | tf_op jit(solution)/shard_map/ppermute | solution.py:22
  19.3 2.9 %collective-permute-start.4 = (f32[2,64,128]{2,1,0:T(8,128)S(1)}, f32[2,64,128]{2,1,0:T(8,128)S(1)}, u32[]{:S(2)}, u32[]{:S(2)}) collective-permute-start(f32[2,64,128]{2,1,0:T(8,128)S(1)} %pad_maximum_fusion.1.mine_ref), channel_id=1, source_target_pairs={{0,1},{1,0},{2,3},{3,2},{4,5},{5,4},{6,7},{7,6},{8,9},{9,8},{10,11... | collective-permute-start | bytes 196616 | tf_op jit(solution)/shard_map/ppermute | solution.py:22
  22.3 4.7 %collective-permute-start.8 = (f32[192,128]{1,0:T(8,128)S(1)}, f32[192,128]{1,0:T(8,128)S(1)}, u32[]{:S(2)}, u32[]{:S(2)}) collective-permute-start(f32[192,128]{1,0:T(8,128)S(1)} %add.23), channel_id=1, source_target_pairs={{0,8},{8,0},{16,24},{24,16},{1,9},{9,1},{17,25},{25,17},{2,10},{10... | collective-permute-start | bytes 294920 | tf_op jit(solution)/shard_map/ppermute | solution.py:22
  27.0 3.5 %collective-permute-start.9 = (f32[2,192,128]{2,1,0:T(8,128)S(1)}, f32[2,192,128]{2,1,0:T(8,128)S(1)}, u32[]{:S(2)}, u32[]{:S(2)}) collective-permute-start(f32[2,192,128]{2,1,0:T(8,128)S(1)} %pad_maximum_fusion.mine_ref), channel_id=1, source_target_pairs={{0,1},{1,0},{2,3},{3,2},{4,5},{5,4},{6,7},{7,6},{8,9},{9,8},{10,11... | collective-permute-start | bytes 589832 | tf_op jit(solution)/shard_map/ppermute | solution.py:22
  27.1 5.6 %copy-start = (f32[320,512]{1,0:T(8,128)S(1)}, f32[320,512]{1,0:T(8,128)}, u32[]{:S(2)}) copy-start(f32[320,512]{1,0:T(8,128)} %get-tuple-element.55.solved_ref) | copy-start | bytes 1966084
  31.0 5.3 %collective-permute-start.10 = (f32[192,128]{1,0:T(8,128)S(1)}, f32[192,128]{1,0:T(8,128)S(1)}, u32[]{:S(2)}, u32[]{:S(2)}) collective-permute-start(f32[192,128]{1,0:T(8,128)S(1)} %get-tuple-element.53.mine_ref), channel_id=1, source_target_pairs={{0,16},{8,24},{16,0},{24,8},{1,17},{9,25},{17,1},{25,9},{2,18},{10... | collective-permute-start | bytes 294920 | tf_op jit(solution)/shard_map/ppermute | solution.py:22

commit v5 on v4

--- a/solution.py
+++ b/solution.py
@@ -263,11 +263,13 @@
     out_ref[...] = base + matmul(last[:rank], last[rank:], TN)
 
 
-def second_tail_kernel(mine_ref, other_ref, pair_ref, out_ref, update_ref):
+def second_tail_kernel(
+    mine_ref, other_ref, sibling_ref, sibling_other_ref, pair_ref, out_ref, update_ref
+):
     rank = pair_ref.shape[0] // 2
     coupling, start = [], []
-    for side in range(2):
-        low, high = in_order(mine_ref[side], other_ref[side])
+    for mine, other in ((mine_ref, other_ref), (sibling_ref, sibling_other_ref)):
+        low, high = in_order(mine[...], other[...])
         coupling.append(low)
         start.append(high)
     terms = jnp.concatenate(coupling, axis=1)
@@ -352,18 +354,18 @@
     factor_1, flipped_1, factor_2, flipped_2 = factors
     gram = jnp.stack((gram, partner(gram, "gx", sibling_mask)))
     other_gram = partner(gram, "gy", 1)
-    other_gram, total = lax.optimization_barrier((other_gram, total))
-    received = partner(total, "gx", sibling_mask)
     lower, scaled, beside, rest = call(
         second_head_kernel, [((rank, rank), F32)] * 4, gram, other_gram, factor_2, flipped_2
     )
-    rest, received = lax.optimization_barrier((rest, received))
-    total = jnp.stack((total, received))
+    rest, total = lax.optimization_barrier((rest, total))
+    received = partner(total, "gx", sibling_mask)
     other = partner(total, "gy", 1)
     (pair,) = call(
         kernel_of_pair, [((2 * rank, 2 * rank), F32)], lower, scaled, beside, rest, flipped_2
     )
-    products, update = call(second_tail_kernel, [(tall, F32)] * 2, total, other, pair)
+    received, pair = lax.optimization_barrier((received, pair))
+    total = (total, other, received, partner(received, "gy", 1))
+    products, update = call(second_tail_kernel, [(tall, F32)] * 2, *total, pair)
     others = partner(products, "gx", 2 ** (one_bits - fine_bits))
     thin, bases = call(
         correct_kernel, [((width, rows), F32), ((rank, rows), F32)], update, solved

time: 43.8 us -> 43.3 us (0.989)
  waiting for transfers between devices: 11.2 us -> 9.68 us
  starting transfers between devices: 13 us -> 14.1 us
    ppermute x11 -> x12, waiting for transfers between devices: 11.2 us -> 9.68 us  [partner(): return lax.ppermute(value, axis, pairs)]
    ppermute x11 -> x12, starting transfers between devices: 13 us -> 14.1 us  [partner(): return lax.ppermute(value, axis, pairs)]
  transfers between devices with their start and end apart: 11 -> 12, of which waited for: 6 -> 7; matrix products, arithmetic and copies ran while one was open for 0% -> 0% of each run, Pallas kernels for 16% -> 16%
where the time goes in v5:
time: 43.3 us; the launch traced here: 43.1 us
  Pallas kernels  18.5 us (43%)
  starting transfers between devices  14.1 us (33%)
  waiting for transfers between devices  9.68 us (22%)
  local copies, waits for them, and re-layouts  0.7 us (2%)
    pallas_call x7, Pallas kernels, call(): pl.pallas_call(kernel, out_shape=[jax.ShapeDtypeStruct(shape, dtype) for...  18.5 us
    ppermute x12, starting transfers between devices, partner(): return lax.ppermute(value, axis, pairs)  14.1 us
    ppermute x12, waiting for transfers between devices, partner(): return lax.ppermute(value, axis, pairs)  9.68 us
  transfers between devices with their start and end apart: 12, of which 7 were waited for; matrix products, arithmetic and copies ran while one was open for 0% of the time, Pallas kernels for 16%

profile of v5, /device:TPU:0, one launch (start us, length us, event | category | flops | bytes accessed | tf_op | source)
XLA Modules:
  0.0 43.1 jit_solution(13435013322616427039)
XLA Ops:
  0.0 3.5 %shard_map.64 = (f32[320,512]{1,0:T(8,128)}, f32[64,128]{1,0:T(8,128)S(1)}, f32[64,128]{1,0:T(8,128)S(1)}, f32[192,128]{1,0:T(8,128)S(1)}, f32[192,128]{1,0:T(8,128)}) custom-call(f32[64,512]{1,0:T(8,128)} %bitcast.5, f32[512,512]{1,0:T(8,128)} %leaf_hbm.1, f32[512,128]{1,0:T(8,128)} %one_hbm.1, f32[512,128]{1,0:T(8,128)} %two_hbm.1), custom_call_target="tpu_custom_call" | custom-call | tf_op jit(solution)/shard_map/pallas_call | solution.py:308
  3.5 0.0 copy-start.1
  3.5 0.5 %collective-permute-start.5 = (f32[192,128]{1,0:T(8,128)}, f32[192,128]{1,0:T(8,128)S(1)}, u32[]{:S(2)}, u32[]{:S(2)}) collective-permute-start(f32[192,128]{1,0:T(8,128)} %get-tuple-element.45), channel_id=1, source_target_pairs={{0,1},{1,0},{2,3},{3,2},{4,5},{5,4},{6,7},{7,6},{8,9},{9,8},{10,11... | collective-permute-start | bytes 294920 | tf_op jit(solution)/shard_map/ppermute | solution.py:22
  4.1 0.1 collective-permute-start
  4.1 1.1 %collective-permute-done = f32[64,128]{1,0:T(8,128)S(1)} collective-permute-done((f32[64,128]{1,0:T(8,128)S(1)}, f32[64,128]{1,0:T(8,128)S(1)}, u32[]{:S(2)}, u32[]{:S(2)}) %collective-permute-start) | collective-permute-done | bytes 32800 | tf_op jit(solution)/shard_map/ppermute | solution.py:22
  5.3 2.7 %collective-permute-start.1 = (f32[64,128]{1,0:T(8,128)S(1)}, f32[64,128]{1,0:T(8,128)S(1)}, u32[]{:S(2)}, u32[]{:S(2)}) collective-permute-start(f32[64,128]{1,0:T(8,128)S(1)} %add.18), channel_id=1, source_target_pairs={{0,2},{1,3},{2,0},{3,1},{4,6},{5,7},{6,4},{7,5},{8,10},{9,11},{10,... | collective-permute-start | bytes 98312 | tf_op jit(solution)/shard_map/ppermute | solution.py:22
  8.0 0.0 collective-permute-done.5
  8.0 0.2 collective-permute-start.6
  8.2 0.7 %copy-done.2 = bf16[1,256,256]{2,1,0:T(8,128)(2,1)S(1)} copy-done((bf16[1,256,256]{2,1,0:T(8,128)(2,1)S(1)}, bf16[1,256,256]{2,1,0:T(8,128)(2,1)}, u32[]{:S(2)}) %copy-start.2) | copy-done | bytes 131096
  8.9 0.1 shard_map.65
  9.1 0.8 %collective-permute-done.1 = f32[64,128]{1,0:T(8,128)S(1)} collective-permute-done((f32[64,128]{1,0:T(8,128)S(1)}, f32[64,128]{1,0:T(8,128)S(1)}, u32[]{:S(2)}, u32[]{:S(2)}) %collective-permute-start.1) | collective-permute-done | bytes 32800 | tf_op jit(solution)/shard_map/ppermute | solution.py:22
  9.9 3.0 %collective-permute-start.2 = (f32[64,128]{1,0:T(8,128)S(1)}, f32[64,128]{1,0:T(8,128)S(1)}, u32[]{:S(2)}, u32[]{:S(2)}) collective-permute-start(f32[64,128]{1,0:T(8,128)S(1)} %add.19), channel_id=1, source_target_pairs={{0,4},{1,5},{2,6},{3,7},{4,0},{5,1},{6,2},{7,3},{8,12},{9,13},{10,... | collective-permute-start | bytes 98312 | tf_op jit(solution)/shard_map/ppermute | solution.py:22
  12.9 2.0 %collective-permute-done.2 = f32[64,128]{1,0:T(8,128)S(1)} collective-permute-done((f32[64,128]{1,0:T(8,128)S(1)}, f32[64,128]{1,0:T(8,128)S(1)}, u32[]{:S(2)}, u32[]{:S(2)}) %collective-permute-start.2) | collective-permute-done | bytes 32800 | tf_op jit(solution)/shard_map/ppermute | solution.py:22
  15.0 1.7 %collective-permute-start.3 = (f32[64,128]{1,0:T(8,128)S(1)}, f32[64,128]{1,0:T(8,128)S(1)}, u32[]{:S(2)}, u32[]{:S(2)}) collective-permute-start(f32[64,128]{1,0:T(8,128)S(1)} %add.20), channel_id=1, source_target_pairs={{0,8},{8,0},{16,24},{24,16},{1,9},{9,1},{17,25},{25,17},{2,10},{10... | collective-permute-start | bytes 98312 | tf_op jit(solution)/shard_map/ppermute | solution.py:22
  16.7 0.0 collective-permute-done.6
  16.7 2.7 %collective-permute-start.7 = (f32[192,128]{1,0:T(8,128)S(1)}, f32[192,128]{1,0:T(8,128)S(1)}, u32[]{:S(2)}, u32[]{:S(2)}) collective-permute-start(f32[192,128]{1,0:T(8,128)S(1)} %add.22), channel_id=1, source_target_pairs={{0,4},{1,5},{2,6},{3,7},{4,0},{5,1},{6,2},{7,3},{8,12},{9,13},{10,... | collective-permute-start | bytes 294920 | tf_op jit(solution)/shard_map/ppermute | solution.py:22
  19.3 0.0 collective-permute-done.3
  19.3 0.1 collective-permute-start.4
  19.4 1.2 %collective-permute-done.4.other_ref = f32[2,64,128]{2,1,0:T(8,128)S(1)} collective-permute-done((f32[2,64,128]{2,1,0:T(8,128)S(1)}, f32[2,64,128]{2,1,0:T(8,128)S(1)}, u32[]{:S(2)}, u32[]{:S(2)}) %collective-permute-start.4) | collective-permute-done | bytes 65568 | tf_op jit(solution)/shard_map/ppermute | solution.py:22
  20.7 3.2 %shard_map.66 = (f32[128,128]{1,0:T(8,128)S(1)}, f32[128,128]{1,0:T(8,128)S(1)}, f32[128,128]{1,0:T(8,128)S(1)}, f32[128,128]{1,0:T(8,128)S(1)}) custom-call(f32[2,64,128]{2,1,0:T(8,128)S(1)} %pad_maximum_fusion.mine_ref, f32[2,64,128]{2,1,0:T(8,128)S(1)} %collective-permute-done.4.other_ref, bf16[256,256]{1,0:T(8,128)(2,1)S(1)} %get-tuple-element.41.factor_ref, ...), custom_call_target="tpu_custom_call" | custom-call | tf_op jit(solution)/shard_map/pallas_call | solution.py:308
  23.9 0.0 collective-permute-done.7
  23.9 1.2 %collective-permute-start.9 = (f32[192,128]{1,0:T(8,128)S(1)}, f32[192,128]{1,0:T(8,128)S(1)}, u32[]{:S(2)}, u32[]{:S(2)}) collective-permute-start(f32[192,128]{1,0:T(8,128)S(1)} %add.23.mine_ref), channel_id=1, source_target_pairs={{0,8},{8,0},{16,24},{24,16},{1,9},{9,1},{17,25},{25,17},{2,10},{10... | collective-permute-start | bytes 294920 | tf_op jit(solution)/shard_map/ppermute | solution.py:22
  25.2 3.4 %shard_map.67.pair_ref = f32[256,256]{1,0:T(8,128)S(1)} custom-call(f32[128,128]{1,0:T(8,128)S(1)} %get-tuple-element.47.lower_ref, f32[128,128]{1,0:T(8,128)S(1)} %get-tuple-element.48.scaled_ref, f32[128,128]{1,0:T(8,128)S(1)} %get-tuple-element.49.beside_ref, f32[128,128]{1,0:T(8,128)S(1)} %get-tuple-element.50.rest_ref, ...), custom_call_target="tpu_custom_call" | custom-call | tf_op jit(solution)/shard_map/pallas_call | solution.py:308
  28.6 0.3 collective-permute-done.9.sibling_ref
  28.9 0.3 collective-permute-start.10
  29.2 0.0 collective-permute-done.8.other_ref
  29.2 1.0 %collective-permute-done.10.sibling_other_ref = f32[192,128]{1,0:T(8,128)S(1)} collective-permute-done((f32[192,128]{1,0:T(8,128)S(1)}, f32[192,128]{1,0:T(8,128)S(1)}, u32[]{:S(2)}, u32[]{:S(2)}) %collective-permute-start.10) | collective-permute-done | bytes 98336 | tf_op jit(solution)/shard_map/ppermute | solution.py:22
  30.2 0.5 %shard_map.68 = (f32[192,128]{1,0:T(8,128)S(1)}, f32[192,128]{1,0:T(8,128)S(1)}) custom-call(f32[192,128]{1,0:T(8,128)S(1)} %add.23.mine_ref, f32[192,128]{1,0:T(8,128)S(1)} %collective-permute-done.8.other_ref, f32[192,128]{1,0:T(8,128)S(1)} %collective-permute-done.9.sibling_ref, f32[192,128]{1,0:T(8,128)S(1)} %collective-permute-done.10.sibling_other_ref, ...), custom_call_target="tpu_custom_call" | custom-call | tf_op jit(solution)/shard_map/pallas_call | solution.py:308
  30.7 1.6 %collective-permute-start.11 = (f32[192,128]{1,0:T(8,128)S(1)}, f32[192,128]{1,0:T(8,128)S(1)}, u32[]{:S(2)}, u32[]{:S(2)}) collective-permute-start(f32[192,128]{1,0:T(8,128)S(1)} %get-tuple-element.53.mine_ref), channel_id=1, source_target_pairs={{0,16},{8,24},{16,0},{24,8},{1,17},{9,25},{17,1},{25,9},{2,18},{10... | collective-permute-start | bytes 294920 | tf_op jit(solution)/shard_map/ppermute | solution.py:22
  32.3 0.3 shard_map.69
  32.6 3.2 %collective-permute-done.11.other_ref = f32[192,128]{1,0:T(8,128)S(1)} collective-permute-done((f32[192,128]{1,0:T(8,128)S(1)}, f32[192,128]{1,0:T(8,128)S(1)}, u32[]{:S(2)}, u32[]{:S(2)}) %collective-permute-start.11) | collective-permute-done | bytes 98336 | tf_op jit(solution)/shard_map/ppermute | solution.py:22
  35.8 7.3 %shard_map.70 = f32[64,512]{1,0:T(8,128)} custom-call(f32[192,128]{1,0:T(8,128)S(1)} %get-tuple-element.53.mine_ref, f32[192,128]{1,0:T(8,128)S(1)} %collective-permute-done.11.other_ref, bf16[256,256]{1,0:T(8,128)(2,1)S(1)} %get-tuple-element.59.factor_ref, bf16[256,256]{1,0:T(8,128)(2,1)S(1)} %get-tuple-element.60.flipped_ref, ...), custom_call_target="tpu_custom_call" | custom-call | tf_op jit(solution)/shard_map/pallas_call | solution.py:308
  (12 shorter events, 0.1 us)
Async XLA Ops:
  3.5 4.7 %copy-start.1 = (bf16[2,256,256]{2,1,0:T(8,128)(2,1)S(1)}, bf16[2,256,256]{2,1,0:T(8,128)(2,1)}, u32[]{:S(2)}) copy-start(bf16[2,256,256]{2,1,0:T(8,128)(2,1)} %two_ref.1) | copy-start | bytes 786436
  3.5 4.5 %collective-permute-start.5 = (f32[192,128]{1,0:T(8,128)}, f32[192,128]{1,0:T(8,128)S(1)}, u32[]{:S(2)}, u32[]{:S(2)}) collective-permute-start(f32[192,128]{1,0:T(8,128)} %get-tuple-element.45), channel_id=1, source_target_pairs={{0,1},{1,0},{2,3},{3,2},{4,5},{5,4},{6,7},{7,6},{8,9},{9,8},{10,11... | collective-permute-start | bytes 294920 | tf_op jit(solution)/shard_map/ppermute | solution.py:22
  4.1 1.2 %collective-permute-start = (f32[64,128]{1,0:T(8,128)S(1)}, f32[64,128]{1,0:T(8,128)S(1)}, u32[]{:S(2)}, u32[]{:S(2)}) collective-permute-start(f32[64,128]{1,0:T(8,128)S(1)} %get-tuple-element.35), channel_id=1, source_target_pairs={{0,1},{1,0},{2,3},{3,2},{4,5},{5,4},{6,7},{7,6},{8,9},{9,8},{10,11... | collective-permute-start | bytes 98312 | tf_op jit(solution)/shard_map/ppermute | solution.py:22
  5.3 4.6 %collective-permute-start.1 = (f32[64,128]{1,0:T(8,128)S(1)}, f32[64,128]{1,0:T(8,128)S(1)}, u32[]{:S(2)}, u32[]{:S(2)}) collective-permute-start(f32[64,128]{1,0:T(8,128)S(1)} %add.18), channel_id=1, source_target_pairs={{0,2},{1,3},{2,0},{3,1},{4,6},{5,7},{6,4},{7,5},{8,10},{9,11},{10,... | collective-permute-start | bytes 98312 | tf_op jit(solution)/shard_map/ppermute | solution.py:22
  8.0 0.9 %copy-start.2 = (bf16[1,256,256]{2,1,0:T(8,128)(2,1)S(1)}, bf16[1,256,256]{2,1,0:T(8,128)(2,1)}, u32[]{:S(2)}) copy-start(bf16[1,256,256]{2,1,0:T(8,128)(2,1)} %one_ref.1) | copy-start | bytes 393220
  8.0 8.6 %collective-permute-start.6 = (f32[192,128]{1,0:T(8,128)S(1)}, f32[192,128]{1,0:T(8,128)S(1)}, u32[]{:S(2)}, u32[]{:S(2)}) collective-permute-start(f32[192,128]{1,0:T(8,128)S(1)} %add.21), channel_id=1, source_target_pairs={{0,2},{1,3},{2,0},{3,1},{4,6},{5,7},{6,4},{7,5},{8,10},{9,11},{10,... | collective-permute-start | bytes 294920 | tf_op jit(solution)/shard_map/ppermute | solution.py:22
  9.9 5.1 %collective-permute-start.2 = (f32[64,128]{1,0:T(8,128)S(1)}, f32[64,128]{1,0:T(8,128)S(1)}, u32[]{:S(2)}, u32[]{:S(2)}) collective-permute-start(f32[64,128]{1,0:T(8,128)S(1)} %add.19), channel_id=1, source_target_pairs={{0,4},{1,5},{2,6},{3,7},{4,0},{5,1},{6,2},{7,3},{8,12},{9,13},{10,... | collective-permute-start | bytes 98312 | tf_op jit(solution)/shard_map/ppermute | solution.py:22
  15.0 4.4 %collective-permute-start.3 = (f32[64,128]{1,0:T(8,128)S(1)}, f32[64,128]{1,0:T(8,128)S(1)}, u32[]{:S(2)}, u32[]{:S(2)}) collective-permute-start(f32[64,128]{1,0:T(8,128)S(1)} %add.20), channel_id=1, source_target_pairs={{0,8},{8,0},{16,24},{24,16},{1,9},{9,1},{17,25},{25,17},{2,10},{10... | collective-permute-start | bytes 98312 | tf_op jit(solution)/shard_map/ppermute | solution.py:22
  16.7 7.2 %collective-permute-start.7 = (f32[192,128]{1,0:T(8,128)S(1)}, f32[192,128]{1,0:T(8,128)S(1)}, u32[]{:S(2)}, u32[]{:S(2)}) collective-permute-start(f32[192,128]{1,0:T(8,128)S(1)} %add.22), channel_id=1, source_target_pairs={{0,4},{1,5},{2,6},{3,7},{4,0},{5,1},{6,2},{7,3},{8,12},{9,13},{10,... | collective-permute-start | bytes 294920 | tf_op jit(solution)/shard_map/ppermute | solution.py:22
  19.3 1.3 %collective-permute-start.4 = (f32[2,64,128]{2,1,0:T(8,128)S(1)}, f32[2,64,128]{2,1,0:T(8,128)S(1)}, u32[]{:S(2)}, u32[]{:S(2)}) collective-permute-start(f32[2,64,128]{2,1,0:T(8,128)S(1)} %pad_maximum_fusion.mine_ref), channel_id=1, source_target_pairs={{0,1},{1,0},{2,3},{3,2},{4,5},{5,4},{6,7},{7,6},{8,9},{9,8},{10,11... | collective-permute-start | bytes 196616 | tf_op jit(solution)/shard_map/ppermute | solution.py:22
  23.9 4.9 %collective-permute-start.9 = (f32[192,128]{1,0:T(8,128)S(1)}, f32[192,128]{1,0:T(8,128)S(1)}, u32[]{:S(2)}, u32[]{:S(2)}) collective-permute-start(f32[192,128]{1,0:T(8,128)S(1)} %add.23.mine_ref), channel_id=1, source_target_pairs={{0,8},{8,0},{16,24},{24,16},{1,9},{9,1},{17,25},{25,17},{2,10},{10... | collective-permute-start | bytes 294920 | tf_op jit(solution)/shard_map/ppermute | solution.py:22
  25.2 4.0 %collective-permute-start.8 = (f32[192,128]{1,0:T(8,128)S(1)}, f32[192,128]{1,0:T(8,128)S(1)}, u32[]{:S(2)}, u32[]{:S(2)}) collective-permute-start(f32[192,128]{1,0:T(8,128)S(1)} %add.23.mine_ref), channel_id=1, source_target_pairs={{0,1},{1,0},{2,3},{3,2},{4,5},{5,4},{6,7},{7,6},{8,9},{9,8},{10,11... | collective-permute-start | bytes 294920 | tf_op jit(solution)/shard_map/ppermute | solution.py:22
  25.2 7.1 %copy-start = (f32[320,512]{1,0:T(8,128)S(1)}, f32[320,512]{1,0:T(8,128)}, u32[]{:S(2)}) copy-start(f32[320,512]{1,0:T(8,128)} %get-tuple-element.55.solved_ref) | copy-start | bytes 1966084
  28.9 1.3 %collective-permute-start.10 = (f32[192,128]{1,0:T(8,128)S(1)}, f32[192,128]{1,0:T(8,128)S(1)}, u32[]{:S(2)}, u32[]{:S(2)}) collective-permute-start(f32[192,128]{1,0:T(8,128)S(1)} %collective-permute-done.9.sibling_ref), channel_id=1, source_target_pairs={{0,1},{1,0},{2,3},{3,2},{4,5},{5,4},{6,7},{7,6},{8,9},{9,8},{10,11... | collective-permute-start | bytes 294920 | tf_op jit(solution)/shard_map/ppermute | solution.py:22
  30.7 5.1 %collective-permute-start.11 = (f32[192,128]{1,0:T(8,128)S(1)}, f32[192,128]{1,0:T(8,128)S(1)}, u32[]{:S(2)}, u32[]{:S(2)}) collective-permute-start(f32[192,128]{1,0:T(8,128)S(1)} %get-tuple-element.53.mine_ref), channel_id=1, source_target_pairs={{0,16},{8,24},{16,0},{24,8},{1,17},{9,25},{17,1},{25,9},{2,18},{10... | collective-permute-start | bytes 294920 | tf_op jit(solution)/shard_map/ppermute | solution.py:22

commit v6 on v5

--- a/solution.py
+++ b/solution.py
@@ -182,14 +182,14 @@
 def local_kernel(
     rhs_hbm, leaf_hbm, one_hbm, two_hbm, solved_ref,
     keep_gram_ref, give_gram_ref, keep_ref, give_ref,
-    rhs_ref, leaf_ref, bases_ref, sems,
+    rhs_ref, leaf_ref, one_ref, two_ref, sems,
 ):
     rank = one_hbm.shape[1]
     rows = leaf_hbm.shape[0]
     chunk = 2 * rank
     copies = [
-        pltpu.make_async_copy(two_hbm, bases_ref.at[:, :rank], sems.at[0]),
-        pltpu.make_async_copy(one_hbm, bases_ref.at[:, rank:], sems.at[1]),
+        pltpu.make_async_copy(two_hbm, two_ref, sems.at[0]),
+        pltpu.make_async_copy(one_hbm, one_ref, sems.at[1]),
         pltpu.make_async_copy(rhs_hbm, rhs_ref, sems.at[2]),
     ] + [
         pltpu.make_async_copy(leaf_hbm.at[at : at + chunk], leaf_ref.at[at : at + chunk], sem)
@@ -199,7 +199,7 @@
         copy.start()
     for copy in copies[:3]:
         copy.wait()
-    bases = bases_ref[...]
+    bases = jnp.concatenate((two_ref[...], one_ref[...]), axis=1)
     left = split_pair(jnp.concatenate((bases.T, rhs_ref[...]), axis=0))
     bases = split_pair(bases)
     solved = None
@@ -332,7 +332,8 @@
         scratch_shapes=[
             pltpu.VMEM((width, rows), F32),
             pltpu.VMEM((rows, rows), F32),
-            pltpu.VMEM((rows, 2 * rank), F32),
+            pltpu.VMEM((rows, rank), F32),
+            pltpu.VMEM((rows, rank), F32),
             pltpu.SemaphoreType.DMA((3 + rows // (2 * rank),)),
         ],
     )

time: 43.3 us -> 43.3 us (level)
  no operation moved by 1% of the time
where the time goes in v6:
time: 43.3 us; the launch traced here: 43.1 us
  Pallas kernels  18.5 us (43%)
  starting transfers between devices  14.1 us (33%)
  waiting for transfers between devices  9.67 us (22%)
  local copies, waits for them, and re-layouts  0.7 us (2%)
    pallas_call x7, Pallas kernels, call(): pl.pallas_call(kernel, out_shape=[jax.ShapeDtypeStruct(shape, dtype) for...  18.5 us
    ppermute x12, starting transfers between devices, partner(): return lax.ppermute(value, axis, pairs)  14.1 us
    ppermute x12, waiting for transfers between devices, partner(): return lax.ppermute(value, axis, pairs)  9.67 us
  transfers between devices with their start and end apart: 12, of which 7 were waited for; matrix products, arithmetic and copies ran while one was open for 0% of the time, Pallas kernels for 16%

profile of v6, /device:TPU:0, one launch (start us, length us, event | category | flops | bytes accessed | tf_op | source)
XLA Modules:
  0.0 43.1 jit_solution(2412642835299163006)
XLA Ops:
  0.0 3.5 %shard_map.64 = (f32[320,512]{1,0:T(8,128)}, f32[64,128]{1,0:T(8,128)S(1)}, f32[64,128]{1,0:T(8,128)S(1)}, f32[192,128]{1,0:T(8,128)S(1)}, f32[192,128]{1,0:T(8,128)}) custom-call(f32[64,512]{1,0:T(8,128)} %bitcast.5, f32[512,512]{1,0:T(8,128)} %leaf_hbm.1, f32[512,128]{1,0:T(8,128)} %one_hbm.1, f32[512,128]{1,0:T(8,128)} %two_hbm.1), custom_call_target="tpu_custom_call" | custom-call | tf_op jit(solution)/shard_map/pallas_call | solution.py:308
  3.5 0.0 copy-start.1
  3.5 0.5 %collective-permute-start.5 = (f32[192,128]{1,0:T(8,128)}, f32[192,128]{1,0:T(8,128)S(1)}, u32[]{:S(2)}, u32[]{:S(2)}) collective-permute-start(f32[192,128]{1,0:T(8,128)} %get-tuple-element.45), channel_id=1, source_target_pairs={{0,1},{1,0},{2,3},{3,2},{4,5},{5,4},{6,7},{7,6},{8,9},{9,8},{10,11... | collective-permute-start | bytes 294920 | tf_op jit(solution)/shard_map/ppermute | solution.py:22
  4.0 0.1 collective-permute-start
  4.1 1.1 %collective-permute-done = f32[64,128]{1,0:T(8,128)S(1)} collective-permute-done((f32[64,128]{1,0:T(8,128)S(1)}, f32[64,128]{1,0:T(8,128)S(1)}, u32[]{:S(2)}, u32[]{:S(2)}) %collective-permute-start) | collective-permute-done | bytes 32800 | tf_op jit(solution)/shard_map/ppermute | solution.py:22
  5.3 2.7 %collective-permute-start.1 = (f32[64,128]{1,0:T(8,128)S(1)}, f32[64,128]{1,0:T(8,128)S(1)}, u32[]{:S(2)}, u32[]{:S(2)}) collective-permute-start(f32[64,128]{1,0:T(8,128)S(1)} %add.18), channel_id=1, source_target_pairs={{0,2},{1,3},{2,0},{3,1},{4,6},{5,7},{6,4},{7,5},{8,10},{9,11},{10,... | collective-permute-start | bytes 98312 | tf_op jit(solution)/shard_map/ppermute | solution.py:22
  8.0 0.0 collective-permute-done.5
  8.0 0.2 collective-permute-start.6
  8.2 0.7 %copy-done.2 = bf16[1,256,256]{2,1,0:T(8,128)(2,1)S(1)} copy-done((bf16[1,256,256]{2,1,0:T(8,128)(2,1)S(1)}, bf16[1,256,256]{2,1,0:T(8,128)(2,1)}, u32[]{:S(2)}) %copy-start.2) | copy-done | bytes 131096
  8.9 0.1 shard_map.65
  9.1 0.8 %collective-permute-done.1 = f32[64,128]{1,0:T(8,128)S(1)} collective-permute-done((f32[64,128]{1,0:T(8,128)S(1)}, f32[64,128]{1,0:T(8,128)S(1)}, u32[]{:S(2)}, u32[]{:S(2)}) %collective-permute-start.1) | collective-permute-done | bytes 32800 | tf_op jit(solution)/shard_map/ppermute | solution.py:22
  9.9 3.0 %collective-permute-start.2 = (f32[64,128]{1,0:T(8,128)S(1)}, f32[64,128]{1,0:T(8,128)S(1)}, u32[]{:S(2)}, u32[]{:S(2)}) collective-permute-start(f32[64,128]{1,0:T(8,128)S(1)} %add.19), channel_id=1, source_target_pairs={{0,4},{1,5},{2,6},{3,7},{4,0},{5,1},{6,2},{7,3},{8,12},{9,13},{10,... | collective-permute-start | bytes 98312 | tf_op jit(solution)/shard_map/ppermute | solution.py:22
  12.9 2.0 %collective-permute-done.2 = f32[64,128]{1,0:T(8,128)S(1)} collective-permute-done((f32[64,128]{1,0:T(8,128)S(1)}, f32[64,128]{1,0:T(8,128)S(1)}, u32[]{:S(2)}, u32[]{:S(2)}) %collective-permute-start.2) | collective-permute-done | bytes 32800 | tf_op jit(solution)/shard_map/ppermute | solution.py:22
  15.0 1.7 %collective-permute-start.3 = (f32[64,128]{1,0:T(8,128)S(1)}, f32[64,128]{1,0:T(8,128)S(1)}, u32[]{:S(2)}, u32[]{:S(2)}) collective-permute-start(f32[64,128]{1,0:T(8,128)S(1)} %add.20), channel_id=1, source_target_pairs={{0,8},{8,0},{16,24},{24,16},{1,9},{9,1},{17,25},{25,17},{2,10},{10... | collective-permute-start | bytes 98312 | tf_op jit(solution)/shard_map/ppermute | solution.py:22
  16.7 0.0 collective-permute-done.6
  16.7 2.7 %collective-permute-start.7 = (f32[192,128]{1,0:T(8,128)S(1)}, f32[192,128]{1,0:T(8,128)S(1)}, u32[]{:S(2)}, u32[]{:S(2)}) collective-permute-start(f32[192,128]{1,0:T(8,128)S(1)} %add.22), channel_id=1, source_target_pairs={{0,4},{1,5},{2,6},{3,7},{4,0},{5,1},{6,2},{7,3},{8,12},{9,13},{10,... | collective-permute-start | bytes 294920 | tf_op jit(solution)/shard_map/ppermute | solution.py:22
  19.3 0.1 collective-permute-start.4
  19.4 1.2 %collective-permute-done.4.other_ref = f32[2,64,128]{2,1,0:T(8,128)S(1)} collective-permute-done((f32[2,64,128]{2,1,0:T(8,128)S(1)}, f32[2,64,128]{2,1,0:T(8,128)S(1)}, u32[]{:S(2)}, u32[]{:S(2)}) %collective-permute-start.4) | collective-permute-done | bytes 65568 | tf_op jit(solution)/shard_map/ppermute | solution.py:22
  20.7 3.2 %shard_map.66 = (f32[128,128]{1,0:T(8,128)S(1)}, f32[128,128]{1,0:T(8,128)S(1)}, f32[128,128]{1,0:T(8,128)S(1)}, f32[128,128]{1,0:T(8,128)S(1)}) custom-call(f32[2,64,128]{2,1,0:T(8,128)S(1)} %pad_maximum_fusion.mine_ref, f32[2,64,128]{2,1,0:T(8,128)S(1)} %collective-permute-done.4.other_ref, bf16[256,256]{1,0:T(8,128)(2,1)S(1)} %get-tuple-element.41.factor_ref, ...), custom_call_target="tpu_custom_call" | custom-call | tf_op jit(solution)/shard_map/pallas_call | solution.py:308
  23.9 0.0 collective-permute-done.7
  23.9 1.2 %collective-permute-start.9 = (f32[192,128]{1,0:T(8,128)S(1)}, f32[192,128]{1,0:T(8,128)S(1)}, u32[]{:S(2)}, u32[]{:S(2)}) collective-permute-start(f32[192,128]{1,0:T(8,128)S(1)} %add.23.mine_ref), channel_id=1, source_target_pairs={{0,8},{8,0},{16,24},{24,16},{1,9},{9,1},{17,25},{25,17},{2,10},{10... | collective-permute-start | bytes 294920 | tf_op jit(solution)/shard_map/ppermute | solution.py:22
  25.2 0.0 collective-permute-start.8
  25.2 3.4 %shard_map.67.pair_ref = f32[256,256]{1,0:T(8,128)S(1)} custom-call(f32[128,128]{1,0:T(8,128)S(1)} %get-tuple-element.47.lower_ref, f32[128,128]{1,0:T(8,128)S(1)} %get-tuple-element.48.scaled_ref, f32[128,128]{1,0:T(8,128)S(1)} %get-tuple-element.49.beside_ref, f32[128,128]{1,0:T(8,128)S(1)} %get-tuple-element.50.rest_ref, ...), custom_call_target="tpu_custom_call" | custom-call | tf_op jit(solution)/shard_map/pallas_call | solution.py:308
  28.6 0.3 collective-permute-done.9.sibling_ref
  28.9 0.3 collective-permute-start.10
  29.2 0.0 collective-permute-done.8.other_ref
  29.2 1.0 %collective-permute-done.10.sibling_other_ref = f32[192,128]{1,0:T(8,128)S(1)} collective-permute-done((f32[192,128]{1,0:T(8,128)S(1)}, f32[192,128]{1,0:T(8,128)S(1)}, u32[]{:S(2)}, u32[]{:S(2)}) %collective-permute-start.10) | collective-permute-done | bytes 98336 | tf_op jit(solution)/shard_map/ppermute | solution.py:22
  30.2 0.5 %shard_map.68 = (f32[192,128]{1,0:T(8,128)S(1)}, f32[192,128]{1,0:T(8,128)S(1)}) custom-call(f32[192,128]{1,0:T(8,128)S(1)} %add.23.mine_ref, f32[192,128]{1,0:T(8,128)S(1)} %collective-permute-done.8.other_ref, f32[192,128]{1,0:T(8,128)S(1)} %collective-permute-done.9.sibling_ref, f32[192,128]{1,0:T(8,128)S(1)} %collective-permute-done.10.sibling_other_ref, ...), custom_call_target="tpu_custom_call" | custom-call | tf_op jit(solution)/shard_map/pallas_call | solution.py:308
  30.7 1.6 %collective-permute-start.11 = (f32[192,128]{1,0:T(8,128)S(1)}, f32[192,128]{1,0:T(8,128)S(1)}, u32[]{:S(2)}, u32[]{:S(2)}) collective-permute-start(f32[192,128]{1,0:T(8,128)S(1)} %get-tuple-element.53.mine_ref), channel_id=1, source_target_pairs={{0,16},{8,24},{16,0},{24,8},{1,17},{9,25},{17,1},{25,9},{2,18},{10... | collective-permute-start | bytes 294920 | tf_op jit(solution)/shard_map/ppermute | solution.py:22
  32.3 0.3 shard_map.69
  32.6 3.2 %collective-permute-done.11.other_ref = f32[192,128]{1,0:T(8,128)S(1)} collective-permute-done((f32[192,128]{1,0:T(8,128)S(1)}, f32[192,128]{1,0:T(8,128)S(1)}, u32[]{:S(2)}, u32[]{:S(2)}) %collective-permute-start.11) | collective-permute-done | bytes 98336 | tf_op jit(solution)/shard_map/ppermute | solution.py:22
  35.8 7.3 %shard_map.70 = f32[64,512]{1,0:T(8,128)} custom-call(f32[192,128]{1,0:T(8,128)S(1)} %get-tuple-element.53.mine_ref, f32[192,128]{1,0:T(8,128)S(1)} %collective-permute-done.11.other_ref, bf16[256,256]{1,0:T(8,128)(2,1)S(1)} %get-tuple-element.59.factor_ref, bf16[256,256]{1,0:T(8,128)(2,1)S(1)} %get-tuple-element.60.flipped_ref, ...), custom_call_target="tpu_custom_call" | custom-call | tf_op jit(solution)/shard_map/pallas_call | solution.py:308
  (12 shorter events, 0.1 us)
Async XLA Ops:
  3.5 4.7 %copy-start.1 = (bf16[2,256,256]{2,1,0:T(8,128)(2,1)S(1)}, bf16[2,256,256]{2,1,0:T(8,128)(2,1)}, u32[]{:S(2)}) copy-start(bf16[2,256,256]{2,1,0:T(8,128)(2,1)} %two_ref.1) | copy-start | bytes 786436
  3.5 4.5 %collective-permute-start.5 = (f32[192,128]{1,0:T(8,128)}, f32[192,128]{1,0:T(8,128)S(1)}, u32[]{:S(2)}, u32[]{:S(2)}) collective-permute-start(f32[192,128]{1,0:T(8,128)} %get-tuple-element.45), channel_id=1, source_target_pairs={{0,1},{1,0},{2,3},{3,2},{4,5},{5,4},{6,7},{7,6},{8,9},{9,8},{10,11... | collective-permute-start | bytes 294920 | tf_op jit(solution)/shard_map/ppermute | solution.py:22
  4.0 1.2 %collective-permute-start = (f32[64,128]{1,0:T(8,128)S(1)}, f32[64,128]{1,0:T(8,128)S(1)}, u32[]{:S(2)}, u32[]{:S(2)}) collective-permute-start(f32[64,128]{1,0:T(8,128)S(1)} %get-tuple-element.35), channel_id=1, source_target_pairs={{0,1},{1,0},{2,3},{3,2},{4,5},{5,4},{6,7},{7,6},{8,9},{9,8},{10,11... | collective-permute-start | bytes 98312 | tf_op jit(solution)/shard_map/ppermute | solution.py:22
  5.3 4.6 %collective-permute-start.1 = (f32[64,128]{1,0:T(8,128)S(1)}, f32[64,128]{1,0:T(8,128)S(1)}, u32[]{:S(2)}, u32[]{:S(2)}) collective-permute-start(f32[64,128]{1,0:T(8,128)S(1)} %add.18), channel_id=1, source_target_pairs={{0,2},{1,3},{2,0},{3,1},{4,6},{5,7},{6,4},{7,5},{8,10},{9,11},{10,... | collective-permute-start | bytes 98312 | tf_op jit(solution)/shard_map/ppermute | solution.py:22
  8.0 0.9 %copy-start.2 = (bf16[1,256,256]{2,1,0:T(8,128)(2,1)S(1)}, bf16[1,256,256]{2,1,0:T(8,128)(2,1)}, u32[]{:S(2)}) copy-start(bf16[1,256,256]{2,1,0:T(8,128)(2,1)} %one_ref.1) | copy-start | bytes 393220
  8.0 8.6 %collective-permute-start.6 = (f32[192,128]{1,0:T(8,128)S(1)}, f32[192,128]{1,0:T(8,128)S(1)}, u32[]{:S(2)}, u32[]{:S(2)}) collective-permute-start(f32[192,128]{1,0:T(8,128)S(1)} %add.21), channel_id=1, source_target_pairs={{0,2},{1,3},{2,0},{3,1},{4,6},{5,7},{6,4},{7,5},{8,10},{9,11},{10,... | collective-permute-start | bytes 294920 | tf_op jit(solution)/shard_map/ppermute | solution.py:22
  9.9 5.1 %collective-permute-start.2 = (f32[64,128]{1,0:T(8,128)S(1)}, f32[64,128]{1,0:T(8,128)S(1)}, u32[]{:S(2)}, u32[]{:S(2)}) collective-permute-start(f32[64,128]{1,0:T(8,128)S(1)} %add.19), channel_id=1, source_target_pairs={{0,4},{1,5},{2,6},{3,7},{4,0},{5,1},{6,2},{7,3},{8,12},{9,13},{10,... | collective-permute-start | bytes 98312 | tf_op jit(solution)/shard_map/ppermute | solution.py:22
  15.0 4.4 %collective-permute-start.3 = (f32[64,128]{1,0:T(8,128)S(1)}, f32[64,128]{1,0:T(8,128)S(1)}, u32[]{:S(2)}, u32[]{:S(2)}) collective-permute-start(f32[64,128]{1,0:T(8,128)S(1)} %add.20), channel_id=1, source_target_pairs={{0,8},{8,0},{16,24},{24,16},{1,9},{9,1},{17,25},{25,17},{2,10},{10... | collective-permute-start | bytes 98312 | tf_op jit(solution)/shard_map/ppermute | solution.py:22
  16.7 7.2 %collective-permute-start.7 = (f32[192,128]{1,0:T(8,128)S(1)}, f32[192,128]{1,0:T(8,128)S(1)}, u32[]{:S(2)}, u32[]{:S(2)}) collective-permute-start(f32[192,128]{1,0:T(8,128)S(1)} %add.22), channel_id=1, source_target_pairs={{0,4},{1,5},{2,6},{3,7},{4,0},{5,1},{6,2},{7,3},{8,12},{9,13},{10,... | collective-permute-start | bytes 294920 | tf_op jit(solution)/shard_map/ppermute | solution.py:22
  19.3 1.3 %collective-permute-start.4 = (f32[2,64,128]{2,1,0:T(8,128)S(1)}, f32[2,64,128]{2,1,0:T(8,128)S(1)}, u32[]{:S(2)}, u32[]{:S(2)}) collective-permute-start(f32[2,64,128]{2,1,0:T(8,128)S(1)} %pad_maximum_fusion.mine_ref), channel_id=1, source_target_pairs={{0,1},{1,0},{2,3},{3,2},{4,5},{5,4},{6,7},{7,6},{8,9},{9,8},{10,11... | collective-permute-start | bytes 196616 | tf_op jit(solution)/shard_map/ppermute | solution.py:22
  23.9 4.9 %collective-permute-start.9 = (f32[192,128]{1,0:T(8,128)S(1)}, f32[192,128]{1,0:T(8,128)S(1)}, u32[]{:S(2)}, u32[]{:S(2)}) collective-permute-start(f32[192,128]{1,0:T(8,128)S(1)} %add.23.mine_ref), channel_id=1, source_target_pairs={{0,8},{8,0},{16,24},{24,16},{1,9},{9,1},{17,25},{25,17},{2,10},{10... | collective-permute-start | bytes 294920 | tf_op jit(solution)/shard_map/ppermute | solution.py:22
  25.2 4.0 %collective-permute-start.8 = (f32[192,128]{1,0:T(8,128)S(1)}, f32[192,128]{1,0:T(8,128)S(1)}, u32[]{:S(2)}, u32[]{:S(2)}) collective-permute-start(f32[192,128]{1,0:T(8,128)S(1)} %add.23.mine_ref), channel_id=1, source_target_pairs={{0,1},{1,0},{2,3},{3,2},{4,5},{5,4},{6,7},{7,6},{8,9},{9,8},{10,11... | collective-permute-start | bytes 294920 | tf_op jit(solution)/shard_map/ppermute | solution.py:22
  25.2 7.1 %copy-start = (f32[320,512]{1,0:T(8,128)S(1)}, f32[320,512]{1,0:T(8,128)}, u32[]{:S(2)}) copy-start(f32[320,512]{1,0:T(8,128)} %get-tuple-element.55.solved_ref) | copy-start | bytes 1966084
  28.9 1.3 %collective-permute-start.10 = (f32[192,128]{1,0:T(8,128)S(1)}, f32[192,128]{1,0:T(8,128)S(1)}, u32[]{:S(2)}, u32[]{:S(2)}) collective-permute-start(f32[192,128]{1,0:T(8,128)S(1)} %collective-permute-done.9.sibling_ref), channel_id=1, source_target_pairs={{0,1},{1,0},{2,3},{3,2},{4,5},{5,4},{6,7},{7,6},{8,9},{9,8},{10,11... | collective-permute-start | bytes 294920 | tf_op jit(solution)/shard_map/ppermute | solution.py:22
  30.7 5.1 %collective-permute-start.11 = (f32[192,128]{1,0:T(8,128)S(1)}, f32[192,128]{1,0:T(8,128)S(1)}, u32[]{:S(2)}, u32[]{:S(2)}) collective-permute-start(f32[192,128]{1,0:T(8,128)S(1)} %get-tuple-element.53.mine_ref), channel_id=1, source_target_pairs={{0,16},{8,24},{16,0},{24,8},{1,17},{9,25},{17,1},{25,9},{2,18},{10... | collective-permute-start | bytes 294920 | tf_op jit(solution)/shard_map/ppermute | solution.py:22

commit v7 on v5

--- a/solution.py
+++ b/solution.py
@@ -346,7 +346,7 @@
     ]
     sibling_mask = 2 ** (two_bits - fine_bits)
     for index, (axis, mask) in enumerate(stages):
-        received = partner(gram, axis, mask)
+        received = partner(gram, *stages[-1 - index])
         if index == 0:
             received, factors = lax.optimization_barrier((received, factors))
         gram = gram + received

time: 43.3 us -> 43.3 us (level)
  starting transfers between devices: 14.1 us -> 15.7 us
  waiting for transfers between devices: 9.68 us -> 8.79 us
  local copies, waits for them, and re-layouts: 0.7 us -> 0.01 us
    ppermute x12, starting transfers between devices: 14.1 us -> 15.7 us  [partner(): return lax.ppermute(value, axis, pairs)]
    ppermute x12, waiting for transfers between devices: 9.68 us -> 8.79 us  [partner(): return lax.ppermute(value, axis, pairs)]
    unnamed x6, local copies, waits for them, and re-layouts: 0.7 us -> 0.01 us
where the time goes in v7:
time: 43.3 us; the launch traced here: 43.1 us
  Pallas kernels  18.5 us (43%)
  starting transfers between devices  15.7 us (36%)
  waiting for transfers between devices  8.79 us (20%)
    pallas_call x7, Pallas kernels, call(): pl.pallas_call(kernel, out_shape=[jax.ShapeDtypeStruct(shape, dtype) for...  18.5 us
    ppermute x12, starting transfers between devices, partner(): return lax.ppermute(value, axis, pairs)  15.7 us
    ppermute x12, waiting for transfers between devices, partner(): return lax.ppermute(value, axis, pairs)  8.79 us
  transfers between devices with their start and end apart: 12, of which 7 were waited for; matrix products, arithmetic and copies ran while one was open for 0% of the time, Pallas kernels for 16%

profile of v7, /device:TPU:0, one launch (start us, length us, event | category | flops | bytes accessed | tf_op | source)
XLA Modules:
  0.0 43.1 jit_solution(16702772860937728129)
XLA Ops:
  0.0 3.5 %shard_map.64 = (f32[320,512]{1,0:T(8,128)}, f32[64,128]{1,0:T(8,128)S(1)}, f32[64,128]{1,0:T(8,128)S(1)}, f32[192,128]{1,0:T(8,128)S(1)}, f32[192,128]{1,0:T(8,128)}) custom-call(f32[64,512]{1,0:T(8,128)} %bitcast.5, f32[512,512]{1,0:T(8,128)} %leaf_hbm.1, f32[512,128]{1,0:T(8,128)} %one_hbm.1, f32[512,128]{1,0:T(8,128)} %two_hbm.1), custom_call_target="tpu_custom_call" | custom-call | tf_op jit(solution)/shard_map/pallas_call | solution.py:308
  3.5 0.0 copy-start.1
  3.5 0.5 %collective-permute-start.5 = (f32[192,128]{1,0:T(8,128)}, f32[192,128]{1,0:T(8,128)S(1)}, u32[]{:S(2)}, u32[]{:S(2)}) collective-permute-start(f32[192,128]{1,0:T(8,128)} %get-tuple-element.45), channel_id=1, source_target_pairs={{0,1},{1,0},{2,3},{3,2},{4,5},{5,4},{6,7},{7,6},{8,9},{9,8},{10,11... | collective-permute-start | bytes 294920 | tf_op jit(solution)/shard_map/ppermute | solution.py:22
  4.1 0.1 collective-permute-start
  4.1 1.1 %collective-permute-done = f32[64,128]{1,0:T(8,128)S(1)} collective-permute-done((f32[64,128]{1,0:T(8,128)S(1)}, f32[64,128]{1,0:T(8,128)S(1)}, u32[]{:S(2)}, u32[]{:S(2)}) %collective-permute-start) | collective-permute-done | bytes 32800 | tf_op jit(solution)/shard_map/ppermute | solution.py:22
  5.3 3.8 %collective-permute-start.1 = (f32[64,128]{1,0:T(8,128)S(1)}, f32[64,128]{1,0:T(8,128)S(1)}, u32[]{:S(2)}, u32[]{:S(2)}) collective-permute-start(f32[64,128]{1,0:T(8,128)S(1)} %add.18), channel_id=1, source_target_pairs={{0,4},{1,5},{2,6},{3,7},{4,0},{5,1},{6,2},{7,3},{8,12},{9,13},{10,... | collective-permute-start | bytes 98312 | tf_op jit(solution)/shard_map/ppermute | solution.py:22
  9.0 0.0 collective-permute-done.5
  9.0 1.6 %collective-permute-start.6 = (f32[192,128]{1,0:T(8,128)S(1)}, f32[192,128]{1,0:T(8,128)S(1)}, u32[]{:S(2)}, u32[]{:S(2)}) collective-permute-start(f32[192,128]{1,0:T(8,128)S(1)} %add.21), channel_id=1, source_target_pairs={{0,2},{1,3},{2,0},{3,1},{4,6},{5,7},{6,4},{7,5},{8,10},{9,11},{10,... | collective-permute-start | bytes 294920 | tf_op jit(solution)/shard_map/ppermute | solution.py:22
  10.7 0.1 shard_map.65
  10.8 0.1 collective-permute-done.1
  10.9 2.2 %collective-permute-start.2 = (f32[64,128]{1,0:T(8,128)S(1)}, f32[64,128]{1,0:T(8,128)S(1)}, u32[]{:S(2)}, u32[]{:S(2)}) collective-permute-start(f32[64,128]{1,0:T(8,128)S(1)} %add.19), channel_id=1, source_target_pairs={{0,2},{1,3},{2,0},{3,1},{4,6},{5,7},{6,4},{7,5},{8,10},{9,11},{10,... | collective-permute-start | bytes 98312 | tf_op jit(solution)/shard_map/ppermute | solution.py:22
  13.1 1.9 %collective-permute-done.2 = f32[64,128]{1,0:T(8,128)S(1)} collective-permute-done((f32[64,128]{1,0:T(8,128)S(1)}, f32[64,128]{1,0:T(8,128)S(1)}, u32[]{:S(2)}, u32[]{:S(2)}) %collective-permute-start.2) | collective-permute-done | bytes 32800 | tf_op jit(solution)/shard_map/ppermute | solution.py:22
  15.0 1.6 %collective-permute-start.3 = (f32[64,128]{1,0:T(8,128)S(1)}, f32[64,128]{1,0:T(8,128)S(1)}, u32[]{:S(2)}, u32[]{:S(2)}) collective-permute-start(f32[64,128]{1,0:T(8,128)S(1)} %add.20), channel_id=1, source_target_pairs={{0,8},{8,0},{16,24},{24,16},{1,9},{9,1},{17,25},{25,17},{2,10},{10... | collective-permute-start | bytes 98312 | tf_op jit(solution)/shard_map/ppermute | solution.py:22
  16.7 0.0 collective-permute-done.6
  16.7 2.7 %collective-permute-start.7 = (f32[192,128]{1,0:T(8,128)S(1)}, f32[192,128]{1,0:T(8,128)S(1)}, u32[]{:S(2)}, u32[]{:S(2)}) collective-permute-start(f32[192,128]{1,0:T(8,128)S(1)} %add.22), channel_id=1, source_target_pairs={{0,4},{1,5},{2,6},{3,7},{4,0},{5,1},{6,2},{7,3},{8,12},{9,13},{10,... | collective-permute-start | bytes 294920 | tf_op jit(solution)/shard_map/ppermute | solution.py:22
  19.3 0.0 collective-permute-done.3
  19.3 0.1 collective-permute-start.4
  19.4 1.2 %collective-permute-done.4.other_ref = f32[2,64,128]{2,1,0:T(8,128)S(1)} collective-permute-done((f32[2,64,128]{2,1,0:T(8,128)S(1)}, f32[2,64,128]{2,1,0:T(8,128)S(1)}, u32[]{:S(2)}, u32[]{:S(2)}) %collective-permute-start.4) | collective-permute-done | bytes 65568 | tf_op jit(solution)/shard_map/ppermute | solution.py:22
  20.7 3.2 %shard_map.66 = (f32[128,128]{1,0:T(8,128)S(1)}, f32[128,128]{1,0:T(8,128)S(1)}, f32[128,128]{1,0:T(8,128)S(1)}, f32[128,128]{1,0:T(8,128)S(1)}) custom-call(f32[2,64,128]{2,1,0:T(8,128)S(1)} %pad_maximum_fusion.mine_ref, f32[2,64,128]{2,1,0:T(8,128)S(1)} %collective-permute-done.4.other_ref, bf16[256,256]{1,0:T(8,128)(2,1)S(1)} %get-tuple-element.41.factor_ref, ...), custom_call_target="tpu_custom_call" | custom-call | tf_op jit(solution)/shard_map/pallas_call | solution.py:308
  23.9 0.0 collective-permute-done.7
  23.9 1.2 %collective-permute-start.9 = (f32[192,128]{1,0:T(8,128)S(1)}, f32[192,128]{1,0:T(8,128)S(1)}, u32[]{:S(2)}, u32[]{:S(2)}) collective-permute-start(f32[192,128]{1,0:T(8,128)S(1)} %add.23.mine_ref), channel_id=1, source_target_pairs={{0,8},{8,0},{16,24},{24,16},{1,9},{9,1},{17,25},{25,17},{2,10},{10... | collective-permute-start | bytes 294920 | tf_op jit(solution)/shard_map/ppermute | solution.py:22
  25.2 0.0 collective-permute-start.8
  25.2 3.4 %shard_map.67.pair_ref = f32[256,256]{1,0:T(8,128)S(1)} custom-call(f32[128,128]{1,0:T(8,128)S(1)} %get-tuple-element.47.lower_ref, f32[128,128]{1,0:T(8,128)S(1)} %get-tuple-element.48.scaled_ref, f32[128,128]{1,0:T(8,128)S(1)} %get-tuple-element.49.beside_ref, f32[128,128]{1,0:T(8,128)S(1)} %get-tuple-element.50.rest_ref, ...), custom_call_target="tpu_custom_call" | custom-call | tf_op jit(solution)/shard_map/pallas_call | solution.py:308
  28.6 0.3 collective-permute-done.9.sibling_ref
  28.9 0.3 collective-permute-start.10
  29.2 0.0 collective-permute-done.8.other_ref
  29.2 1.0 %collective-permute-done.10.sibling_other_ref = f32[192,128]{1,0:T(8,128)S(1)} collective-permute-done((f32[192,128]{1,0:T(8,128)S(1)}, f32[192,128]{1,0:T(8,128)S(1)}, u32[]{:S(2)}, u32[]{:S(2)}) %collective-permute-start.10) | collective-permute-done | bytes 98336 | tf_op jit(solution)/shard_map/ppermute | solution.py:22
  30.2 0.5 %shard_map.68 = (f32[192,128]{1,0:T(8,128)S(1)}, f32[192,128]{1,0:T(8,128)S(1)}) custom-call(f32[192,128]{1,0:T(8,128)S(1)} %add.23.mine_ref, f32[192,128]{1,0:T(8,128)S(1)} %collective-permute-done.8.other_ref, f32[192,128]{1,0:T(8,128)S(1)} %collective-permute-done.9.sibling_ref, f32[192,128]{1,0:T(8,128)S(1)} %collective-permute-done.10.sibling_other_ref, ...), custom_call_target="tpu_custom_call" | custom-call | tf_op jit(solution)/shard_map/pallas_call | solution.py:308
  30.7 1.6 %collective-permute-start.11 = (f32[192,128]{1,0:T(8,128)S(1)}, f32[192,128]{1,0:T(8,128)S(1)}, u32[]{:S(2)}, u32[]{:S(2)}) collective-permute-start(f32[192,128]{1,0:T(8,128)S(1)} %get-tuple-element.53.mine_ref), channel_id=1, source_target_pairs={{0,16},{8,24},{16,0},{24,8},{1,17},{9,25},{17,1},{25,9},{2,18},{10... | collective-permute-start | bytes 294920 | tf_op jit(solution)/shard_map/ppermute | solution.py:22
  32.3 0.3 shard_map.69
  32.6 3.2 %collective-permute-done.11.other_ref = f32[192,128]{1,0:T(8,128)S(1)} collective-permute-done((f32[192,128]{1,0:T(8,128)S(1)}, f32[192,128]{1,0:T(8,128)S(1)}, u32[]{:S(2)}, u32[]{:S(2)}) %collective-permute-start.11) | collective-permute-done | bytes 98336 | tf_op jit(solution)/shard_map/ppermute | solution.py:22
  35.8 7.3 %shard_map.70 = f32[64,512]{1,0:T(8,128)} custom-call(f32[192,128]{1,0:T(8,128)S(1)} %get-tuple-element.53.mine_ref, f32[192,128]{1,0:T(8,128)S(1)} %collective-permute-done.11.other_ref, bf16[256,256]{1,0:T(8,128)(2,1)S(1)} %get-tuple-element.59.factor_ref, bf16[256,256]{1,0:T(8,128)(2,1)S(1)} %get-tuple-element.60.flipped_ref, ...), custom_call_target="tpu_custom_call" | custom-call | tf_op jit(solution)/shard_map/pallas_call | solution.py:308
  (12 shorter events, 0.1 us)
Async XLA Ops:
  3.5 7.2 %copy-start.1 = (bf16[2,256,256]{2,1,0:T(8,128)(2,1)S(1)}, bf16[2,256,256]{2,1,0:T(8,128)(2,1)}, u32[]{:S(2)}) copy-start(bf16[2,256,256]{2,1,0:T(8,128)(2,1)} %two_ref.1) | copy-start | bytes 786436
  3.5 5.5 %collective-permute-start.5 = (f32[192,128]{1,0:T(8,128)}, f32[192,128]{1,0:T(8,128)S(1)}, u32[]{:S(2)}, u32[]{:S(2)}) collective-permute-start(f32[192,128]{1,0:T(8,128)} %get-tuple-element.45), channel_id=1, source_target_pairs={{0,1},{1,0},{2,3},{3,2},{4,5},{5,4},{6,7},{7,6},{8,9},{9,8},{10,11... | collective-permute-start | bytes 294920 | tf_op jit(solution)/shard_map/ppermute | solution.py:22
  4.1 1.2 %collective-permute-start = (f32[64,128]{1,0:T(8,128)S(1)}, f32[64,128]{1,0:T(8,128)S(1)}, u32[]{:S(2)}, u32[]{:S(2)}) collective-permute-start(f32[64,128]{1,0:T(8,128)S(1)} %get-tuple-element.35), channel_id=1, source_target_pairs={{0,1},{1,0},{2,3},{3,2},{4,5},{5,4},{6,7},{7,6},{8,9},{9,8},{10,11... | collective-permute-start | bytes 98312 | tf_op jit(solution)/shard_map/ppermute | solution.py:22
  5.3 5.7 %collective-permute-start.1 = (f32[64,128]{1,0:T(8,128)S(1)}, f32[64,128]{1,0:T(8,128)S(1)}, u32[]{:S(2)}, u32[]{:S(2)}) collective-permute-start(f32[64,128]{1,0:T(8,128)S(1)} %add.18), channel_id=1, source_target_pairs={{0,4},{1,5},{2,6},{3,7},{4,0},{5,1},{6,2},{7,3},{8,12},{9,13},{10,... | collective-permute-start | bytes 98312 | tf_op jit(solution)/shard_map/ppermute | solution.py:22
  9.0 1.7 %copy-start.2 = (bf16[1,256,256]{2,1,0:T(8,128)(2,1)S(1)}, bf16[1,256,256]{2,1,0:T(8,128)(2,1)}, u32[]{:S(2)}) copy-start(bf16[1,256,256]{2,1,0:T(8,128)(2,1)} %one_ref.1) | copy-start | bytes 393220
  9.0 7.6 %collective-permute-start.6 = (f32[192,128]{1,0:T(8,128)S(1)}, f32[192,128]{1,0:T(8,128)S(1)}, u32[]{:S(2)}, u32[]{:S(2)}) collective-permute-start(f32[192,128]{1,0:T(8,128)S(1)} %add.21), channel_id=1, source_target_pairs={{0,2},{1,3},{2,0},{3,1},{4,6},{5,7},{6,4},{7,5},{8,10},{9,11},{10,... | collective-permute-start | bytes 294920 | tf_op jit(solution)/shard_map/ppermute | solution.py:22
  10.9 4.1 %collective-permute-start.2 = (f32[64,128]{1,0:T(8,128)S(1)}, f32[64,128]{1,0:T(8,128)S(1)}, u32[]{:S(2)}, u32[]{:S(2)}) collective-permute-start(f32[64,128]{1,0:T(8,128)S(1)} %add.19), channel_id=1, source_target_pairs={{0,2},{1,3},{2,0},{3,1},{4,6},{5,7},{6,4},{7,5},{8,10},{9,11},{10,... | collective-permute-start | bytes 98312 | tf_op jit(solution)/shard_map/ppermute | solution.py:22
  15.0 4.3 %collective-permute-start.3 = (f32[64,128]{1,0:T(8,128)S(1)}, f32[64,128]{1,0:T(8,128)S(1)}, u32[]{:S(2)}, u32[]{:S(2)}) collective-permute-start(f32[64,128]{1,0:T(8,128)S(1)} %add.20), channel_id=1, source_target_pairs={{0,8},{8,0},{16,24},{24,16},{1,9},{9,1},{17,25},{25,17},{2,10},{10... | collective-permute-start | bytes 98312 | tf_op jit(solution)/shard_map/ppermute | solution.py:22
  16.7 7.2 %collective-permute-start.7 = (f32[192,128]{1,0:T(8,128)S(1)}, f32[192,128]{1,0:T(8,128)S(1)}, u32[]{:S(2)}, u32[]{:S(2)}) collective-permute-start(f32[192,128]{1,0:T(8,128)S(1)} %add.22), channel_id=1, source_target_pairs={{0,4},{1,5},{2,6},{3,7},{4,0},{5,1},{6,2},{7,3},{8,12},{9,13},{10,... | collective-permute-start | bytes 294920 | tf_op jit(solution)/shard_map/ppermute | solution.py:22
  19.3 1.3 %collective-permute-start.4 = (f32[2,64,128]{2,1,0:T(8,128)S(1)}, f32[2,64,128]{2,1,0:T(8,128)S(1)}, u32[]{:S(2)}, u32[]{:S(2)}) collective-permute-start(f32[2,64,128]{2,1,0:T(8,128)S(1)} %pad_maximum_fusion.mine_ref), channel_id=1, source_target_pairs={{0,1},{1,0},{2,3},{3,2},{4,5},{5,4},{6,7},{7,6},{8,9},{9,8},{10,11... | collective-permute-start | bytes 196616 | tf_op jit(solution)/shard_map/ppermute | solution.py:22
  23.9 4.9 %collective-permute-start.9 = (f32[192,128]{1,0:T(8,128)S(1)}, f32[192,128]{1,0:T(8,128)S(1)}, u32[]{:S(2)}, u32[]{:S(2)}) collective-permute-start(f32[192,128]{1,0:T(8,128)S(1)} %add.23.mine_ref), channel_id=1, source_target_pairs={{0,8},{8,0},{16,24},{24,16},{1,9},{9,1},{17,25},{25,17},{2,10},{10... | collective-permute-start | bytes 294920 | tf_op jit(solution)/shard_map/ppermute | solution.py:22
  25.2 4.0 %collective-permute-start.8 = (f32[192,128]{1,0:T(8,128)S(1)}, f32[192,128]{1,0:T(8,128)S(1)}, u32[]{:S(2)}, u32[]{:S(2)}) collective-permute-start(f32[192,128]{1,0:T(8,128)S(1)} %add.23.mine_ref), channel_id=1, source_target_pairs={{0,1},{1,0},{2,3},{3,2},{4,5},{5,4},{6,7},{7,6},{8,9},{9,8},{10,11... | collective-permute-start | bytes 294920 | tf_op jit(solution)/shard_map/ppermute | solution.py:22
  25.2 7.1 %copy-start = (f32[320,512]{1,0:T(8,128)S(1)}, f32[320,512]{1,0:T(8,128)}, u32[]{:S(2)}) copy-start(f32[320,512]{1,0:T(8,128)} %get-tuple-element.55.solved_ref) | copy-start | bytes 1966084
  28.9 1.3 %collective-permute-start.10 = (f32[192,128]{1,0:T(8,128)S(1)}, f32[192,128]{1,0:T(8,128)S(1)}, u32[]{:S(2)}, u32[]{:S(2)}) collective-permute-start(f32[192,128]{1,0:T(8,128)S(1)} %collective-permute-done.9.sibling_ref), channel_id=1, source_target_pairs={{0,1},{1,0},{2,3},{3,2},{4,5},{5,4},{6,7},{7,6},{8,9},{9,8},{10,11... | collective-permute-start | bytes 294920 | tf_op jit(solution)/shard_map/ppermute | solution.py:22
  30.7 5.1 %collective-permute-start.11 = (f32[192,128]{1,0:T(8,128)S(1)}, f32[192,128]{1,0:T(8,128)S(1)}, u32[]{:S(2)}, u32[]{:S(2)}) collective-permute-start(f32[192,128]{1,0:T(8,128)S(1)} %get-tuple-element.53.mine_ref), channel_id=1, source_target_pairs={{0,16},{8,24},{16,0},{24,8},{1,17},{9,25},{17,1},{25,9},{2,18},{10... | collective-permute-start | bytes 294920 | tf_op jit(solution)/shard_map/ppermute | solution.py:22
